TPU v7x, 32 devices: a whole 2x2x4 slice. The times are simulated.
32 devices in a mesh: parts: 2 (over y), expert: 4 (over x, core), cuts: 4 (over z).
Axes of the slice: x: 2, y: 2, z: 4, core: 2. Of those that a mesh axis runs over, the one named last changes fastest.
Arguments:
- inputs: bfloat16 [1536, 3072], P(('parts', 'expert'), 'cuts'), parts along dimension 0, may hold values from -6 to 6
- out_grad: bfloat16 [1536, 3072], P(('parts', 'expert'), 'cuts'), parts along dimension 0, may hold values from -6 to 6
- experts: int32 [1536, 2], P(('parts', 'expert')), parts along dimension 0, may hold values from 0 to 7, all different within a row; in each aligned block of 192 rows (0 to 191, 192 to 383, ...) at most 64 rows name the same one
- route_gates: float32 [1536, 2], P(('parts', 'expert')), parts along dimension 0, may hold values from 0.1 to 0.9
- gate_proj: bfloat16 [8, 3072, 8192], P('expert', None, 'cuts'), may hold values from -0.109375 to 0.109375
- up_proj: bfloat16 [8, 3072, 8192], P('expert', None, 'cuts'), may hold values from -0.109375 to 0.109375
- down_proj: bfloat16 [8, 8192, 3072], P('expert', 'cuts'), may hold values from -0.0625 to 0.0625
- gate_in: bfloat16 [8, 16, 3072], P('expert', None, 'cuts'), may hold values from -0.109375 to 0.109375
- gate_out: bfloat16 [8, 16, 8192], P('expert', None, 'cuts'), may hold values from -0.59765625 to 0.59765625
- up_in: bfloat16 [8, 16, 3072], P('expert', None, 'cuts'), may hold values from -0.109375 to 0.109375
- up_out: bfloat16 [8, 16, 8192], P('expert', None, 'cuts'), may hold values from -0.59765625 to 0.59765625
- down_in: bfloat16 [8, 16, 8192], P('expert', None, 'cuts'), may hold values from -0.0625 to 0.0625
- down_out: bfloat16 [8, 16, 3072], P('expert', None, 'cuts'), may hold values from -0.59765625 to 0.59765625
Outputs:
- input_grad: bfloat16 [1536, 3072], P(('parts', 'expert'), 'cuts'), parts along dimension 0
- grad_gate_in: float32 [16, 16, 3072], P(('parts', 'expert'), None, 'cuts'), parts along dimension 0
- gate_output_gradient: float32 [16, 16, 8192], P(('parts', 'expert'), None, 'cuts'), parts along dimension 0
- grad_up_in: float32 [16, 16, 3072], P(('parts', 'expert'), None, 'cuts'), parts along dimension 0
- up_output_gradient: float32 [16, 16, 8192], P(('parts', 'expert'), None, 'cuts'), parts along dimension 0
- down_input_gradient: float32 [16, 16, 8192], P(('parts', 'expert'), None, 'cuts'), parts along dimension 0
- grad_down_out: float32 [16, 16, 3072], P(('parts', 'expert'), None, 'cuts'), parts along dimension 0
There are 2 independent parts, one for each index of `parts`. A program takes and returns all parts, laid end to end along the dimension named above; an argument that names none is the same for every part. Nothing has to cross between parts.
Inputs may be any that keep to these rules, and one draw needn't show every extreme that they name: Each token names two different experts; among the 192 tokens of one index of expert (aligned blocks of 192 rows) no expert is named more than 64 times.
All inputs are finite; a program needn't handle non-finite values.
Results may differ from a plain program's by a relative error of at most 0.012.
Values may be sent and summed in bfloat16 or wider, within the bound.
No kernel may reach another device: no remote copies, remote signals or barrier semaphores. Data moves between devices by JAX's collectives and lax.ppermute only.
A program may use at most 256 MiB of HBM per device.

v0:
```python
import jax
import jax.numpy as jnp
from jax import lax
from jax.sharding import PartitionSpec as P

EXPERTS = 8
SLOT = 64


adapter_scale = 0.25


def body(
    inputs,
    out_grad,
    experts,
    route_gates,
    gate_proj,
    up_proj,
    down_proj,
    gate_in,
    gate_out,
    up_in,
    up_out,
    down_in,
    down_out,
):
    group_count = lax.axis_size("expert")
    local_count = gate_proj.shape[0]
    col_width = inputs.shape[1]
    tok_count = inputs.shape[0]
    flat_ids = experts.reshape(2 * tok_count)
    onehot = (flat_ids[:, None] == jnp.arange(EXPERTS, dtype=jnp.int32)[None, :]).astype(jnp.int32)
    earlier = jnp.sum((jnp.cumsum(onehot, axis=0) - 1) * onehot, axis=1)
    target = flat_ids * SLOT + earlier
    placing = (jnp.arange(EXPERTS * SLOT, dtype=jnp.int32)[:, None] == target[None, :]).astype(
        jnp.bfloat16
    )
    scaled = (
        (route_gates[:, :, None] * out_grad[:, None, :].astype(jnp.float32))
        .astype(jnp.bfloat16)
        .reshape(2 * tok_count, col_width)
    )
    doubled = jnp.repeat(inputs, 2, axis=0)
    send_input = (
        jnp.dot(placing, doubled, preferred_element_type=jnp.float32)
        .astype(jnp.bfloat16)
        .reshape(group_count, local_count * SLOT, col_width)
    )
    send_grad = (
        jnp.dot(placing, scaled, preferred_element_type=jnp.float32)
        .astype(jnp.bfloat16)
        .reshape(group_count, local_count * SLOT, col_width)
    )
    recv_input, recv_grad = (
        lax.all_to_all(send_input, "expert", split_axis=0, concat_axis=0, tiled=True),
        lax.all_to_all(send_grad, "expert", split_axis=0, concat_axis=0, tiled=True),
    )
    gate_in_all, up_in_all, down_out_all = (
        lax.all_gather(gate_in, "cuts", axis=2, tiled=True),
        lax.all_gather(up_in, "cuts", axis=2, tiled=True),
        lax.all_gather(down_out, "cuts", axis=2, tiled=True),
    )
    model_width = gate_in_all.shape[2]
    rows_input, rows_grad = (
        lax.all_gather(recv_input, "cuts", axis=2, tiled=True),
        lax.all_gather(recv_grad, "cuts", axis=2, tiled=True),
    )
    grad_block = rows_grad.reshape(-1, local_count, SLOT, model_width)
    down_low_rank = jnp.einsum(
        "blsd,lrd->blsr", grad_block, down_out_all, preferred_element_type=jnp.float32
    ).astype(jnp.bfloat16)
    hidden_state_gradient = jnp.einsum(
        "blsd,lfd->blsf", grad_block, down_proj, preferred_element_type=jnp.float32
    )
    hidden_state_gradient = hidden_state_gradient + adapter_scale * jnp.einsum(
        "blsr,lrf->blsf", down_low_rank, down_in, preferred_element_type=jnp.float32
    )
    grad_block, down_low_rank, hidden_state_gradient = (
        grad_block,
        down_low_rank,
        hidden_state_gradient,
    )
    input_block = rows_input.reshape(-1, local_count, SLOT, model_width)
    gate_low_rank = jnp.einsum(
        "blsd,lrd->blsr", input_block, gate_in_all, preferred_element_type=jnp.float32
    ).astype(jnp.bfloat16)
    up_low_rank = jnp.einsum(
        "blsd,lrd->blsr", input_block, up_in_all, preferred_element_type=jnp.float32
    ).astype(jnp.bfloat16)
    gate_preactivation = jnp.einsum(
        "blsd,ldf->blsf", input_block, gate_proj, preferred_element_type=jnp.float32
    )
    gate_preactivation = gate_preactivation + adapter_scale * jnp.einsum(
        "blsr,lrf->blsf", gate_low_rank, gate_out, preferred_element_type=jnp.float32
    )
    up_preactivation = jnp.einsum(
        "blsd,ldf->blsf", input_block, up_proj, preferred_element_type=jnp.float32
    )
    up_preactivation = up_preactivation + adapter_scale * jnp.einsum(
        "blsr,lrf->blsf", up_low_rank, up_out, preferred_element_type=jnp.float32
    )
    sigmoid_gate = jax.nn.sigmoid(gate_preactivation)
    activated = gate_preactivation * sigmoid_gate
    hidden_state = (activated * up_preactivation).astype(jnp.bfloat16)
    gate_preact_grad = (
        hidden_state_gradient
        * up_preactivation
        * sigmoid_gate
        * (1.0 + gate_preactivation * (1.0 - sigmoid_gate))
    ).astype(jnp.bfloat16)
    up_preact_grad = (hidden_state_gradient * activated).astype(jnp.bfloat16)
    gate_output_gradient = adapter_scale * jnp.einsum(
        "blsr,blsf->lrf", gate_low_rank, gate_preact_grad, preferred_element_type=jnp.float32
    )
    up_output_gradient = adapter_scale * jnp.einsum(
        "blsr,blsf->lrf", up_low_rank, up_preact_grad, preferred_element_type=jnp.float32
    )
    down_input_gradient = adapter_scale * jnp.einsum(
        "blsr,blsf->lrf", down_low_rank, hidden_state, preferred_element_type=jnp.float32
    )
    gate_projected = jnp.einsum(
        "blsf,lrf->blsr", gate_preact_grad, gate_out, preferred_element_type=jnp.float32
    )
    up_projected = jnp.einsum(
        "blsf,lrf->blsr", up_preact_grad, up_out, preferred_element_type=jnp.float32
    )
    down_projected = jnp.einsum(
        "blsf,lrf->blsr", hidden_state, down_in, preferred_element_type=jnp.float32
    )
    gate_in_wide = gate_in_all.astype(jnp.float32)
    up_in_wide = up_in_all.astype(jnp.float32)
    partial_product = jnp.einsum(
        "blsf,ldf->dbls", gate_preact_grad, gate_proj, preferred_element_type=jnp.float32
    )
    partial_product = partial_product + jnp.einsum(
        "blsf,ldf->dbls", up_preact_grad, up_proj, preferred_element_type=jnp.float32
    )
    adapter_product = jnp.einsum(
        "blsr,lrd->dbls", gate_projected, gate_in_wide, precision=lax.Precision.HIGHEST
    )
    adapter_product = adapter_product + jnp.einsum(
        "blsr,lrd->dbls", up_projected, up_in_wide, precision=lax.Precision.HIGHEST
    )
    summed = lax.psum_scatter(
        (partial_product + adapter_scale * adapter_product)
        .reshape(lax.axis_size("cuts") * col_width, -1)
        .astype(jnp.bfloat16),
        "cuts",
        scatter_dimension=0,
        tiled=True,
    )
    row_grad = summed.reshape(col_width, group_count, local_count * SLOT)
    returned = lax.all_to_all(row_grad, "expert", split_axis=1, concat_axis=1, tiled=True)
    assigned = jnp.einsum(
        "de,et->td",
        returned.reshape(col_width, EXPERTS * SLOT),
        placing,
        preferred_element_type=jnp.float32,
    )
    input_grad = jnp.sum(assigned.reshape(tok_count, 2, col_width), axis=1).astype(jnp.bfloat16)
    widened_input = input_block.astype(jnp.float32)
    gate_adapter_product = adapter_scale * jnp.einsum(
        "blsr,blsd->lrd", gate_projected, widened_input, precision=lax.Precision.HIGHEST
    )
    up_adapter_product = adapter_scale * jnp.einsum(
        "blsr,blsd->lrd", up_projected, widened_input, precision=lax.Precision.HIGHEST
    )
    down_adapter_product = adapter_scale * jnp.einsum(
        "blsr,blsd->lrd",
        down_projected,
        grad_block.astype(jnp.float32),
        precision=lax.Precision.HIGHEST,
    )
    grad_gate_in, grad_up_in, grad_down_out = (
        lax.psum_scatter(gate_adapter_product, "cuts", scatter_dimension=2, tiled=True),
        lax.psum_scatter(up_adapter_product, "cuts", scatter_dimension=2, tiled=True),
        lax.psum_scatter(down_adapter_product, "cuts", scatter_dimension=2, tiled=True),
    )
    return (
        input_grad,
        grad_gate_in,
        gate_output_gradient,
        grad_up_in,
        up_output_gradient,
        down_input_gradient,
        grad_down_out,
    )


def solution(mesh):
    return jax.shard_map(
        body,
        mesh=mesh,
        in_specs=(
            P(("parts", "expert"), "cuts"),
            P(("parts", "expert"), "cuts"),
            P(("parts", "expert"), None),
            P(("parts", "expert"), None),
            P("expert", None, "cuts"),
            P("expert", None, "cuts"),
            P("expert", "cuts", None),
            P("expert", None, "cuts"),
            P("expert", None, "cuts"),
            P("expert", None, "cuts"),
            P("expert", None, "cuts"),
            P("expert", None, "cuts"),
            P("expert", None, "cuts"),
        ),
        out_specs=(
            P(("parts", "expert"), "cuts"),
            P(("parts", "expert"), None, "cuts"),
            P(("parts", "expert"), None, "cuts"),
            P(("parts", "expert"), None, "cuts"),
            P(("parts", "expert"), None, "cuts"),
            P(("parts", "expert"), None, "cuts"),
            P(("parts", "expert"), None, "cuts"),
        ),
        check_vma=False,
    )
```

profile of v0, /device:TPU:0, one launch (start us, length us, event | category | flops | bytes accessed | tf_op | source)
XLA Modules:
  0.0 390.3 jit_solution(3270088173002684693)
XLA Ops:
  7.2 0.8 copy.35
  8.3 0.9 reduce-window.6
  9.6 1.3 broadcast_in_dim.2
  11.1 0.6 convolution_convert_fusion
  11.6 15.8 %all_to_all.15 = bf16[4,128,768]{2,1,0:T(8,128)(2,1)} all-to-all(bf16[4,128,768]{2,1,0:T(8,128)(2,1)S(1)} %bitcast.189), channel_id=1, replica_groups=mesh['parts'=2,'expert'=4,'cuts'=4] {'expert'}, dimensions={0} | all-to-all | bytes 1572864 | tf_op jit(solution)/shard_map/all_to_all | solution.py:56
  27.8 0.3 mul.94
  28.1 0.8 mul.95
  28.9 0.7 convolution_convert_fusion.1
  29.6 14.8 %all_to_all.16 = bf16[4,128,768]{2,1,0:T(8,128)(2,1)} all-to-all(bf16[4,128,768]{2,1,0:T(8,128)(2,1)S(1)} %bitcast.187), channel_id=1, replica_groups=mesh['parts'=2,'expert'=4,'cuts'=4] {'expert'}, dimensions={0} | all-to-all | bytes 1572864 | tf_op jit(solution)/shard_map/all_to_all | solution.py:57
  44.5 16.5 %all_gather.19 = bf16[2,16,3072]{2,1,0:T(8,128)(2,1)} all-gather(bf16[2,16,768]{2,1,0:T(8,128)(2,1)S(1)} %copy-done.11), channel_id=1, replica_groups=mesh['parts'=2,'expert'=4,'cuts'=4] {'cuts'}, dimensions={2}, use_global_device_ids=true | all-gather | bytes 245760 | tf_op jit(solution)/shard_map/all_gather | solution.py:60
  61.0 15.3 %all_gather.18 = bf16[2,16,3072]{2,1,0:T(8,128)(2,1)S(1)} all-gather(bf16[2,16,768]{2,1,0:T(8,128)(2,1)S(1)} %copy-done.12), channel_id=1, replica_groups=mesh['parts'=2,'expert'=4,'cuts'=4] {'cuts'}, dimensions={2}, use_global_device_ids=true | all-gather | bytes 245760 | tf_op jit(solution)/shard_map/all_gather | solution.py:61
  76.3 15.8 %all_gather.16 = bf16[2,16,3072]{2,1,0:T(8,128)(2,1)} all-gather(bf16[2,16,768]{2,1,0:T(8,128)(2,1)S(1)} %copy-done.13), channel_id=1, replica_groups=mesh['parts'=2,'expert'=4,'cuts'=4] {'cuts'}, dimensions={2}, use_global_device_ids=true | all-gather | bytes 245760 | tf_op jit(solution)/shard_map/all_gather | solution.py:62
  92.1 8.9 %all-gather.5.cloned.1.call-done = bf16[4,128,3072]{2,1,0:T(8,128)(2,1)} async-done(((bf16[4,128,768]{2,1,0:T(8,128)(2,1)}), bf16[4,128,3072]{2,1,0:T(8,128)(2,1)}) %all-gather.5.cloned.1.call-update) | async-done | bytes 3145744 | tf_op jit(solution)/shard_map/all_gather | solution.py:66
  101.0 4.0 %fusion.53 = bf16[4,2,64,16]{2,3,0,1:T(8,128)(2,1)} fusion(bf16[4,2,64,3072]{3,2,1,0:T(8,128)(2,1)} %bitcast.177, bf16[2,16,3072]{2,1,0:T(8,128)(2,1)S(1)} %all_gather.18), kind=kOutput, calls=%fused_computation.66 | convolution fusion | flops 50339840 | bytes 3358720 | tf_op jit(solution)/shard_map/blsd,lrd->blsr/dot_general | solution.py:88
  105.0 1.3 fusion.50
  106.3 58.4 %all-gather.3.cloned.1.call-done = bf16[4,128,3072]{2,1,0:T(8,128)(2,1)} async-done(((bf16[4,128,768]{2,1,0:T(8,128)(2,1)}), bf16[4,128,3072]{2,1,0:T(8,128)(2,1)}) %all-gather.3.cloned.1.call-update) | async-done | bytes 3145744 | tf_op jit(solution)/shard_map/all_gather | solution.py:67
  164.7 3.2 fusion.47
  167.9 14.7 %fusion.4 = f32[2,4,64,2048]{3,2,1,0:T(8,128)} fusion(bf16[2,2048,3072]{2,1,0:T(8,128)(2,1)} %param.19, bf16[4,2,64,3072]{3,2,1,0:T(8,128)(2,1)} %bitcast.185), kind=kOutput, calls=%fused_computation.4 | convolution fusion | flops 6442450944 | bytes 32505856 | tf_op jit(solution)/shard_map/blsd,lfd->blsf/dot_general | solution.py:73
  182.6 11.6 %fusion.2 = f32[2,4,64,2048]{3,2,1,0:T(8,128)S(1)} fusion(bf16[2,3072,2048]{2,1,0:T(8,128)(2,1)} %param.17, bf16[4,2,64,3072]{3,2,1,0:T(8,128)(2,1)S(1)} %bitcast.181), kind=kOutput, calls=%fused_computation.2 | convolution fusion | flops 6442450944 | bytes 32505856 | tf_op jit(solution)/shard_map/blsd,ldf->blsf/dot_general | solution.py:91
  194.2 13.8 %fusion.8 = f32[2,4,64,2048]{3,2,1,0:T(8,128)} fusion(bf16[2,3072,2048]{2,1,0:T(8,128)(2,1)} %param.18, bf16[4,2,64,3072]{3,2,1,0:T(8,128)(2,1)S(1)} %bitcast.182), kind=kOutput, calls=%fused_computation.8 | convolution fusion | flops 6442450944 | bytes 32505856 | tf_op jit(solution)/shard_map/blsd,ldf->blsf/dot_general | solution.py:97
  208.0 0.7 multiply_add_fusion.2
  208.9 0.7 multiply_add_fusion
  209.6 1.4 copy-done.17
  211.1 4.1 %fusion.17 = (bf16[4,2,64,2048]{3,2,0,1:T(8,128)(2,1)}, bf16[4,2,64,2048]{3,2,0,1:T(8,128)(2,1)}, bf16[4,2,64,2048]{3,2,0,1:T(8,128)(2,1)S(1)}) fusion(f32[2,4,64,2048]{3,2,1,0:T(8,128)S(1)} %multiply_add_fusion, f32[2,4,64,2048]{3,2,1,0:T(8,128)S(1)} %multiply_add_fusion.2, f32[2,4,64,2048]{3,2,1,0:T(8,128)S(1)} %copy-done.17, ...), kind=kOutput, calls=%fused_computation.23 | convolution fusion | flops 51380224 | bytes 19021824 | tf_op jit(solution)/shard_map/blsr,lrf->blsf/dot_general | solution.py:100
  215.2 0.9 convolution_bitcast_fusion.7
  216.1 14.5 %fusion.6 = f32[2,4,64,3072]{3,2,1,0:T(8,128)} fusion(bf16[4,2,64,2048]{3,2,0,1:T(8,128)(2,1)S(1)} %get-tuple-element.9, bf16[2,3072,2048]{2,1,0:T(8,128)(2,1)} %param.18), kind=kOutput, calls=%fused_computation.6 | convolution fusion | flops 6442450944 | bytes 33554432 | tf_op jit(solution)/shard_map/blsf,ldf->dbls/dot_general | solution.py:136
  230.5 2.5 convolution_bitcast_fusion.8
  233.0 14.0 %fusion = f32[2,4,64,3072]{3,2,1,0:T(8,128)} fusion(bf16[4,2,64,2048]{3,2,0,1:T(8,128)(2,1)} %get-tuple-element.8, bf16[2,3072,2048]{2,1,0:T(8,128)(2,1)} %param.17), kind=kOutput, calls=%fused_computation | convolution fusion | flops 6442450944 | bytes 33554432 | tf_op jit(solution)/shard_map/blsf,ldf->dbls/dot_general | solution.py:133
  247.1 2.7 fusion.63
  249.9 5.5 %fusion.19 = bf16[3072,4,2,64]{0,3,1,2:T(8,128)(2,1)S(1)} fusion(f32[2,4,64,3072]{3,2,1,0:T(8,128)S(1)} %fusion.63, f32[4,2,64,16]{2,3,0,1:T(8,128)S(1)} %convolution_bitcast_fusion.7, f32[2,4,64,3072]{3,2,1,0:T(8,128)} %fusion, f32[2,4,64,3072]{3,2,1,0:T(8,128)S(1)} %copy-done.2, bf16[2,16,3072]{2,1,0:T(8,128)(2,1)S(1)} %all_gather.18), kind=kOutput, calls=%fused_computation.29 | convolution fusion | flops 309854208 | bytes 22249472 | tf_op jit(solution)/shard_map/blsr,lrd->dbls/dot_general | solution.py:142
  255.4 1.8 copy.44
  257.5 0.6 copy-done.9
  258.1 2.5 convolution_bitcast_fusion.6
  260.6 4.5 %fusion.20 = f32[2,16,3072]{2,1,0:T(8,128)} fusion(f32[4,2,64,16]{2,3,0,1:T(8,128)S(1)} %convolution_bitcast_fusion.6, bf16[4,2,64,3072]{3,2,1,0:T(8,128)(2,1)} %bitcast.186), kind=kOutput, calls=%fused_computation.31 | convolution fusion | flops 302088192 | bytes 3571712 | tf_op jit(solution)/shard_map/blsr,blsd->lrd/dot_general | solution.py:169
  265.2 4.0 %fusion.22 = f32[2,16,3072]{2,1,0:T(8,128)} fusion(f32[4,2,64,16]{2,3,0,1:T(8,128)S(1)} %convolution_bitcast_fusion.8, bf16[4,2,64,3072]{3,2,1,0:T(8,128)(2,1)} %bitcast.178), kind=kOutput, calls=%fused_computation.35 | convolution fusion | flops 302088192 | bytes 3571712 | tf_op jit(solution)/shard_map/blsr,blsd->lrd/dot_general | solution.py:163
  269.7 4.1 %fusion.21 = f32[2,16,3072]{2,1,0:T(8,128)} fusion(f32[4,2,64,16]{2,3,0,1:T(8,128)S(1)} %convolution_bitcast_fusion.7, bf16[4,2,64,3072]{3,2,1,0:T(8,128)(2,1)} %bitcast.179), kind=kOutput, calls=%fused_computation.33 | convolution fusion | flops 302088192 | bytes 3571712 | tf_op jit(solution)/shard_map/blsr,blsd->lrd/dot_general | solution.py:166
  273.8 42.6 %reduce-scatter.5.cloned.1.call-done = bf16[768,512]{0,1:T(8,128)(2,1)} async-done(((bf16[3072,512]{0,1:T(8,128)(2,1)}), bf16[768,512]{0,1:T(8,128)(2,1)}) %reduce-scatter.5.cloned.1.call-update) | async-done | bytes 786448 | tf_op jit(solution)/shard_map/reduce_scatter | solution.py:145
  316.4 2.3 copy.45
  318.7 3.6 all-to-all-start.2
  322.3 2.7 fusion.27
  325.0 2.7 fusion.29
  327.8 1.1 fusion.28
  328.9 5.0 %all-to-all-done.2 = bf16[768,4,128]{2,0,1:T(8,128)(2,1)S(1)} async-done(((bf16[768,4,128]{2,0,1:T(8,128)(2,1)}), bf16[768,4,128]{2,0,1:T(8,128)(2,1)S(1)}, u32[]{:S(2)}, u32[]{:S(2)}) %all-to-all-start.2) | async-done | bytes 786464 | tf_op jit(solution)/shard_map/all_to_all | solution.py:154
  333.9 0.6 copy.46
  334.8 1.2 convolution_reduce_fusion
  336.1 3.6 reduce-scatter.11.cloned.1.call-done
  339.7 21.7 %reduce-scatter.7.cloned.1.call-done = f32[2,16,768]{2,1,0:T(8,128)} async-done(((f32[2,16,3072]{2,1,0:T(8,128)}), f32[2,16,768]{2,1,0:T(8,128)}) %reduce-scatter.7.cloned.1.call-update) | async-done | bytes 98320 | tf_op jit(solution)/shard_map/reduce_scatter | solution.py:176
  361.4 21.6 %reduce-scatter.9.cloned.1.call-done = f32[2,16,768]{2,1,0:T(8,128)} async-done(((f32[2,16,3072]{2,1,0:T(8,128)}), f32[2,16,768]{2,1,0:T(8,128)}) %reduce-scatter.9.cloned.1.call-update) | async-done | bytes 98320 | tf_op jit(solution)/shard_map/reduce_scatter | solution.py:177
  (59 shorter events, 2.8 us)
Async XLA Ops:
  7.2 202.5 %copy-start = (bf16[2,16,2048]{2,1,0:T(8,128)(2,1)S(1)}, bf16[2,16,2048]{2,1,0:T(8,128)(2,1)}, u32[]{:S(2)}) copy-start(bf16[2,16,2048]{2,1,0:T(8,128)(2,1)} %param.23) | copy-start | bytes 393220
  7.2 20.3 %copy-start.16 = (f32[192,2]{0,1:T(2,128)S(1)}, f32[192,2]{0,1:T(2,128)}, u32[]{:S(2)}) copy-start(f32[192,2]{0,1:T(2,128)} %param.16) | copy-start | bytes 4612
  7.2 93.8 %all-gather.5.cloned.1.call-start = ((), (), s32[]{:S(2)}) async-start(), calls=%async_computation.8 | async-start | bytes 3932160 | tf_op jit(solution)/shard_map/all_gather | solution.py:66
  8.2 19.6 %copy-start.10 = (bf16[192,768]{1,0:T(8,128)(2,1)S(1)}, bf16[192,768]{1,0:T(8,128)(2,1)}, u32[]{:S(2)}) copy-start(bf16[192,768]{1,0:T(8,128)(2,1)} %param.14) | copy-start | bytes 884740
  27.4 137.3 %all-gather.3.cloned.1.call-start = ((), (), s32[]{:S(2)}) async-start(), calls=%async_computation.7 | async-start | bytes 3932160 | tf_op jit(solution)/shard_map/all_gather | solution.py:67
  28.1 16.4 %copy-start.11 = (bf16[2,16,768]{2,1,0:T(8,128)(2,1)S(1)}, bf16[2,16,768]{2,1,0:T(8,128)(2,1)}, u32[]{:S(2)}) copy-start(bf16[2,16,768]{2,1,0:T(8,128)(2,1)} %param.20) | copy-start | bytes 147460
  28.1 32.9 %copy-start.12 = (bf16[2,16,768]{2,1,0:T(8,128)(2,1)S(1)}, bf16[2,16,768]{2,1,0:T(8,128)(2,1)}, u32[]{:S(2)}) copy-start(bf16[2,16,768]{2,1,0:T(8,128)(2,1)} %param.22) | copy-start | bytes 147460
  28.1 48.2 %copy-start.13 = (bf16[2,16,768]{2,1,0:T(8,128)(2,1)S(1)}, bf16[2,16,768]{2,1,0:T(8,128)(2,1)}, u32[]{:S(2)}) copy-start(bf16[2,16,768]{2,1,0:T(8,128)(2,1)} %param.25) | copy-start | bytes 147460
  44.4 272.0 %reduce-scatter.5.cloned.1.call-start = ((), (), s32[]{:S(2)}) async-start(), calls=%async_computation.9 | async-start | bytes 3932160 | tf_op jit(solution)/shard_map/reduce_scatter | solution.py:145
  101.0 4.0 %copy-start.3 = (bf16[4,128,3072]{2,1,0:T(8,128)(2,1)S(1)}, bf16[4,128,3072]{2,1,0:T(8,128)(2,1)}, u32[]{:S(2)}) copy-start(bf16[4,128,3072]{2,1,0:T(8,128)(2,1)} %all-gather.5.cloned.1.call-done) | copy-start | bytes 9437188
  101.0 4.0 %copy-start.5 = (bf16[2,16,3072]{2,1,0:T(8,128)(2,1)S(1)}, bf16[2,16,3072]{2,1,0:T(8,128)(2,1)}, u32[]{:S(2)}) copy-start(bf16[2,16,3072]{2,1,0:T(8,128)(2,1)} %all_gather.19) | copy-start | bytes 589828
  194.2 13.8 %copy-start.4 = (f32[2,4,64,2048]{3,2,1,0:T(8,128)S(1)}, f32[2,4,64,2048]{3,2,1,0:T(8,128)}, u32[]{:S(2)}) copy-start(f32[2,4,64,2048]{3,2,1,0:T(8,128)} %fusion.4) | copy-start | bytes 12582916
  194.2 13.8 %copy-start.8 = (bf16[2,16,2048]{2,1,0:T(8,128)(2,1)S(1)}, bf16[2,16,2048]{2,1,0:T(8,128)(2,1)}, u32[]{:S(2)}) copy-start(bf16[2,16,2048]{2,1,0:T(8,128)(2,1)} %param.24) | copy-start | bytes 393220
  208.0 0.9 copy-start.7
  208.9 0.8 copy-start.14
  208.9 2.2 copy-start.17
  233.0 14.0 %copy-start.6 = (bf16[2,16,3072]{2,1,0:T(8,128)(2,1)S(1)}, bf16[2,16,3072]{2,1,0:T(8,128)(2,1)}, u32[]{:S(2)}) copy-start(bf16[2,16,3072]{2,1,0:T(8,128)(2,1)} %all_gather.19) | copy-start | bytes 589828
  247.1 2.8 copy-start.2
  257.2 0.9 copy-start.9
  257.2 82.5 %reduce-scatter.11.cloned.1.call-start = ((), (), s32[]{:S(2)}) async-start(), calls=%async_computation.12 | async-start | bytes 491520 | tf_op jit(solution)/shard_map/reduce_scatter | solution.py:178
  265.1 96.2 %reduce-scatter.7.cloned.1.call-start = ((), (), s32[]{:S(2)}) async-start(), calls=%async_computation.10 | async-start | bytes 491520 | tf_op jit(solution)/shard_map/reduce_scatter | solution.py:176
  269.3 113.7 %reduce-scatter.9.cloned.1.call-start = ((), (), s32[]{:S(2)}) async-start(), calls=%async_computation.11 | async-start | bytes 491520 | tf_op jit(solution)/shard_map/reduce_scatter | solution.py:177
  318.7 9.1 %copy-start.15 = (bf16[4,2,64,16]{2,3,0,1:T(8,128)(2,1)S(1)}, bf16[4,2,64,16]{2,3,0,1:T(8,128)(2,1)}, u32[]{:S(2)}) copy-start(bf16[4,2,64,16]{2,3,0,1:T(8,128)(2,1)} %fusion.53) | copy-start | bytes 49156
  318.7 15.3 %all-to-all-start.2 = ((bf16[768,4,128]{2,0,1:T(8,128)(2,1)}), bf16[768,4,128]{2,0,1:T(8,128)(2,1)S(1)}, u32[]{:S(2)}, u32[]{:S(2)}) async-start(bf16[768,4,128]{2,0,1:T(8,128)(2,1)} %copy.45), calls=%async_computation.3 | async-start | bytes 1572864 | tf_op jit(solution)/shard_map/all_to_all | solution.py:154
  327.8 55.2 %copy-start.1 = (bf16[2,16,2048]{2,1,0:T(8,128)(2,1)S(1)}, bf16[2,16,2048]{2,1,0:T(8,128)(2,1)}, u32[]{:S(2)}) copy-start(bf16[2,16,2048]{2,1,0:T(8,128)(2,1)} %param.23) | copy-start | bytes 393220
Sparse Core Ops, SparseCore 0:
  27.6 73.3 all-gather.4
  102.5 62.1 all-gather.2
  257.3 58.9 reduce-scatter.4
  319.1 20.5 reduce-scatter.10
  342.5 18.8 reduce-scatter.6
  364.1 18.8 reduce-scatter.8
where the time goes:
time: 396 us; the launch traced here: 390 us
  waiting for transfers between devices  162 us (41%)
  matrix products  118 us (30%)
  blocking collectives  78.2 us (20%)
  between operations  14.8 us (4%)
  local copies, waits for them, and re-layouts  11.8 us (3%)
  starting transfers between devices  4.12 us (1%)
    all_gather x1, waiting for transfers between devices, body(): lax.all_gather(recv_grad, 'cuts', axis=2, tiled=True)  58.4 us
    reduce_scatter x1, waiting for transfers between devices, body(): lax.psum_scatter((partial_product + adapter_scale * adapter_product).resh...  42.6 us
    reduce_scatter x1, waiting for transfers between devices, body(): lax.psum_scatter(gate_adapter_product, 'cuts', scatter_dimension=2, tiled...  21.7 us
    reduce_scatter x1, waiting for transfers between devices, body(): lax.psum_scatter(up_adapter_product, 'cuts', scatter_dimension=2, tiled=T...  21.6 us
    all_gather x1, blocking collectives, body(): lax.all_gather(gate_in, 'cuts', axis=2, tiled=True)  16.5 us
    all_gather x1, blocking collectives, body(): lax.all_gather(down_out, 'cuts', axis=2, tiled=True)  15.8 us
    all_to_all x1, blocking collectives, body(): lax.all_to_all(send_input, 'expert', split_axis=0, concat_axis=0, tiled=T...  15.8 us
    all_gather x1, blocking collectives, body(): lax.all_gather(up_in, 'cuts', axis=2, tiled=True)  15.3 us
  transfers between devices with their start and end apart: 7, of which 7 were waited for; matrix products, arithmetic and copies ran while one was open for 9% of the time, Pallas kernels for 0%

commit v1 on v0

v1 whole, which is shorter than its diff:
```python
import functools

import jax
import jax.numpy as jnp
from jax import lax
from jax.experimental import pallas as pl
from jax.experimental.pallas import tpu as pltpu
from jax.sharding import PartitionSpec as P

EXPERTS = 8
SLOT = 64

adapter_scale = 0.25

F32 = jnp.float32
BF16 = jnp.bfloat16
NN = (((1,), (0,)), ((), ()))
NT = (((1,), (1,)), ((), ()))


def mm(a, b, dims=NN):
    return lax.dot_general(a, b, dims, preferred_element_type=F32)


def params(semantics):
    return pltpu.CompilerParams(dimension_semantics=semantics, vmem_limit_bytes=56 * 1024 * 1024)


def swap(x, k, axis):
    n = lax.axis_size(axis)
    return lax.ppermute(x, axis, [(i, i ^ k) for i in range(n)])


def forward_kernel(x_ref, wg_ref, wu_ref, low_ref, go_ref, uo_ref, a_ref, b_ref, h_ref):
    x = x_ref[0]
    rank = go_ref.shape[1]
    low = low_ref[0]
    gate = mm(x, wg_ref[0]) + adapter_scale * mm(low[:, :rank], go_ref[0])
    up = mm(x, wu_ref[0]) + adapter_scale * mm(low[:, rank:], uo_ref[0])
    q = jax.nn.sigmoid(gate)
    silu = gate * q
    a_ref[0] = (up * q * (1.0 + gate * (1.0 - q))).astype(BF16)
    b_ref[0] = silu.astype(BF16)
    h_ref[0] = (silu * up).astype(BF16)


def forward(rows, wg, wu, low, go, uo):
    count, n, width = rows.shape
    units = wg.shape[2]
    rank = go.shape[1]
    ft = min(512, units)
    out = jax.ShapeDtypeStruct((count, n, units), BF16)
    wide = pl.BlockSpec((1, n, ft), lambda l, f: (l, 0, f))
    weight = pl.BlockSpec((1, width, ft), lambda l, f: (l, 0, f))
    factor = pl.BlockSpec((1, rank, ft), lambda l, f: (l, 0, f))
    return pl.pallas_call(
        forward_kernel,
        grid=(count, units // ft),
        in_specs=[
            pl.BlockSpec((1, n, width), lambda l, f: (l, 0, 0)),
            weight,
            weight,
            pl.BlockSpec((1, n, 2 * rank), lambda l, f: (l, 0, 0)),
            factor,
            factor,
        ],
        out_specs=[wide, wide, wide],
        out_shape=[out, out, out],
        compiler_params=params(("arbitrary", "arbitrary")),
        cost_estimate=pl.CostEstimate(
            flops=4 * count * n * width * units,
            bytes_accessed=4 * count * width * units,
            transcendentals=count * n * units,
        ),
        name="forward_units",
    )(rows, wg, wu, low, go, uo)


def hidden_kernel(
    g_ref, wd_ref, low_ref, lowt_ref, di_ref, go_ref, uo_ref, a_ref, b_ref, h_ref,
    gg_ref, ug_ref, ggo_ref, guo_ref, gdi_ref, proj_ref,
):
    rank = di_ref.shape[1]
    hg = mm(g_ref[0], wd_ref[0], NT) + adapter_scale * mm(low_ref[0], di_ref[0])
    gg = (hg * a_ref[0].astype(F32)).astype(BF16)
    ug = (hg * b_ref[0].astype(F32)).astype(BF16)
    h = h_ref[0]
    gg_ref[0] = gg
    ug_ref[0] = ug
    lowt = lowt_ref[0]
    ggo_ref[0] = adapter_scale * mm(lowt[:rank], gg)
    guo_ref[0] = adapter_scale * mm(lowt[rank : 2 * rank], ug)
    gdi_ref[0] = adapter_scale * mm(lowt[2 * rank :], h)
    proj = jnp.concatenate(
        [mm(gg, go_ref[0], NT), mm(ug, uo_ref[0], NT), mm(h, di_ref[0], NT)], axis=1
    )

    @pl.when(pl.program_id(1) == 0)
    def _():
        proj_ref[0] = proj

    @pl.when(pl.program_id(1) > 0)
    def _():
        proj_ref[0] = proj_ref[0] + proj


def hidden_back(rows, wd, low, lowt, di, go, uo, a, b, h):
    count, n, width = rows.shape
    units = wd.shape[1]
    rank = di.shape[1]
    ft = min(512, units)
    wide = pl.BlockSpec((1, n, ft), lambda l, f: (l, 0, f))
    factor = pl.BlockSpec((1, rank, ft), lambda l, f: (l, 0, f))
    return pl.pallas_call(
        hidden_kernel,
        grid=(count, units // ft),
        in_specs=[
            pl.BlockSpec((1, n, width), lambda l, f: (l, 0, 0)),
            pl.BlockSpec((1, ft, width), lambda l, f: (l, f, 0)),
            pl.BlockSpec((1, n, rank), lambda l, f: (l, 0, 0)),
            pl.BlockSpec((1, 3 * rank, n), lambda l, f: (l, 0, 0)),
            factor,
            factor,
            factor,
            wide,
            wide,
            wide,
        ],
        out_specs=[
            wide,
            wide,
            factor,
            factor,
            factor,
            pl.BlockSpec((1, n, 3 * rank), lambda l, f: (l, 0, 0)),
        ],
        out_shape=[
            jax.ShapeDtypeStruct((count, n, units), BF16),
            jax.ShapeDtypeStruct((count, n, units), BF16),
            jax.ShapeDtypeStruct((count, rank, units), F32),
            jax.ShapeDtypeStruct((count, rank, units), F32),
            jax.ShapeDtypeStruct((count, rank, units), F32),
            jax.ShapeDtypeStruct((count, n, 3 * rank), F32),
        ],
        compiler_params=params(("arbitrary", "arbitrary")),
        cost_estimate=pl.CostEstimate(
            flops=2 * count * n * width * units,
            bytes_accessed=2 * count * width * units,
            transcendentals=0,
        ),
        name="hidden_back",
    )(rows, wd, low, lowt, di, go, uo, a, b, h)


def rows_kernel(with_adapter, place_ref, gg_ref, ug_ref, wg_ref, wu_ref, back_ref, *rest):
    if with_adapter:
        proj_ref, in_ref, out_ref, y_ref = rest
    else:
        out_ref, y_ref = rest
    l = pl.program_id(1)
    count = pl.num_programs(1)
    y = mm(gg_ref[0], wg_ref[0], NT) + mm(ug_ref[0], wu_ref[0], NT)
    if with_adapter:
        y = y + adapter_scale * mm(proj_ref[0], in_ref[0])
    groups = back_ref.shape[0]
    tokens = back_ref.shape[1]
    y_ref[l] = y.astype(BF16).reshape(groups, SLOT, -1)

    @pl.when(l == count - 1)
    def _():
        for g in range(groups):
            held = y_ref[:, g].reshape(-1, y_ref.shape[3])
            out_ref[g * tokens : (g + 1) * tokens] = mm(back_ref[g], held).astype(BF16)


def row_back(place, gg, ug, wg, wu, back, span, adapter=None):
    count, n, units = gg.shape
    groups, tokens, _ = back.shape
    dt = 384 if span % 384 == 0 else span
    tiles = span // dt
    rows_spec = pl.BlockSpec((1, n, units), lambda d, l, p: (l, 0, 0))
    weight = pl.BlockSpec((1, dt, units), lambda d, l, p: (l, p[0] * tiles + d, 0))
    in_specs = [
        rows_spec,
        rows_spec,
        weight,
        weight,
        pl.BlockSpec(back.shape, lambda d, l, p: (0, 0, 0)),
    ]
    operands = [gg, ug, wg, wu, back]
    if adapter is not None:
        proj, factor = adapter
        in_specs += [
            pl.BlockSpec((1, n, proj.shape[2]), lambda d, l, p: (l, 0, 0)),
            pl.BlockSpec((1, factor.shape[1], dt), lambda d, l, p: (l, 0, d)),
        ]
        operands += [proj, factor]
    return pl.pallas_call(
        functools.partial(rows_kernel, adapter is not None),
        grid_spec=pltpu.PrefetchScalarGridSpec(
            num_scalar_prefetch=1,
            grid=(tiles, count),
            in_specs=in_specs,
            out_specs=pl.BlockSpec((groups * tokens, dt), lambda d, l, p: (0, d)),
            scratch_shapes=[pltpu.VMEM((count, groups, SLOT, dt), BF16)],
        ),
        out_shape=jax.ShapeDtypeStruct((groups * tokens, span), BF16),
        compiler_params=params(("arbitrary", "arbitrary")),
        cost_estimate=pl.CostEstimate(
            flops=4 * count * n * span * units,
            bytes_accessed=4 * count * span * units,
            transcendentals=0,
        ),
        name="row_back",
    )(place, *operands)


def routing(ids, gates, me, order, local_count):
    groups, tokens, _ = ids.shape
    flat = ids.reshape(groups, 2 * tokens)
    onehot = (flat[:, :, None] == jnp.arange(EXPERTS, dtype=jnp.int32)).astype(jnp.int32)
    earlier = jnp.sum((jnp.cumsum(onehot, axis=1) - 1) * onehot, axis=2)
    target = (flat * SLOT + earlier).reshape(groups, 1, tokens, 2)
    slots = me * (local_count * SLOT) + jnp.arange(local_count * SLOT, dtype=jnp.int32)
    match = target == slots[None, :, None, None]
    match = jnp.take(match, order, axis=0)
    gates = jnp.take(gates, order, axis=0)
    place = jnp.any(match, axis=3).astype(BF16)
    slot_gate = jnp.sum(jnp.where(match, gates[:, None], 0.0), axis=(2, 3))
    return place, jnp.swapaxes(place, 1, 2), slot_gate


def body(
    inputs,
    out_grad,
    experts,
    route_gates,
    gate_proj,
    up_proj,
    down_proj,
    gate_in,
    gate_out,
    up_in,
    up_out,
    down_in,
    down_out,
):
    groups = lax.axis_size("expert")
    cuts = lax.axis_size("cuts")
    me = lax.axis_index("expert")
    cut = lax.axis_index("cuts")
    count = gate_proj.shape[0]
    tokens, col = inputs.shape
    width = gate_proj.shape[1]
    rank = gate_in.shape[1]
    n = groups * SLOT
    paired = groups == 4 and cuts == 4

    routes = lax.all_gather(
        jnp.concatenate([experts.astype(F32), route_gates], axis=1), "expert"
    )
    relative = jnp.array([0, 2, 1, 3] if paired else list(range(groups)), jnp.int32)
    order = relative ^ me if paired else relative
    place, back, slot_gate = routing(
        routes[:, :, :2].astype(jnp.int32), routes[:, :, 2:], me, order, count
    )

    def to_rows(held, gate=None):
        rows = jnp.einsum("gst,gtd->gsd", place, held, preferred_element_type=F32)
        if gate is not None:
            rows = rows * gate[:, :, None]
        rows = rows.astype(BF16).reshape(groups, count, SLOT, -1)
        return jnp.swapaxes(rows, 0, 1).reshape(count, n, -1)

    def spread(x):
        if not paired:
            return lax.all_gather(x, "expert")
        mine = jnp.stack([x, swap(x, 2, "expert")])
        return jnp.concatenate([mine, swap(mine, 1, "expert")])

    def sum_cuts(x):
        if not paired:
            return lax.psum(x, "cuts")
        x = x.astype(BF16)
        total = x.astype(F32)
        for k in (1, 2, 3):
            total = total + swap(x, k, "cuts").astype(F32)
        return total

    def collect(x, gate=None):
        if not paired:
            own = to_rows(spread(x), gate)
            return lax.all_gather(own, "cuts", axis=2, tiled=True), own
        arrived = [x] + [swap(x, k, "cuts") for k in (1, 2, 3)]
        rows = jnp.zeros((count, n, width), BF16)
        own = None
        for k in range(4):
            part = to_rows(spread(arrived[k]), gate)
            if k == 0:
                own = part
            rows = lax.dynamic_update_slice(rows, part, (0, 0, (cut ^ k) * col))
        return rows, own

    rows_x, own_x = collect(inputs)
    factor_x = jnp.concatenate([gate_in, up_in], axis=1)
    low_x = sum_cuts(
        jnp.einsum("lnd,lrd->lnr", own_x, factor_x, preferred_element_type=F32)
    ).astype(BF16)
    a, b, h = forward(rows_x, gate_proj, up_proj, low_x, gate_out, up_out)

    rows_g, own_g = collect(out_grad, slot_gate)
    low_g = sum_cuts(
        jnp.einsum("lnd,lrd->lnr", own_g, down_out, preferred_element_type=F32)
    ).astype(BF16)
    lowt = jnp.swapaxes(jnp.concatenate([low_x, low_g], axis=2), 1, 2)
    gg, ug, gate_output_gradient, up_output_gradient, down_input_gradient, proj = hidden_back(
        rows_g, down_proj, low_g, lowt, down_in, gate_out, up_out, a, b, h
    )
    proj = sum_cuts(proj).astype(BF16)
    proj_x = proj[:, :, : 2 * rank]
    proj_g = proj[:, :, 2 * rank :]
    grad_x = adapter_scale * jnp.einsum(
        "lnr,lnd->lrd", proj_x, own_x, preferred_element_type=F32
    )
    grad_down_out = adapter_scale * jnp.einsum(
        "lnr,lnd->lrd", proj_g, own_g, preferred_element_type=F32
    )

    back_rows = functools.partial(row_back, gg=gg, ug=ug, wg=gate_proj, wu=up_proj, back=back)
    if paired:
        total = jnp.zeros((tokens, col), F32)
        for k in (2, 3, 1, 0):
            chunk = back_rows(
                jnp.reshape(cut ^ k, (1,)).astype(jnp.int32),
                span=col,
                adapter=(proj_x, factor_x) if k == 0 else None,
            )
            half = 2 * tokens
            chunk = chunk[:half].astype(F32) + swap(chunk[half:], 1, "expert").astype(F32)
            chunk = chunk[:tokens] + swap(chunk[tokens:].astype(BF16), 2, "expert").astype(F32)
            if k:
                chunk = swap(chunk.astype(BF16), k, "cuts").astype(F32)
            total = total + chunk
        input_grad = total.astype(BF16)
    else:
        chunk = back_rows(jnp.zeros((1,), jnp.int32), span=width)
        local = mm_adapter(proj_x, factor_x, back)
        chunk = chunk.astype(F32) + lax.dynamic_update_slice(
            jnp.zeros(chunk.shape, F32), local, (0, cut * col)
        )
        chunk = lax.psum_scatter(
            chunk.astype(BF16), "expert", scatter_dimension=0, tiled=True
        )
        input_grad = lax.psum_scatter(chunk, "cuts", scatter_dimension=1, tiled=True)
    return (
        input_grad,
        grad_x[:, :rank],
        gate_output_gradient,
        grad_x[:, rank:],
        up_output_gradient,
        down_input_gradient,
        grad_down_out,
    )


def mm_adapter(proj, factor, back):
    count, n, _ = proj.shape
    groups, tokens, _ = back.shape
    term = adapter_scale * jnp.einsum("lnr,lrd->lnd", proj, factor, preferred_element_type=F32)
    term = term.astype(BF16).reshape(count, groups, SLOT, -1)
    term = jnp.swapaxes(term, 0, 1).reshape(groups, count * SLOT, -1)
    return jnp.einsum("gts,gsd->gtd", back, term, preferred_element_type=F32).reshape(
        groups * tokens, -1
    )


def solution(mesh):
    return jax.shard_map(
        body,
        mesh=mesh,
        in_specs=(
            P(("parts", "expert"), "cuts"),
            P(("parts", "expert"), "cuts"),
            P(("parts", "expert"), None),
            P(("parts", "expert"), None),
            P("expert", None, "cuts"),
            P("expert", None, "cuts"),
            P("expert", "cuts", None),
            P("expert", None, "cuts"),
            P("expert", None, "cuts"),
            P("expert", None, "cuts"),
            P("expert", None, "cuts"),
            P("expert", None, "cuts"),
            P("expert", None, "cuts"),
        ),
        out_specs=(
            P(("parts", "expert"), "cuts"),
            P(("parts", "expert"), None, "cuts"),
            P(("parts", "expert"), None, "cuts"),
            P(("parts", "expert"), None, "cuts"),
            P(("parts", "expert"), None, "cuts"),
            P(("parts", "expert"), None, "cuts"),
            P(("parts", "expert"), None, "cuts"),
        ),
        check_vma=False,
    )
```

time: 396 us -> 246 us (0.62); the launches traced: 390 us -> 245 us
  matrix products: 118 us -> 10.8 us
  waiting for transfers between devices: 162 us -> 57.8 us
  Pallas kernels: 0 us -> 91.2 us
  blocking collectives: 78.2 us -> 8.45 us
  starting transfers between devices: 4.12 us -> 40.9 us
  other arithmetic: 1.18 us -> 16 us
  between operations: 14.8 us -> 1.56 us
  local copies, waits for them, and re-layouts: 11.8 us -> 18.2 us
    dot_general x25 -> x12, matrix products: 118 us -> 10.8 us  [the longest x8 8.91 us: to_rows(): rows = jnp.einsum('gst,gtd->gsd', place, held, preferred_element_type=F32)]
    pallas_call x0 -> x6, Pallas kernels: none -> 91.2 us  [the longest x4 46.2 us: row_back(): pl.pallas_call(functools.partial(rows_kernel, adapter is not None), grid_...]
    reduce_scatter x4 -> x0, waiting for transfers between devices: 89.5 us -> none  [the longest x1 42.6 us: body(): lax.psum_scatter((partial_product + adapter_scale * adapter_product).resh...]
    all_gather x2 -> x0, waiting for transfers between devices: 67.3 us -> none  [the longest x1 58.4 us: body(): lax.all_gather(recv_grad, 'cuts', axis=2, tiled=True)]
    ppermute x0 -> x42, waiting for transfers between devices: none -> 57.8 us  [swap(): return lax.ppermute(x, axis, [(i, i ^ k) for i in range(n)])]
    ppermute x0 -> x42, starting transfers between devices: none -> 40.9 us  [swap(): return lax.ppermute(x, axis, [(i, i ^ k) for i in range(n)])]
    all_gather x3 -> x1, blocking collectives: 47.6 us -> 8.45 us  [body(): lax.all_gather(jnp.concatenate([experts.astype(F32), route_gates], axis=1...]
    all_to_all x2 -> x0, blocking collectives: 30.5 us -> none  [the longest x1 15.8 us: body(): lax.all_to_all(send_input, 'expert', split_axis=0, concat_axis=0, tiled=T...]
  transfers between devices with their start and end apart: 7 -> 42, of which waited for: 7 -> 11; matrix products, arithmetic and copies ran while one was open for 9% -> 14% of each run, Pallas kernels for 0% -> 19%
where the time goes in v1:
time: 246 us; the launch traced here: 245 us
  Pallas kernels  91.2 us (37%)
  waiting for transfers between devices  57.8 us (23%)
  starting transfers between devices  40.9 us (17%)
  local copies, waits for them, and re-layouts  18.2 us (7%)
  other arithmetic  16 us (7%)
  matrix products  10.8 us (4%)
  blocking collectives  8.45 us (3%)
    ppermute x42, waiting for transfers between devices, swap(): return lax.ppermute(x, axis, [(i, i ^ k) for i in range(n)])  57.8 us
    pallas_call x4, Pallas kernels, row_back(): pl.pallas_call(functools.partial(rows_kernel, adapter is not None), grid_...  46.2 us
    ppermute x42, starting transfers between devices, swap(): return lax.ppermute(x, axis, [(i, i ^ k) for i in range(n)])  40.9 us
    pallas_call x1, Pallas kernels, forward(): pl.pallas_call(forward_kernel, grid=(count, units // ft), in_specs=[pl.Bl...  26 us
    pallas_call x1, Pallas kernels, hidden_back(): pl.pallas_call(hidden_kernel, grid=(count, units // ft), in_specs=[pl.Blo...  19 us
    dot_general x8, matrix products, to_rows(): rows = jnp.einsum('gst,gtd->gsd', place, held, preferred_element_type=F32)  8.91 us
    all_gather x1, blocking collectives, body(): lax.all_gather(jnp.concatenate([experts.astype(F32), route_gates], axis=1...  8.45 us
    unnamed x89, local copies, waits for them, and re-layouts  7.34 us
  transfers between devices with their start and end apart: 42, of which 11 were waited for; matrix products, arithmetic and copies ran while one was open for 14% of the time, Pallas kernels for 19%

profile of v1, /device:TPU:0, one launch (start us, length us, event | category | flops | bytes accessed | tf_op | source)
XLA Modules:
  0.0 244.9 jit_solution(8455954479511612117)
XLA Ops:
  0.6 3.0 %collective-permute-start.14 = (bf16[192,768]{1,0:T(8,128)(2,1)}, bf16[192,768]{1,0:T(8,128)(2,1)S(1)}, u32[]{:S(2)}, u32[]{:S(2)}) collective-permute-start(bf16[192,768]{1,0:T(8,128)(2,1)} %param.14), channel_id=1, source_target_pairs={{0,8},{4,12},{8,0},{12,4},{1,9},{5,13},{9,1},{13,5},{2,10},{6,14},... | collective-permute-start | bytes 884744 | tf_op jit(solution)/shard_map/ppermute | solution.py:31
  3.7 1.6 collective-permute-start.19
  5.2 2.6 %collective-permute-start.22 = (bf16[192,768]{1,0:T(8,128)(2,1)}, bf16[192,768]{1,0:T(8,128)(2,1)S(1)}, u32[]{:S(2)}, u32[]{:S(2)}) collective-permute-start(bf16[192,768]{1,0:T(8,128)(2,1)} %param.14), channel_id=1, source_target_pairs={{0,2},{1,3},{2,0},{3,1},{4,6},{5,7},{6,4},{7,5},{8,10},{9,11},{10,... | collective-permute-start | bytes 884744 | tf_op jit(solution)/shard_map/ppermute | solution.py:31
  9.7 8.4 %all-gather.1 = f32[4,192,4]{1,2,0:T(4,128)S(1)} all-gather(f32[1,192,4]{1,2,0:T(4,128)S(1)} %maximum_bitcast_fusion.1), channel_id=2, replica_groups=mesh['parts'=2,'expert'=4,'cuts'=4] {'expert'}, dimensions={0}, use_global_device_ids=true | all-gather | bytes 15360 | tf_op jit(solution)/shard_map/all_gather | solution.py:259
  18.6 3.4 %reduce-window.6 = s32[4,8,3,128]{3,1,2,0:T(8,128)S(1)} reduce-window(s32[4,8,3,128]{3,1,2,0:T(8,128)S(1)} %fusion.47, s32[]{:T(128)} %constant.31.clone.1), window={size=1x1x1x128 pad=0_0x0_0x0_0x127_0}, to_apply=%region_0.0 | reduce-window | flops 1560576 | bytes 98308 | tf_op jit(solution)/shard_map/reduce-window
  25.6 1.9 collective-permute-start.2
  27.5 1.6 collective-permute-start.20
  29.2 2.7 %collective-permute-start.5 = (bf16[192,768]{1,0:T(8,128)(2,1)S(1)}, bf16[192,768]{1,0:T(8,128)(2,1)S(1)}, u32[]{:S(2)}, u32[]{:S(2)}) collective-permute-start(bf16[192,768]{1,0:T(8,128)(2,1)S(1)} %copy-done.17), channel_id=1, source_target_pairs={{0,2},{1,3},{2,0},{3,1},{4,6},{5,7},{6,4},{7,5},{8,10},{9,11},{10,... | collective-permute-start | bytes 884744 | tf_op jit(solution)/shard_map/ppermute | solution.py:31
  32.5 6.3 %collective-permute-done.2 = bf16[192,768]{1,0:T(8,128)(2,1)S(1)} collective-permute-done((bf16[192,768]{1,0:T(8,128)(2,1)S(1)}, bf16[192,768]{1,0:T(8,128)(2,1)S(1)}, u32[]{:S(2)}, u32[]{:S(2)}) %collective-permute-start.2) | collective-permute-done | bytes 294944 | tf_op jit(solution)/shard_map/ppermute | solution.py:31
  38.8 2.5 %collective-permute-start.26 = (bf16[192,768]{1,0:T(8,128)(2,1)S(1)}, bf16[192,768]{1,0:T(8,128)(2,1)S(1)}, u32[]{:S(2)}, u32[]{:S(2)}) collective-permute-start(bf16[192,768]{1,0:T(8,128)(2,1)S(1)} %collective-permute-done.25), channel_id=1, source_target_pairs={{0,8},{4,12},{8,0},{12,4},{1,9},{5,13},{9,1},{13,5},{2,10},{6,14},... | collective-permute-start | bytes 884744 | tf_op jit(solution)/shard_map/ppermute | solution.py:31
  42.3 11.2 %collective-permute-done.5 = bf16[192,768]{1,0:T(8,128)(2,1)S(1)} collective-permute-done((bf16[192,768]{1,0:T(8,128)(2,1)S(1)}, bf16[192,768]{1,0:T(8,128)(2,1)S(1)}, u32[]{:S(2)}, u32[]{:S(2)}) %collective-permute-start.5) | collective-permute-done | bytes 294944 | tf_op jit(solution)/shard_map/ppermute | solution.py:31
  55.3 1.5 collective-permute-start.9
  58.7 4.8 %collective-permute-done.6 = bf16[192,768]{1,0:T(8,128)(2,1)S(1)} collective-permute-done((bf16[192,768]{1,0:T(8,128)(2,1)S(1)}, bf16[192,768]{1,0:T(8,128)(2,1)S(1)}, u32[]{:S(2)}, u32[]{:S(2)}) %collective-permute-start.6) | collective-permute-done | bytes 294944 | tf_op jit(solution)/shard_map/ppermute | solution.py:31
  64.5 4.9 %collective-permute-done.9 = bf16[192,768]{1,0:T(8,128)(2,1)S(1)} collective-permute-done((bf16[192,768]{1,0:T(8,128)(2,1)S(1)}, bf16[192,768]{1,0:T(8,128)(2,1)S(1)}, u32[]{:S(2)}, u32[]{:S(2)}) %collective-permute-start.9) | collective-permute-done | bytes 294944 | tf_op jit(solution)/shard_map/ppermute | solution.py:31
  71.1 3.0 %collective-permute-start.12 = (bf16[2,256,16]{1,2,0:T(8,128)(2,1)S(1)}, bf16[2,256,16]{1,2,0:T(8,128)(2,1)S(1)}, u32[]{:S(2)}, u32[]{:S(2)}) collective-permute-start(bf16[2,256,16]{1,2,0:T(8,128)(2,1)S(1)} %convolution_convert_fusion.5), channel_id=1, source_target_pairs={{0,2},{1,3},{2,0},{3,1},{4,6},{5,7},{6,4},{7,5},{8,10},{9,11},{10,... | collective-permute-start | bytes 49160 | tf_op jit(solution)/shard_map/ppermute | solution.py:31
  74.1 1.4 collective-permute-start.13
  77.6 1.1 copy-done.3
  78.7 3.0 %collective-permute-start.17 = (bf16[2,256,32]{1,2,0:T(8,128)(2,1)S(1)}, bf16[2,256,32]{1,2,0:T(8,128)(2,1)S(1)}, u32[]{:S(2)}, u32[]{:S(2)}) collective-permute-start(bf16[2,256,32]{1,2,0:T(8,128)(2,1)S(1)} %convolution_convert_fusion.4), channel_id=1, source_target_pairs={{0,2},{1,3},{2,0},{3,1},{4,6},{5,7},{6,4},{7,5},{8,10},{9,11},{10,... | collective-permute-start | bytes 98312 | tf_op jit(solution)/shard_map/ppermute | solution.py:31
  81.7 1.4 collective-permute-start.18
  84.4 3.0 %collective-permute-done.18 = bf16[2,256,32]{1,2,0:T(8,128)(2,1)S(1)} collective-permute-done((bf16[2,256,32]{1,2,0:T(8,128)(2,1)S(1)}, bf16[2,256,32]{1,2,0:T(8,128)(2,1)S(1)}, u32[]{:S(2)}, u32[]{:S(2)}) %collective-permute-start.18) | collective-permute-done | bytes 32800 | tf_op jit(solution)/shard_map/ppermute | solution.py:31
  89.3 1.6 convolution_convert_fusion.2
  91.0 1.5 convolution_convert_fusion.1
  92.6 1.5 convolution_convert_fusion
  95.2 1.5 multiply_convert_fusion.2
  97.8 1.5 multiply_convert_fusion.1
  100.8 1.4 copy-done.4
  102.9 1.6 copy-done.5
  104.5 26.0 %forward_units.1 = (bf16[2,256,2048]{2,1,0:T(8,128)(2,1)}, bf16[2,256,2048]{2,1,0:T(8,128)(2,1)}, bf16[2,256,2048]{2,1,0:T(8,128)(2,1)}) custom-call(bf16[2,256,3072]{2,1,0:T(8,128)(2,1)} %copy-done.5, bf16[2,3072,2048]{2,1,0:T(8,128)(2,1)} %wg_ref.9, bf16[2,3072,2048]{2,1,0:T(8,128)(2,1)} %wu_ref.9, bf16[2,256,32]{2,1,0:T(8,128)(2,1)} %copy.113.low_ref, ...), custom_call_target="tpu_custom_call" | custom-call | flops 12884901888 | bytes 50331648 | tf_op jit(solution)/shard_map/forward_units/pallas_call | solution.py:56
  130.5 19.0 %hidden_back.1 = (bf16[2,256,2048]{2,1,0:T(8,128)(2,1)}, bf16[2,256,2048]{2,1,0:T(8,128)(2,1)}, f32[2,16,2048]{2,1,0:T(8,128)}, f32[2,16,2048]{2,1,0:T(8,128)}, ...) custom-call(bf16[2,256,3072]{2,1,0:T(8,128)(2,1)} %copy-done.2, bf16[2,2048,3072]{2,1,0:T(8,128)(2,1)} %wd_ref.1, ...), custom_call_target="tpu_custom_call" | custom-call | flops 6442450944 | bytes 25165824 | tf_op jit(solution)/shard_map/hidden_back/pallas_call | solution.py:114
  150.6 2.0 collective-permute-start.38
  152.5 2.4 collective-permute-start.39
  154.9 11.3 %row_back.4 = bf16[768,768]{1,0:T(8,128)(2,1)} custom-call(s32[1]{0:T(128)} %bitcast.place_ref, bf16[2,256,2048]{2,1,0:T(8,128)(2,1)} %get-tuple-element.19.gg_ref, bf16[2,256,2048]{2,1,0:T(8,128)(2,1)} %get-tuple-element.20.ug_ref, bf16[2,3072,2048]{2,1,0:T(8,128)(2,1)} %wg_ref.9, bf16[2,3072,2048]{2,1,0:T(8,128)(2,1)} %wu_ref.9, ...), custom_call_target="tpu_custom_call" | custom-call | flops 3221225472 | bytes 12582912 | tf_op jit(solution)/shard_map/row_back/pallas_call | solution.py:198
  166.3 1.1 slice.109
  167.4 11.4 %row_back.5 = bf16[768,768]{1,0:T(8,128)(2,1)} custom-call(s32[1]{0:T(128)} %bitcast.52.place_ref, bf16[2,256,2048]{2,1,0:T(8,128)(2,1)} %get-tuple-element.19.gg_ref, bf16[2,256,2048]{2,1,0:T(8,128)(2,1)} %get-tuple-element.20.ug_ref, bf16[2,3072,2048]{2,1,0:T(8,128)(2,1)} %wg_ref.9, bf16[2,3072,2048]{2,1,0:T(8,128)(2,1)} %wu_ref.9, ...), custom_call_target="tpu_custom_call" | custom-call | flops 3221225472 | bytes 12582912 | tf_op jit(solution)/shard_map/row_back/pallas_call | solution.py:198
  178.8 1.1 slice.113
  180.5 11.4 %row_back.6 = bf16[768,768]{1,0:T(8,128)(2,1)} custom-call(s32[1]{0:T(128)} %bitcast.53.place_ref, bf16[2,256,2048]{2,1,0:T(8,128)(2,1)} %get-tuple-element.19.gg_ref, bf16[2,256,2048]{2,1,0:T(8,128)(2,1)} %get-tuple-element.20.ug_ref, bf16[2,3072,2048]{2,1,0:T(8,128)(2,1)} %wg_ref.9, bf16[2,3072,2048]{2,1,0:T(8,128)(2,1)} %wu_ref.9, ...), custom_call_target="tpu_custom_call" | custom-call | flops 3221225472 | bytes 12582912 | tf_op jit(solution)/shard_map/row_back/pallas_call | solution.py:198
  191.9 1.1 slice.117
  193.9 12.1 %row_back.7 = bf16[768,768]{1,0:T(8,128)(2,1)} custom-call(s32[1]{0:T(128)} %bitcast.54.place_ref, bf16[2,256,2048]{2,1,0:T(8,128)(2,1)} %get-tuple-element.19.gg_ref, bf16[2,256,2048]{2,1,0:T(8,128)(2,1)} %get-tuple-element.20.ug_ref, bf16[2,3072,2048]{2,1,0:T(8,128)(2,1)} %wg_ref.9, bf16[2,3072,2048]{2,1,0:T(8,128)(2,1)} %wu_ref.9, ...), custom_call_target="tpu_custom_call" | custom-call | flops 3221225472 | bytes 12582912 | tf_op jit(solution)/shard_map/row_back/pallas_call | solution.py:198
  206.3 1.2 slice.122
  209.0 1.5 collective-permute-start.32
  211.5 1.5 collective-permute-start.41
  213.0 5.1 %collective-permute-done.29 = bf16[192,768]{1,0:T(8,128)(2,1)S(1)} collective-permute-done((bf16[192,768]{1,0:T(8,128)(2,1)S(1)}, bf16[192,768]{1,0:T(8,128)(2,1)S(1)}, u32[]{:S(2)}, u32[]{:S(2)}) %collective-permute-start.29) | collective-permute-done | bytes 294944 | tf_op jit(solution)/shard_map/ppermute | solution.py:31
  218.2 6.2 %collective-permute-done.32 = bf16[192,768]{1,0:T(8,128)(2,1)S(1)} collective-permute-done((bf16[192,768]{1,0:T(8,128)(2,1)S(1)}, bf16[192,768]{1,0:T(8,128)(2,1)S(1)}, u32[]{:S(2)}, u32[]{:S(2)}) %collective-permute-start.32) | collective-permute-done | bytes 294944 | tf_op jit(solution)/shard_map/ppermute | solution.py:31
  224.5 1.5 collective-permute-start.33
  226.0 4.8 %collective-permute-done.35 = bf16[192,768]{1,0:T(8,128)(2,1)S(1)} collective-permute-done((bf16[192,768]{1,0:T(8,128)(2,1)S(1)}, bf16[192,768]{1,0:T(8,128)(2,1)S(1)}, u32[]{:S(2)}, u32[]{:S(2)}) %collective-permute-start.35) | collective-permute-done | bytes 294944 | tf_op jit(solution)/shard_map/ppermute | solution.py:31
  232.5 3.6 %collective-permute-done.41 = bf16[192,768]{1,0:T(8,128)(2,1)S(1)} collective-permute-done((bf16[192,768]{1,0:T(8,128)(2,1)S(1)}, bf16[192,768]{1,0:T(8,128)(2,1)S(1)}, u32[]{:S(2)}, u32[]{:S(2)}) %collective-permute-start.41) | collective-permute-done | bytes 294944 | tf_op jit(solution)/shard_map/ppermute | solution.py:31
  236.1 1.7 collective-permute-done.30
  237.9 6.2 %collective-permute-done.36 = bf16[192,768]{1,0:T(8,128)(2,1)S(1)} collective-permute-done((bf16[192,768]{1,0:T(8,128)(2,1)S(1)}, bf16[192,768]{1,0:T(8,128)(2,1)S(1)}, u32[]{:S(2)}, u32[]{:S(2)}) %collective-permute-start.36) | collective-permute-done | bytes 294944 | tf_op jit(solution)/shard_map/ppermute | solution.py:31
  (223 shorter events, 31.4 us)
Async XLA Ops:
  0.6 70.2 %copy-start = (bf16[2,16,768]{2,1,0:T(8,128)(2,1)S(1)}, bf16[2,16,768]{2,1,0:T(8,128)(2,1)}, u32[]{:S(2)}) copy-start(bf16[2,16,768]{2,1,0:T(8,128)(2,1)} %param.26) | copy-start | bytes 147460
  0.6 25.0 %collective-permute-start.14 = (bf16[192,768]{1,0:T(8,128)(2,1)}, bf16[192,768]{1,0:T(8,128)(2,1)S(1)}, u32[]{:S(2)}, u32[]{:S(2)}) collective-permute-start(bf16[192,768]{1,0:T(8,128)(2,1)} %param.14), channel_id=1, source_target_pairs={{0,8},{4,12},{8,0},{12,4},{1,9},{5,13},{9,1},{13,5},{2,10},{6,14},... | collective-permute-start | bytes 884744 | tf_op jit(solution)/shard_map/ppermute | solution.py:31
  3.7 23.9 %collective-permute-start.19 = (bf16[192,768]{1,0:T(8,128)(2,1)}, bf16[192,768]{1,0:T(8,128)(2,1)S(1)}, u32[]{:S(2)}, u32[]{:S(2)}) collective-permute-start(bf16[192,768]{1,0:T(8,128)(2,1)} %param.14), channel_id=1, source_target_pairs={{0,1},{1,0},{2,3},{3,2},{4,5},{5,4},{6,7},{7,6},{8,9},{9,8},{10,11... | collective-permute-start | bytes 884744 | tf_op jit(solution)/shard_map/ppermute | solution.py:31
  5.2 23.9 %collective-permute-start.22 = (bf16[192,768]{1,0:T(8,128)(2,1)}, bf16[192,768]{1,0:T(8,128)(2,1)S(1)}, u32[]{:S(2)}, u32[]{:S(2)}) collective-permute-start(bf16[192,768]{1,0:T(8,128)(2,1)} %param.14), channel_id=1, source_target_pairs={{0,2},{1,3},{2,0},{3,1},{4,6},{5,7},{6,4},{7,5},{8,10},{9,11},{10,... | collective-permute-start | bytes 884744 | tf_op jit(solution)/shard_map/ppermute | solution.py:31
  7.8 24.0 %collective-permute-start.25 = (bf16[192,768]{1,0:T(8,128)(2,1)}, bf16[192,768]{1,0:T(8,128)(2,1)S(1)}, u32[]{:S(2)}, u32[]{:S(2)}) collective-permute-start(bf16[192,768]{1,0:T(8,128)(2,1)} %param.14), channel_id=1, source_target_pairs={{0,3},{1,2},{2,1},{3,0},{4,7},{5,6},{6,5},{7,4},{8,11},{9,10},{10,... | collective-permute-start | bytes 884744 | tf_op jit(solution)/shard_map/ppermute | solution.py:31
  8.0 24.4 %collective-permute-start = (bf16[192,768]{1,0:T(8,128)(2,1)}, bf16[192,768]{1,0:T(8,128)(2,1)S(1)}, u32[]{:S(2)}, u32[]{:S(2)}) collective-permute-start(bf16[192,768]{1,0:T(8,128)(2,1)} %param.15), channel_id=1, source_target_pairs={{0,8},{4,12},{8,0},{12,4},{1,9},{5,13},{9,1},{13,5},{2,10},{6,14},... | collective-permute-start | bytes 884744 | tf_op jit(solution)/shard_map/ppermute | solution.py:31
  25.6 13.2 %collective-permute-start.2 = (bf16[192,768]{1,0:T(8,128)(2,1)S(1)}, bf16[192,768]{1,0:T(8,128)(2,1)S(1)}, u32[]{:S(2)}, u32[]{:S(2)}) collective-permute-start(bf16[192,768]{1,0:T(8,128)(2,1)S(1)} %copy-done.17), channel_id=1, source_target_pairs={{0,1},{1,0},{2,3},{3,2},{4,5},{5,4},{6,7},{7,6},{8,9},{9,8},{10,11... | collective-permute-start | bytes 884744 | tf_op jit(solution)/shard_map/ppermute | solution.py:31
  27.5 13.8 %collective-permute-start.20 = (bf16[192,768]{1,0:T(8,128)(2,1)S(1)}, bf16[192,768]{1,0:T(8,128)(2,1)S(1)}, u32[]{:S(2)}, u32[]{:S(2)}) collective-permute-start(bf16[192,768]{1,0:T(8,128)(2,1)S(1)} %collective-permute-done.19), channel_id=1, source_target_pairs={{0,8},{4,12},{8,0},{12,4},{1,9},{5,13},{9,1},{13,5},{2,10},{6,14},... | collective-permute-start | bytes 884744 | tf_op jit(solution)/shard_map/ppermute | solution.py:31
  29.1 46.9 %copy-start.16 = (bf16[2,32,768]{2,1,0:T(8,128)(2,1)}, bf16[2,32,768]{2,1,0:T(8,128)(2,1)S(1)}, u32[]{:S(2)}) copy-start(bf16[2,32,768]{2,1,0:T(8,128)(2,1)S(1)} %constant_dynamic-update-slice_fusion.rest_1_) | copy-start | bytes 294916
  29.1 25.0 %copy-start.21 = (bf16[192,768]{1,0:T(8,128)(2,1)}, bf16[192,768]{1,0:T(8,128)(2,1)S(1)}, u32[]{:S(2)}) copy-start(bf16[192,768]{1,0:T(8,128)(2,1)S(1)} %collective-permute-done.22) | copy-start | bytes 884740
  29.2 24.4 %collective-permute-start.5 = (bf16[192,768]{1,0:T(8,128)(2,1)S(1)}, bf16[192,768]{1,0:T(8,128)(2,1)S(1)}, u32[]{:S(2)}, u32[]{:S(2)}) collective-permute-start(bf16[192,768]{1,0:T(8,128)(2,1)S(1)} %copy-done.17), channel_id=1, source_target_pairs={{0,2},{1,3},{2,0},{3,1},{4,6},{5,7},{6,4},{7,5},{8,10},{9,11},{10,... | collective-permute-start | bytes 884744 | tf_op jit(solution)/shard_map/ppermute | solution.py:31
  31.8 25.0 %copy-start.19 = (bf16[192,768]{1,0:T(8,128)(2,1)}, bf16[192,768]{1,0:T(8,128)(2,1)S(1)}, u32[]{:S(2)}) copy-start(bf16[192,768]{1,0:T(8,128)(2,1)S(1)} %collective-permute-done.25) | copy-start | bytes 884740
  31.8 21.8 %collective-permute-start.23 = (bf16[192,768]{1,0:T(8,128)(2,1)S(1)}, bf16[192,768]{1,0:T(8,128)(2,1)S(1)}, u32[]{:S(2)}, u32[]{:S(2)}) collective-permute-start(bf16[192,768]{1,0:T(8,128)(2,1)S(1)} %collective-permute-done.22), channel_id=1, source_target_pairs={{0,8},{4,12},{8,0},{12,4},{1,9},{5,13},{9,1},{13,5},{2,10},{6,14},... | collective-permute-start | bytes 884744 | tf_op jit(solution)/shard_map/ppermute | solution.py:31
  32.4 22.7 %collective-permute-start.8 = (bf16[192,768]{1,0:T(8,128)(2,1)S(1)}, bf16[192,768]{1,0:T(8,128)(2,1)S(1)}, u32[]{:S(2)}, u32[]{:S(2)}) collective-permute-start(bf16[192,768]{1,0:T(8,128)(2,1)S(1)} %copy-done.17), channel_id=1, source_target_pairs={{0,3},{1,2},{2,1},{3,0},{4,7},{5,6},{6,5},{7,4},{8,11},{9,10},{10,... | collective-permute-start | bytes 884744 | tf_op jit(solution)/shard_map/ppermute | solution.py:31
  38.8 19.0 %copy-start.24 = (bf16[192,768]{1,0:T(8,128)(2,1)}, bf16[192,768]{1,0:T(8,128)(2,1)S(1)}, u32[]{:S(2)}) copy-start(bf16[192,768]{1,0:T(8,128)(2,1)S(1)} %collective-permute-done.2) | copy-start | bytes 884740
  38.8 16.5 %collective-permute-start.26 = (bf16[192,768]{1,0:T(8,128)(2,1)S(1)}, bf16[192,768]{1,0:T(8,128)(2,1)S(1)}, u32[]{:S(2)}, u32[]{:S(2)}) collective-permute-start(bf16[192,768]{1,0:T(8,128)(2,1)S(1)} %collective-permute-done.25), channel_id=1, source_target_pairs={{0,8},{4,12},{8,0},{12,4},{1,9},{5,13},{9,1},{13,5},{2,10},{6,14},... | collective-permute-start | bytes 884744 | tf_op jit(solution)/shard_map/ppermute | solution.py:31
  41.4 16.3 %collective-permute-start.3 = (bf16[192,768]{1,0:T(8,128)(2,1)S(1)}, bf16[192,768]{1,0:T(8,128)(2,1)S(1)}, u32[]{:S(2)}, u32[]{:S(2)}) collective-permute-start(bf16[192,768]{1,0:T(8,128)(2,1)S(1)} %collective-permute-done.2), channel_id=1, source_target_pairs={{0,8},{4,12},{8,0},{12,4},{1,9},{5,13},{9,1},{13,5},{2,10},{6,14},... | collective-permute-start | bytes 884744 | tf_op jit(solution)/shard_map/ppermute | solution.py:31
  53.6 16.7 %collective-permute-start.1 = (bf16[2,192,768]{2,1,0:T(8,128)(2,1)S(1)}, bf16[2,192,768]{2,1,0:T(8,128)(2,1)S(1)}, u32[]{:S(2)}, u32[]{:S(2)}) collective-permute-start(bf16[2,192,768]{2,1,0:T(8,128)(2,1)S(1)} %pad_maximum_fusion), channel_id=1, source_target_pairs={{0,4},{4,0},{8,12},{12,8},{1,5},{5,1},{9,13},{13,9},{2,6},{6,2},{1... | collective-permute-start | bytes 1769480 | tf_op jit(solution)/shard_map/ppermute | solution.py:31
  53.6 9.9 %collective-permute-start.6 = (bf16[192,768]{1,0:T(8,128)(2,1)S(1)}, bf16[192,768]{1,0:T(8,128)(2,1)S(1)}, u32[]{:S(2)}, u32[]{:S(2)}) collective-permute-start(bf16[192,768]{1,0:T(8,128)(2,1)S(1)} %collective-permute-done.5), channel_id=1, source_target_pairs={{0,8},{4,12},{8,0},{12,4},{1,9},{5,13},{9,1},{13,5},{2,10},{6,14},... | collective-permute-start | bytes 884744 | tf_op jit(solution)/shard_map/ppermute | solution.py:31
  55.1 19.0 %collective-permute-start.15 = (bf16[2,192,768]{2,1,0:T(8,128)(2,1)S(1)}, bf16[2,192,768]{2,1,0:T(8,128)(2,1)S(1)}, u32[]{:S(2)}, u32[]{:S(2)}) collective-permute-start(bf16[2,192,768]{2,1,0:T(8,128)(2,1)S(1)} %pad_maximum_fusion.4), channel_id=1, source_target_pairs={{0,4},{4,0},{8,12},{12,8},{1,5},{5,1},{9,13},{13,9},{2,6},{6,2},{1... | collective-permute-start | bytes 1769480 | tf_op jit(solution)/shard_map/ppermute | solution.py:31
  55.3 14.0 %collective-permute-start.9 = (bf16[192,768]{1,0:T(8,128)(2,1)S(1)}, bf16[192,768]{1,0:T(8,128)(2,1)S(1)}, u32[]{:S(2)}, u32[]{:S(2)}) collective-permute-start(bf16[192,768]{1,0:T(8,128)(2,1)S(1)} %collective-permute-done.8), channel_id=1, source_target_pairs={{0,8},{4,12},{8,0},{12,4},{1,9},{5,13},{9,1},{13,5},{2,10},{6,14},... | collective-permute-start | bytes 884744 | tf_op jit(solution)/shard_map/ppermute | solution.py:31
  57.7 31.1 %collective-permute-start.21 = (bf16[2,192,768]{2,1,0:T(8,128)(2,1)}, bf16[2,192,768]{2,1,0:T(8,128)(2,1)}, u32[]{:S(2)}, u32[]{:S(2)}) collective-permute-start(bf16[2,192,768]{2,1,0:T(8,128)(2,1)} %pad_maximum_fusion.5), channel_id=1, source_target_pairs={{0,4},{4,0},{8,12},{12,8},{1,5},{5,1},{9,13},{13,9},{2,6},{6,2},{1... | collective-permute-start | bytes 1769480 | tf_op jit(solution)/shard_map/ppermute | solution.py:31
  63.5 27.5 %collective-permute-start.24 = (bf16[2,192,768]{2,1,0:T(8,128)(2,1)}, bf16[2,192,768]{2,1,0:T(8,128)(2,1)}, u32[]{:S(2)}, u32[]{:S(2)}) collective-permute-start(bf16[2,192,768]{2,1,0:T(8,128)(2,1)} %pad_maximum_fusion.6), channel_id=1, source_target_pairs={{0,4},{4,0},{8,12},{12,8},{1,5},{5,1},{9,13},{13,9},{2,6},{6,2},{1... | collective-permute-start | bytes 1769480 | tf_op jit(solution)/shard_map/ppermute | solution.py:31
  71.1 7.6 %collective-permute-start.11 = (bf16[2,256,16]{1,2,0:T(8,128)(2,1)S(1)}, bf16[2,256,16]{1,2,0:T(8,128)(2,1)S(1)}, u32[]{:S(2)}, u32[]{:S(2)}) collective-permute-start(bf16[2,256,16]{1,2,0:T(8,128)(2,1)S(1)} %convolution_convert_fusion.5), channel_id=1, source_target_pairs={{0,1},{1,0},{2,3},{3,2},{4,5},{5,4},{6,7},{7,6},{8,9},{9,8},{10,11... | collective-permute-start | bytes 49160 | tf_op jit(solution)/shard_map/ppermute | solution.py:31
  71.1 7.6 %collective-permute-start.12 = (bf16[2,256,16]{1,2,0:T(8,128)(2,1)S(1)}, bf16[2,256,16]{1,2,0:T(8,128)(2,1)S(1)}, u32[]{:S(2)}, u32[]{:S(2)}) collective-permute-start(bf16[2,256,16]{1,2,0:T(8,128)(2,1)S(1)} %convolution_convert_fusion.5), channel_id=1, source_target_pairs={{0,2},{1,3},{2,0},{3,1},{4,6},{5,7},{6,4},{7,5},{8,10},{9,11},{10,... | collective-permute-start | bytes 49160 | tf_op jit(solution)/shard_map/ppermute | solution.py:31
  74.1 7.6 %collective-permute-start.13 = (bf16[2,256,16]{1,2,0:T(8,128)(2,1)S(1)}, bf16[2,256,16]{1,2,0:T(8,128)(2,1)S(1)}, u32[]{:S(2)}, u32[]{:S(2)}) collective-permute-start(bf16[2,256,16]{1,2,0:T(8,128)(2,1)S(1)} %convolution_convert_fusion.5), channel_id=1, source_target_pairs={{0,3},{1,2},{2,1},{3,0},{4,7},{5,6},{6,5},{7,4},{8,11},{9,10},{10,... | collective-permute-start | bytes 49160 | tf_op jit(solution)/shard_map/ppermute | solution.py:31
  78.7 5.2 %collective-permute-start.16 = (bf16[2,256,32]{1,2,0:T(8,128)(2,1)S(1)}, bf16[2,256,32]{1,2,0:T(8,128)(2,1)S(1)}, u32[]{:S(2)}, u32[]{:S(2)}) collective-permute-start(bf16[2,256,32]{1,2,0:T(8,128)(2,1)S(1)} %convolution_convert_fusion.4), channel_id=1, source_target_pairs={{0,1},{1,0},{2,3},{3,2},{4,5},{5,4},{6,7},{7,6},{8,9},{9,8},{10,11... | collective-permute-start | bytes 98312 | tf_op jit(solution)/shard_map/ppermute | solution.py:31
  78.7 5.2 %collective-permute-start.17 = (bf16[2,256,32]{1,2,0:T(8,128)(2,1)S(1)}, bf16[2,256,32]{1,2,0:T(8,128)(2,1)S(1)}, u32[]{:S(2)}, u32[]{:S(2)}) collective-permute-start(bf16[2,256,32]{1,2,0:T(8,128)(2,1)S(1)} %convolution_convert_fusion.4), channel_id=1, source_target_pairs={{0,2},{1,3},{2,0},{3,1},{4,6},{5,7},{6,4},{7,5},{8,10},{9,11},{10,... | collective-permute-start | bytes 98312 | tf_op jit(solution)/shard_map/ppermute | solution.py:31
  81.7 5.7 %collective-permute-start.18 = (bf16[2,256,32]{1,2,0:T(8,128)(2,1)S(1)}, bf16[2,256,32]{1,2,0:T(8,128)(2,1)S(1)}, u32[]{:S(2)}, u32[]{:S(2)}) collective-permute-start(bf16[2,256,32]{1,2,0:T(8,128)(2,1)S(1)} %convolution_convert_fusion.4), channel_id=1, source_target_pairs={{0,3},{1,2},{2,1},{3,0},{4,7},{5,6},{6,5},{7,4},{8,11},{9,10},{10,... | collective-permute-start | bytes 98312 | tf_op jit(solution)/shard_map/ppermute | solution.py:31
  83.9 8.7 %collective-permute-start.27 = (bf16[2,192,768]{2,1,0:T(8,128)(2,1)}, bf16[2,192,768]{2,1,0:T(8,128)(2,1)}, u32[]{:S(2)}, u32[]{:S(2)}) collective-permute-start(bf16[2,192,768]{2,1,0:T(8,128)(2,1)} %pad_maximum_fusion.7), channel_id=1, source_target_pairs={{0,4},{4,0},{8,12},{12,8},{1,5},{5,1},{9,13},{13,9},{2,6},{6,2},{1... | collective-permute-start | bytes 1769480 | tf_op jit(solution)/shard_map/ppermute | solution.py:31
  83.9 10.4 %collective-permute-start.4 = (bf16[2,192,768]{2,1,0:T(8,128)(2,1)}, bf16[2,192,768]{2,1,0:T(8,128)(2,1)}, u32[]{:S(2)}, u32[]{:S(2)}) collective-permute-start(bf16[2,192,768]{2,1,0:T(8,128)(2,1)} %pad_maximum_fusion.1), channel_id=1, source_target_pairs={{0,4},{4,0},{8,12},{12,8},{1,5},{5,1},{9,13},{13,9},{2,6},{6,2},{1... | collective-permute-start | bytes 1769480 | tf_op jit(solution)/shard_map/ppermute | solution.py:31
  87.4 9.4 %collective-permute-start.7 = (bf16[2,192,768]{2,1,0:T(8,128)(2,1)}, bf16[2,192,768]{2,1,0:T(8,128)(2,1)}, u32[]{:S(2)}, u32[]{:S(2)}) collective-permute-start(bf16[2,192,768]{2,1,0:T(8,128)(2,1)} %pad_maximum_fusion.2), channel_id=1, source_target_pairs={{0,4},{4,0},{8,12},{12,8},{1,5},{5,1},{9,13},{13,9},{2,6},{6,2},{1... | collective-permute-start | bytes 1769480 | tf_op jit(solution)/shard_map/ppermute | solution.py:31
  88.8 10.6 %collective-permute-start.10 = (bf16[2,192,768]{2,1,0:T(8,128)(2,1)}, bf16[2,192,768]{2,1,0:T(8,128)(2,1)S(1)}, u32[]{:S(2)}, u32[]{:S(2)}) collective-permute-start(bf16[2,192,768]{2,1,0:T(8,128)(2,1)} %pad_maximum_fusion.3), channel_id=1, source_target_pairs={{0,4},{4,0},{8,12},{12,8},{1,5},{5,1},{9,13},{13,9},{2,6},{6,2},{1... | collective-permute-start | bytes 1769480 | tf_op jit(solution)/shard_map/ppermute | solution.py:31
  104.5 26.0 %copy-start.2 = (bf16[2,256,3072]{2,1,0:T(8,128)(2,1)}, bf16[2,256,3072]{2,1,0:T(8,128)(2,1)S(1)}, u32[]{:S(2)}) copy-start(bf16[2,256,3072]{2,1,0:T(8,128)(2,1)S(1)} %constant_dynamic-update-slice_fusion.5.g_ref) | copy-start | bytes 9437188
  150.5 42.5 %collective-permute-start.37 = (bf16[2,256,48]{2,1,0:T(8,128)(2,1)S(1)}, bf16[2,256,48]{2,1,0:T(8,128)(2,1)S(1)}, u32[]{:S(2)}, u32[]{:S(2)}) collective-permute-start(bf16[2,256,48]{2,1,0:T(8,128)(2,1)S(1)} %convert_element_type.197), channel_id=1, source_target_pairs={{0,1},{1,0},{2,3},{3,2},{4,5},{5,4},{6,7},{7,6},{8,9},{9,8},{10,11... | collective-permute-start | bytes 147464 | tf_op jit(solution)/shard_map/ppermute | solution.py:31
  150.6 42.6 %collective-permute-start.38 = (bf16[2,256,48]{2,1,0:T(8,128)(2,1)S(1)}, bf16[2,256,48]{2,1,0:T(8,128)(2,1)S(1)}, u32[]{:S(2)}, u32[]{:S(2)}) collective-permute-start(bf16[2,256,48]{2,1,0:T(8,128)(2,1)S(1)} %convert_element_type.197), channel_id=1, source_target_pairs={{0,2},{1,3},{2,0},{3,1},{4,6},{5,7},{6,4},{7,5},{8,10},{9,11},{10,... | collective-permute-start | bytes 147464 | tf_op jit(solution)/shard_map/ppermute | solution.py:31
  152.5 40.6 %collective-permute-start.39 = (bf16[2,256,48]{2,1,0:T(8,128)(2,1)S(1)}, bf16[2,256,48]{2,1,0:T(8,128)(2,1)S(1)}, u32[]{:S(2)}, u32[]{:S(2)}) collective-permute-start(bf16[2,256,48]{2,1,0:T(8,128)(2,1)S(1)} %convert_element_type.197), channel_id=1, source_target_pairs={{0,3},{1,2},{2,1},{3,0},{4,7},{5,6},{6,5},{7,4},{8,11},{9,10},{10,... | collective-permute-start | bytes 147464 | tf_op jit(solution)/shard_map/ppermute | solution.py:31
  167.4 40.6 %collective-permute-start.28 = (bf16[384,768]{1,0:T(8,128)(2,1)S(1)}, bf16[384,768]{1,0:T(8,128)(2,1)S(1)}, u32[]{:S(2)}, u32[]{:S(2)}) collective-permute-start(bf16[384,768]{1,0:T(8,128)(2,1)S(1)} %slice.109), channel_id=1, source_target_pairs={{0,4},{4,0},{8,12},{12,8},{1,5},{5,1},{9,13},{13,9},{2,6},{6,2},{1... | collective-permute-start | bytes 1769480 | tf_op jit(solution)/shard_map/ppermute | solution.py:31
  180.0 28.9 %collective-permute-start.31 = (bf16[384,768]{1,0:T(8,128)(2,1)S(1)}, bf16[384,768]{1,0:T(8,128)(2,1)S(1)}, u32[]{:S(2)}, u32[]{:S(2)}) collective-permute-start(bf16[384,768]{1,0:T(8,128)(2,1)S(1)} %slice.113), channel_id=1, source_target_pairs={{0,4},{4,0},{8,12},{12,8},{1,5},{5,1},{9,13},{13,9},{2,6},{6,2},{1... | collective-permute-start | bytes 1769480 | tf_op jit(solution)/shard_map/ppermute | solution.py:31
  193.0 17.5 %collective-permute-start.34 = (bf16[384,768]{1,0:T(8,128)(2,1)S(1)}, bf16[384,768]{1,0:T(8,128)(2,1)S(1)}, u32[]{:S(2)}, u32[]{:S(2)}) collective-permute-start(bf16[384,768]{1,0:T(8,128)(2,1)S(1)} %slice.117), channel_id=1, source_target_pairs={{0,4},{4,0},{8,12},{12,8},{1,5},{5,1},{9,13},{13,9},{2,6},{6,2},{1... | collective-permute-start | bytes 1769480 | tf_op jit(solution)/shard_map/ppermute | solution.py:31
  207.4 3.9 %collective-permute-start.40 = (bf16[384,768]{1,0:T(8,128)(2,1)S(1)}, bf16[384,768]{1,0:T(8,128)(2,1)S(1)}, u32[]{:S(2)}, u32[]{:S(2)}) collective-permute-start(bf16[384,768]{1,0:T(8,128)(2,1)S(1)} %slice.122), channel_id=1, source_target_pairs={{0,4},{4,0},{8,12},{12,8},{1,5},{5,1},{9,13},{13,9},{2,6},{6,2},{1... | collective-permute-start | bytes 1769480 | tf_op jit(solution)/shard_map/ppermute | solution.py:31
  208.2 9.9 %collective-permute-start.29 = (bf16[192,768]{1,0:T(8,128)(2,1)S(1)}, bf16[192,768]{1,0:T(8,128)(2,1)S(1)}, u32[]{:S(2)}, u32[]{:S(2)}) collective-permute-start(bf16[192,768]{1,0:T(8,128)(2,1)S(1)} %slice.157), channel_id=1, source_target_pairs={{0,8},{4,12},{8,0},{12,4},{1,9},{5,13},{9,1},{13,5},{2,10},{6,14},... | collective-permute-start | bytes 884744 | tf_op jit(solution)/shard_map/ppermute | solution.py:31
  209.0 15.4 %collective-permute-start.32 = (bf16[192,768]{1,0:T(8,128)(2,1)S(1)}, bf16[192,768]{1,0:T(8,128)(2,1)S(1)}, u32[]{:S(2)}, u32[]{:S(2)}) collective-permute-start(bf16[192,768]{1,0:T(8,128)(2,1)S(1)} %slice.156), channel_id=1, source_target_pairs={{0,8},{4,12},{8,0},{12,4},{1,9},{5,13},{9,1},{13,5},{2,10},{6,14},... | collective-permute-start | bytes 884744 | tf_op jit(solution)/shard_map/ppermute | solution.py:31
  210.7 20.1 %collective-permute-start.35 = (bf16[192,768]{1,0:T(8,128)(2,1)S(1)}, bf16[192,768]{1,0:T(8,128)(2,1)S(1)}, u32[]{:S(2)}, u32[]{:S(2)}) collective-permute-start(bf16[192,768]{1,0:T(8,128)(2,1)S(1)} %slice.155), channel_id=1, source_target_pairs={{0,8},{4,12},{8,0},{12,4},{1,9},{5,13},{9,1},{13,5},{2,10},{6,14},... | collective-permute-start | bytes 884744 | tf_op jit(solution)/shard_map/ppermute | solution.py:31
  211.5 24.6 %collective-permute-start.41 = (bf16[192,768]{1,0:T(8,128)(2,1)S(1)}, bf16[192,768]{1,0:T(8,128)(2,1)S(1)}, u32[]{:S(2)}, u32[]{:S(2)}) collective-permute-start(bf16[192,768]{1,0:T(8,128)(2,1)S(1)} %slice.154), channel_id=1, source_target_pairs={{0,8},{4,12},{8,0},{12,4},{1,9},{5,13},{9,1},{13,5},{2,10},{6,14},... | collective-permute-start | bytes 884744 | tf_op jit(solution)/shard_map/ppermute | solution.py:31
  218.2 19.7 %collective-permute-start.30 = (bf16[192,768]{1,0:T(8,128)(2,1)S(1)}, bf16[192,768]{1,0:T(8,128)(2,1)S(1)}, u32[]{:S(2)}, u32[]{:S(2)}) collective-permute-start(bf16[192,768]{1,0:T(8,128)(2,1)S(1)} %fusion.44), channel_id=1, source_target_pairs={{0,2},{1,3},{2,0},{3,1},{4,6},{5,7},{6,4},{7,5},{8,10},{9,11},{10,... | collective-permute-start | bytes 884744 | tf_op jit(solution)/shard_map/ppermute | solution.py:31
  224.5 13.4 %collective-permute-start.33 = (bf16[192,768]{1,0:T(8,128)(2,1)S(1)}, bf16[192,768]{1,0:T(8,128)(2,1)S(1)}, u32[]{:S(2)}, u32[]{:S(2)}) collective-permute-start(bf16[192,768]{1,0:T(8,128)(2,1)S(1)} %fusion.43), channel_id=1, source_target_pairs={{0,3},{1,2},{2,1},{3,0},{4,7},{5,6},{6,5},{7,4},{8,11},{9,10},{10,... | collective-permute-start | bytes 884744 | tf_op jit(solution)/shard_map/ppermute | solution.py:31
  230.8 13.3 %collective-permute-start.36 = (bf16[192,768]{1,0:T(8,128)(2,1)S(1)}, bf16[192,768]{1,0:T(8,128)(2,1)S(1)}, u32[]{:S(2)}, u32[]{:S(2)}) collective-permute-start(bf16[192,768]{1,0:T(8,128)(2,1)S(1)} %fusion.42), channel_id=1, source_target_pairs={{0,1},{1,0},{2,3},{3,2},{4,5},{5,4},{6,7},{7,6},{8,9},{9,8},{10,11... | collective-permute-start | bytes 884744 | tf_op jit(solution)/shard_map/ppermute | solution.py:31
  (38 other events, 185.3 us)

commit v2 on v1

v2 whole, which is shorter than its diff:
```python
import functools

import jax
import jax.numpy as jnp
from jax import lax
from jax.experimental import pallas as pl
from jax.experimental.pallas import tpu as pltpu
from jax.sharding import PartitionSpec as P

EXPERTS = 8
SLOT = 64

adapter_scale = 0.25

F32 = jnp.float32
BF16 = jnp.bfloat16
NN = (((1,), (0,)), ((), ()))
NT = (((1,), (1,)), ((), ()))


def mm(a, b, dims=NN):
    return lax.dot_general(a, b, dims, preferred_element_type=F32)


def params(semantics):
    return pltpu.CompilerParams(dimension_semantics=semantics, vmem_limit_bytes=56 * 1024 * 1024)


def swap(x, k, axis):
    n = lax.axis_size(axis)
    return lax.ppermute(x, axis, [(i, i ^ k) for i in range(n)])


def without(kernel, start, number):
    def run(*refs):
        kernel(*refs[:start], *refs[start + number :])

    return run


ANY = pl.BlockSpec(memory_space=pl.ANY)
COST = pl.CostEstimate(flops=1, bytes_accessed=1, transcendentals=0)


def tie(x, *others):
    return pl.pallas_call(
        lambda *refs: None,
        in_specs=[ANY] * (1 + len(others)),
        out_specs=ANY,
        out_shape=jax.ShapeDtypeStruct(x.shape, x.dtype),
        input_output_aliases={0: 0},
        cost_estimate=COST,
        name="tie",
    )(x, *others)


def place_kernel(scaled, far, at_ref, place_ref, *rest):
    if scaled:
        gate_ref, rest = rest[0], rest[1:]
    pieces, out_ref = rest[:-1], rest[-1]
    count = out_ref.shape[0]
    col = pieces[0].shape[2]
    groups = place_ref.shape[0]
    for i, k in enumerate(far):
        start = pl.multiple_of((at_ref[0] ^ k) * col, col)
        for r in range(groups):
            rows = mm(place_ref[r], pieces[i * groups + r][0])
            if scaled:
                rows = rows * gate_ref[r]
            rows = rows.astype(BF16).reshape(count, SLOT, col)
            out_ref[:, r * SLOT : (r + 1) * SLOT, pl.ds(start, col)] = rows


def place_rows(at, place, pieces, far, count, gate=None):
    groups, slots, tokens = place.shape
    n = groups * SLOT
    col = pieces[0][0].shape[2]
    whole = lambda *shape: pl.BlockSpec(shape, lambda i, p: (0,) * len(shape))
    gates = [] if gate is None else [gate]
    return pl.pallas_call(
        functools.partial(place_kernel, gate is not None, far),
        grid_spec=pltpu.PrefetchScalarGridSpec(
            num_scalar_prefetch=1,
            grid=(1,),
            in_specs=[whole(groups, slots, tokens)]
            + [whole(groups, slots, 1) for _ in gates]
            + [
                pl.BlockSpec((1, tokens, col), lambda i, p, index=index: (index, 0, 0))
                for _, index in pieces
            ],
            out_specs=whole(count, n, len(far) * col),
        ),
        out_shape=jax.ShapeDtypeStruct((count, n, len(far) * col), BF16),
        compiler_params=params(("arbitrary",)),
        cost_estimate=COST,
        name="place_rows",
    )(at, place, *gates, *[array for array, _ in pieces])


def forward_kernel(x_ref, wg_ref, wu_ref, in_ref, go_ref, uo_ref, a_ref, b_ref, h_ref, low_ref):
    x = x_ref[0]
    rank = go_ref.shape[1]

    @pl.when(pl.program_id(1) == 0)
    def _():
        low_ref[0] = mm(x, in_ref[0], NT).astype(BF16)

    low = low_ref[0]
    gate = mm(x, wg_ref[0]) + adapter_scale * mm(low[:, :rank], go_ref[0])
    up = mm(x, wu_ref[0]) + adapter_scale * mm(low[:, rank:], uo_ref[0])
    q = jax.nn.sigmoid(gate)
    silu = gate * q
    a_ref[0] = (up * (q + silu * (1.0 - q))).astype(BF16)
    b_ref[0] = silu.astype(BF16)
    h_ref[0] = (silu * up).astype(BF16)


def forward(first, number, rows, wg, wu, factor_in, go, uo, held=()):
    count, n, width = rows.shape
    units = wg.shape[2]
    rank = go.shape[1]
    ft = min(512, units)
    out = jax.ShapeDtypeStruct((count, n, units), BF16)
    wide = pl.BlockSpec((1, n, ft), lambda l, f: (l + first, 0, f))
    weight = pl.BlockSpec((1, width, ft), lambda l, f: (l + first, 0, f))
    factor = pl.BlockSpec((1, rank, ft), lambda l, f: (l + first, 0, f))
    one = lambda *shape: pl.BlockSpec((1,) + shape, lambda l, f: (l + first, 0, 0))
    return pl.pallas_call(
        without(forward_kernel, 6, len(held)),
        grid=(number, units // ft),
        in_specs=[one(n, width), weight, weight, one(2 * rank, width), factor, factor]
        + [ANY for _ in held],
        out_specs=[wide, wide, wide, one(n, 2 * rank)],
        out_shape=[out, out, out, jax.ShapeDtypeStruct((count, n, 2 * rank), BF16)],
        input_output_aliases={6 + i: i for i in range(len(held))},
        compiler_params=params(("arbitrary", "arbitrary")),
        cost_estimate=COST,
        name="forward_units",
    )(rows, wg, wu, factor_in, go, uo, *held)


def hidden_kernel(
    g_ref, wd_ref, out_ref, di_ref, go_ref, uo_ref, a_ref, b_ref, h_ref,
    gg_ref, ug_ref, proj_ref, low_ref, sum_ref,
):
    g = g_ref[0]
    first = pl.program_id(1) == 0

    @pl.when(first)
    def _():
        low_ref[0] = mm(g, out_ref[0], NT).astype(BF16)

    hg = mm(g, wd_ref[0], NT) + adapter_scale * mm(low_ref[0], di_ref[0])
    gg = (hg * a_ref[0].astype(F32)).astype(BF16)
    ug = (hg * b_ref[0].astype(F32)).astype(BF16)
    gg_ref[0] = gg
    ug_ref[0] = ug
    proj = jnp.concatenate(
        [mm(gg, go_ref[0], NT), mm(ug, uo_ref[0], NT), mm(h_ref[0], di_ref[0], NT)], axis=1
    )
    total = jnp.where(first, 0.0, sum_ref[...]) + proj
    sum_ref[...] = total
    proj_ref[0] = total.astype(BF16)


def hidden_back(rows, wd, factor_out, di, go, uo, a, b, h):
    count, n, width = rows.shape
    units = wd.shape[1]
    rank = di.shape[1]
    ft = min(1024, units)
    wide = pl.BlockSpec((1, n, ft), lambda l, f: (l, 0, f))
    factor = pl.BlockSpec((1, rank, ft), lambda l, f: (l, 0, f))
    one = lambda *shape: pl.BlockSpec((1,) + shape, lambda l, f: (l, 0, 0))
    out = jax.ShapeDtypeStruct((count, n, units), BF16)
    return pl.pallas_call(
        hidden_kernel,
        grid=(count, units // ft),
        in_specs=[
            one(n, width),
            pl.BlockSpec((1, ft, width), lambda l, f: (l, f, 0)),
            one(rank, width),
            factor,
            factor,
            factor,
            wide,
            wide,
            wide,
        ],
        out_specs=[wide, wide, one(n, 3 * rank), one(n, rank)],
        out_shape=[
            out,
            out,
            jax.ShapeDtypeStruct((count, n, 3 * rank), BF16),
            jax.ShapeDtypeStruct((count, n, rank), BF16),
        ],
        scratch_shapes=[pltpu.VMEM((n, 3 * rank), F32)],
        compiler_params=params(("arbitrary", "arbitrary")),
        cost_estimate=COST,
        name="hidden_back",
    )(rows, wd, factor_out, di, go, uo, a, b, h)


def adapter_kernel(lowt_ref, gg_ref, ug_ref, h_ref, ggo_ref, guo_ref, gdi_ref):
    rank = ggo_ref.shape[1]
    lowt = lowt_ref[0]
    ggo_ref[0] = adapter_scale * mm(lowt[:rank], gg_ref[0])
    guo_ref[0] = adapter_scale * mm(lowt[rank : 2 * rank], ug_ref[0])
    gdi_ref[0] = adapter_scale * mm(lowt[2 * rank :], h_ref[0])


def adapter_back(lowt, gg, ug, h, wait=()):
    count, n, units = gg.shape
    rank = lowt.shape[1] // 3
    one = lambda *shape: pl.BlockSpec((1,) + shape, lambda l: (l, 0, 0))
    return pl.pallas_call(
        without(adapter_kernel, 4, len(wait)),
        grid=(count,),
        in_specs=[one(3 * rank, n)] + [one(n, units)] * 3 + [ANY for _ in wait],
        out_specs=[one(rank, units)] * 3,
        out_shape=[jax.ShapeDtypeStruct((count, rank, units), F32)] * 3,
        compiler_params=params(("arbitrary",)),
        cost_estimate=COST,
        name="adapter_back",
    )(lowt, gg, ug, h, *wait)


def rows_kernel(at_ref, gg_ref, ug_ref, wg_ref, wu_ref, back_ref, proj_ref, in_ref, *rest):
    *out_refs, y_ref = rest
    d = pl.program_id(0)
    l = pl.program_id(1)
    tiles = len(out_refs) // 2
    count = pl.num_programs(1)
    rank2 = in_ref.shape[1]
    y = mm(gg_ref[l], wg_ref[0], NT) + mm(ug_ref[l], wu_ref[0], NT)
    y = y + adapter_scale * mm(proj_ref[l][:, :rank2], in_ref[0])
    groups, tokens, _ = back_ref.shape
    y_ref[l] = y.astype(BF16).reshape(groups, SLOT, -1)

    def finish(keep_ref, send_ref):
        for g in range(groups):
            held = y_ref[:, g].reshape(-1, y_ref.shape[3])
            out_ref, at = (keep_ref, g) if g < groups // 2 else (send_ref, g - groups // 2)
            out_ref[at * tokens : (at + 1) * tokens] = mm(back_ref[g], held).astype(BF16)

    for i in range(tiles):
        pl.when((l == count - 1) & (d == i))(
            functools.partial(finish, out_refs[2 * i], out_refs[2 * i + 1])
        )


def row_back(at, gg, ug, wg, wu, back, proj, factor_in, dt, wait=()):
    count, n, units = gg.shape
    groups, tokens, _ = back.shape
    tiles = at.shape[0]
    whole = lambda *shape: pl.BlockSpec(shape, lambda d, l, p: (0,) * len(shape))
    weight = pl.BlockSpec((1, dt, units), lambda d, l, p: (l, p[d], 0))
    half = groups // 2 * tokens
    return pl.pallas_call(
        without(rows_kernel, 8, len(wait)),
        grid_spec=pltpu.PrefetchScalarGridSpec(
            num_scalar_prefetch=1,
            grid=(tiles, count),
            in_specs=[
                whole(*gg.shape),
                whole(*gg.shape),
                weight,
                weight,
                whole(*back.shape),
                whole(*proj.shape),
                pl.BlockSpec((1, factor_in.shape[1], dt), lambda d, l, p: (l, 0, p[d])),
            ]
            + [ANY for _ in wait],
            out_specs=[whole(half, dt)] * (2 * tiles),
            scratch_shapes=[pltpu.VMEM((count, groups, SLOT, dt), BF16)],
        ),
        out_shape=[jax.ShapeDtypeStruct((half, dt), BF16)] * (2 * tiles),
        compiler_params=params(("arbitrary", "arbitrary")),
        cost_estimate=COST,
        name="row_back",
    )(at, gg, ug, wg, wu, back, proj, factor_in, *wait)


def slots_of(experts):
    tokens = experts.shape[0]
    flat = experts.reshape(2 * tokens)
    onehot = (flat[:, None] == jnp.arange(EXPERTS, dtype=jnp.int32)).astype(BF16)
    pairs = jnp.arange(2 * tokens, dtype=jnp.int32)
    before = (pairs[:, None] > pairs[None, :]).astype(BF16)
    earlier = jnp.sum(mm(before, onehot) * onehot.astype(F32), axis=1)
    return (flat.astype(F32) * SLOT + earlier).reshape(tokens, 2)


def written(experts, routes, gates, col):
    tokens = experts.shape[0]
    number = experts.astype(F32)
    terms = [number, routes[:, :2] - number * SLOT]
    left = gates
    for _ in range(3):
        term = lax.reduce_precision(left, 8, 7)
        terms.append(term)
        left = left - term
    flat = jnp.concatenate(terms, axis=1).reshape(-1)
    rows = -(-flat.shape[0] // (16 * col)) * 16
    return jnp.pad(flat, (0, rows * col - flat.shape[0])).astype(BF16).reshape(rows, col)


def read(rows, tokens):
    terms = rows.reshape(-1)[: 10 * tokens].astype(F32).reshape(tokens, 10)
    gates = terms[:, 4:6] + terms[:, 6:8] + terms[:, 8:10]
    return jnp.concatenate([terms[:, :2] * SLOT + terms[:, 2:4], gates], axis=1)[None]


def routing(routes, me, count):
    slots = me * (count * SLOT) + jnp.arange(count * SLOT, dtype=jnp.int32)
    slots = slots.astype(F32)[None, :, None]
    first = routes[:, None, :, 0] == slots
    second = routes[:, None, :, 1] == slots
    gate = jnp.where(first, routes[:, None, :, 2], 0.0) + jnp.where(
        second, routes[:, None, :, 3], 0.0
    )
    place = (first | second).astype(BF16)
    slots = jnp.swapaxes(slots, 1, 2)
    back = ((routes[:, :, :1] == slots) | (routes[:, :, 1:2] == slots)).astype(BF16)
    return place, back, jnp.sum(gate, axis=2, keepdims=True)


def body(
    inputs,
    out_grad,
    experts,
    route_gates,
    gate_proj,
    up_proj,
    down_proj,
    gate_in,
    gate_out,
    up_in,
    up_out,
    down_in,
    down_out,
):
    groups = lax.axis_size("expert")
    cuts = lax.axis_size("cuts")
    me = lax.axis_index("expert")
    cut = lax.axis_index("cuts")
    count = gate_proj.shape[0]
    tokens, col = inputs.shape
    width = gate_proj.shape[1]
    rank = gate_in.shape[1]
    n = groups * SLOT
    paired = groups == 4 and cuts == 4 and count > 1
    factors = jnp.concatenate([gate_in, up_in, down_out], axis=1)
    routes = jnp.concatenate([slots_of(experts), route_gates], axis=1)

    def other_chip(x):
        return swap(x, 2, "expert")

    def other_core(x):
        return swap(x, 1, "expert")

    if paired:
        at = jnp.reshape(cut, (1,)).astype(jnp.int32)

        def over_cuts(x, k):
            return swap(x, k, "cuts")

        own = jnp.concatenate([inputs, written(experts, routes, route_gates, col)])[None]
        x2 = over_cuts(inputs[None], 2)
        own_over = other_chip(own)
        own_cross, own_both = other_core(own), other_core(own_over)
        first = [own, own_over, own_cross, own_both]
        routes = jnp.concatenate([read(x[0, tokens:], tokens) for x in first])
        place, back, gate = routing(routes, me, count)
        x13 = over_cuts(jnp.concatenate([inputs[None], x2]), 1)
        g2 = over_cuts(tie(out_grad, x2)[None], 2)
        x2_over = other_chip(x2)
        x2_cross = other_core(x2)
        x13 = tie(x13, g2, x2_over)
        g02 = jnp.concatenate([out_grad[None], g2])
        g13 = over_cuts(g02, 1)
        far_factors = over_cuts(tie(factors, x13)[None], 2)
        x13_over, x13_cross = other_chip(x13), other_core(x13)
        x13_over = tie(x13_over, g13, far_factors, x13_cross)
        x2_both, x13_both = other_core(x2_over), other_core(x13_over)
        f02 = jnp.concatenate([factors[None], far_factors])
        f13 = over_cuts(f02, 1)
        all_factors = jnp.concatenate([f02, f13])
        near = jnp.array([0, 2, 1, 3], jnp.int32)
        all_factors = jnp.take(all_factors, near[cut ^ jnp.arange(cuts)], axis=0)
        all_factors = jnp.moveaxis(all_factors, 0, 2).reshape(count, 3 * rank, width)
        at = jnp.reshape(cut, (1,)).astype(jnp.int32)
        pieces = [(x, 0) for x in first]
        pieces += [(x, 0) for x in (x2, x2_over, x2_cross, x2_both)]
        pieces += [(x, 0) for x in (x13, x13_over, x13_cross, x13_both)]
        pieces += [(x, 1) for x in (x13, x13_over, x13_cross, x13_both)]
        rows_x = place_rows(at, place, pieces, (0, 2, 1, 3), count)
    else:
        place, back, gate = routing(lax.all_gather(routes, "expert"), me, count)
        all_factors = lax.all_gather(factors, "cuts", axis=2, tiled=True)

        def collect(x, gate=None):
            x = lax.all_gather(x, "expert")
            rows = jnp.einsum("gst,gtd->gsd", place, x, preferred_element_type=F32)
            if gate is not None:
                rows = rows * gate
            rows = rows.astype(BF16).reshape(groups, count, SLOT, col)
            own = jnp.swapaxes(rows, 0, 1).reshape(count, n, col)
            return lax.all_gather(own, "cuts", axis=2, tiled=True)

        rows_x = collect(inputs)

    factors_in = all_factors[:, : 2 * rank]
    a, b, h, low_x = forward(
        0, count, rows_x, gate_proj, up_proj, factors_in, gate_out, up_out
    )
    if paired:
        pieces = []
        for x in (g02, g13):
            over, cross = other_chip(x), other_core(x)
            over = tie(over, h, cross)
            both = other_core(over)
            pieces += [(y, i) for i in range(2) for y in (x, over, cross, both)]
        rows_g = place_rows(at, place, pieces, (0, 2, 1, 3), count, gate)
    else:
        rows_g = collect(out_grad, gate)
    gg, ug, proj, low_g = hidden_back(
        rows_g, down_proj, all_factors[:, 2 * rank :], down_in, gate_out, up_out, a, b, h
    )
    lowt = jnp.swapaxes(jnp.concatenate([low_x, low_g], axis=2), 1, 2)

    if paired:
        def chunks(first, second, wait=()):
            return row_back(
                jnp.stack([cut ^ first, cut ^ second]).astype(jnp.int32),
                gg, ug, gate_proj, up_proj, back, proj, factors_in, col, wait,
            )

        def to_chip(keep, send):
            total = keep.astype(F32) + other_core(send).astype(F32)
            return total[:tokens], total[tokens:].astype(BF16)

        keep3, send3, keep1, send1 = chunks(3, 1)
        half3, send3 = to_chip(keep3, send3)
        half1, send1 = to_chip(keep1, send1)
        keep2, send2, keep0, send0 = chunks(2, 0, [send3, send1])
        over3 = tie(other_chip(send3), keep2)
        over1 = tie(other_chip(send1), keep2)
        half2, send2 = to_chip(keep2, tie(send2, over3, over1))
        half0, send0 = to_chip(keep0, send0)
        rows = proj.reshape(-1, col)
        near = swap(
            jnp.concatenate(
                [(half1 + over1.astype(F32)).astype(BF16), (half3 + over3.astype(F32)).astype(BF16), rows]
            ),
            1,
            "cuts",
        )
        grads = adapter_back(lowt, gg, ug, h, [send2, send0])
        over2 = tie(other_chip(send2), near, grads[0])
        over0 = other_chip(send0)
        near = near.astype(F32)
        rows = rows.astype(F32) + near[2 * tokens :]
        sum2 = half2 + over2.astype(F32) + near[tokens : 2 * tokens]
        far = swap(jnp.concatenate([sum2.astype(BF16), rows.astype(BF16)]), 2, "cuts").astype(F32)
        input_grad = (half0 + over0.astype(F32) + near[:tokens] + far[:tokens]).astype(BF16)
        proj = (rows + far[tokens:]).astype(BF16).reshape(proj.shape)
    else:
        grads = adapter_back(lowt, gg, ug, h)
        dt = 768 if width % 768 == 0 else width
        at = jnp.arange(width // dt, dtype=jnp.int32)
        chunks = row_back(at, gg, ug, gate_proj, up_proj, back, proj, factors_in, dt)
        partial = jnp.concatenate(
            [jnp.concatenate(chunks[i : i + 2]) for i in range(0, len(chunks), 2)], axis=1
        )
        partial = lax.psum_scatter(partial, "expert", scatter_dimension=0, tiled=True)
        input_grad = lax.psum_scatter(partial, "cuts", scatter_dimension=1, tiled=True)
        proj = lax.psum(proj.astype(F32), "cuts").astype(BF16)

    own_x = lax.dynamic_slice(rows_x, (0, 0, cut * col), (count, n, col))
    own_g = lax.dynamic_slice(rows_g, (0, 0, cut * col), (count, n, col))
    grad_x = adapter_scale * jnp.einsum(
        "lnr,lnd->lrd", proj[:, :, : 2 * rank], own_x, preferred_element_type=F32
    )
    grad_down_out = adapter_scale * jnp.einsum(
        "lnr,lnd->lrd", proj[:, :, 2 * rank :], own_g, preferred_element_type=F32
    )
    return (
        input_grad,
        grad_x[:, :rank],
        grads[0],
        grad_x[:, rank:],
        grads[1],
        grads[2],
        grad_down_out,
    )


def solution(mesh):
    return jax.shard_map(
        body,
        mesh=mesh,
        in_specs=(
            P(("parts", "expert"), "cuts"),
            P(("parts", "expert"), "cuts"),
            P(("parts", "expert"), None),
            P(("parts", "expert"), None),
            P("expert", None, "cuts"),
            P("expert", None, "cuts"),
            P("expert", "cuts", None),
            P("expert", None, "cuts"),
            P("expert", None, "cuts"),
            P("expert", None, "cuts"),
            P("expert", None, "cuts"),
            P("expert", None, "cuts"),
            P("expert", None, "cuts"),
        ),
        out_specs=(
            P(("parts", "expert"), "cuts"),
            P(("parts", "expert"), None, "cuts"),
            P(("parts", "expert"), None, "cuts"),
            P(("parts", "expert"), None, "cuts"),
            P(("parts", "expert"), None, "cuts"),
            P(("parts", "expert"), None, "cuts"),
            P(("parts", "expert"), None, "cuts"),
        ),
        check_vma=False,
    )
```

time: 246 us -> 231 us (0.939)
  starting transfers between devices: 40.9 us -> 23.3 us
  local copies, waits for them, and re-layouts: 18.2 us -> 27.5 us
  blocking collectives: 8.45 us -> 0 us
  matrix products: 10.8 us -> 3.81 us
  waiting for transfers between devices: 57.8 us -> 62.9 us
  other arithmetic: 16 us -> 19.8 us
    ppermute x42 -> x31, starting transfers between devices: 40.9 us -> 23.3 us  [swap(): return lax.ppermute(x, axis, [(i, i ^ k) for i in range(n)])]
    all_gather x1 -> x0, blocking collectives: 8.45 us -> none  [body(): lax.all_gather(jnp.concatenate([experts.astype(F32), route_gates], axis=1...]
    unnamed x89 -> x99, local copies, waits for them, and re-layouts: 7.34 us -> 15 us
    dot_general x12 -> x3, matrix products: 10.8 us -> 3.81 us  [the longest x1 2.11 us: body(): jnp.einsum('lnr,lnd->lrd', proj[:, :, 2 * rank:], own_g, preferred_elemen...]
    another operation x10 -> x4, other arithmetic: 8.94 us -> 2.62 us  [the longest x8 5.53 us: spread(): mine = jnp.stack([x, swap(x, 2, 'expert')])]
    ppermute x42 -> x31, waiting for transfers between devices: 57.8 us -> 62.9 us  [swap(): return lax.ppermute(x, axis, [(i, i ^ k) for i in range(n)])]
    concatenate x0 -> x7, other arithmetic: none -> 3.05 us  [the longest x1 1.13 us: body(): all_factors = jnp.concatenate([f02, f13])]
    add x6 -> x8, other arithmetic: 0.59 us -> 3.35 us  [the longest x4 2.66 us: to_chip(): total = keep.astype(F32) + other_core(send).astype(F32)]
  transfers between devices with their start and end apart: 42 -> 31, of which waited for: 11 -> 9; matrix products, arithmetic and copies ran while one was open for 14% -> 15% of each run, Pallas kernels for 19% -> 23%
where the time goes in v2:
time: 231 us; the launch traced here: 230 us
  Pallas kernels  91.8 us (40%)
  waiting for transfers between devices  62.9 us (27%)
  local copies, waits for them, and re-layouts  27.5 us (12%)
  starting transfers between devices  23.3 us (10%)
  other arithmetic  19.8 us (9%)
  matrix products  3.81 us (2%)
    ppermute x31, waiting for transfers between devices, swap(): return lax.ppermute(x, axis, [(i, i ^ k) for i in range(n)])  62.9 us
    pallas_call x2, Pallas kernels, row_back(): pl.pallas_call(without(rows_kernel, 8, len(wait)), grid_spec=pltpu.Prefet...  33.5 us
    pallas_call x1, Pallas kernels, forward(): pl.pallas_call(without(forward_kernel, 6, len(held)), grid=(number, units...  26.3 us
    ppermute x31, starting transfers between devices, swap(): return lax.ppermute(x, axis, [(i, i ^ k) for i in range(n)])  23.3 us
    pallas_call x1, Pallas kernels, hidden_back(): pl.pallas_call(hidden_kernel, grid=(count, units // ft), in_specs=[one(n,...  17.8 us
    unnamed x99, local copies, waits for them, and re-layouts  15 us
    pallas_call x2, Pallas kernels, place_rows(): pl.pallas_call(functools.partial(place_kernel, gate is not None, far), gr...  10.1 us
  transfers between devices with their start and end apart: 31, of which 9 were waited for; matrix products, arithmetic and copies ran while one was open for 15% of the time, Pallas kernels for 23%

profile of v2, /device:TPU:0, one launch (start us, length us, event | category | flops | bytes accessed | tf_op | source)
XLA Modules:
  0.0 230.5 jit_solution(2387527227658453374)
XLA Ops:
  3.9 1.0 maximum_bitcast_fusion.rest_0_
  4.9 3.0 %collective-permute-start = (bf16[1,208,768]{2,1,0:T(8,128)(2,1)S(1)}, bf16[1,208,768]{2,1,0:T(8,128)(2,1)S(1)}, u32[]{:S(2)}, u32[]{:S(2)}) collective-permute-start(bf16[1,208,768]{2,1,0:T(8,128)(2,1)S(1)} %maximum_bitcast_fusion.rest_0_), channel_id=1, source_target_pairs={{0,8},{4,12},{8,0},{12,4},{1,9},{5,13},{9,1},{13,5},{2,10},{6,14},... | collective-permute-start | bytes 958472 | tf_op jit(solution)/shard_map/ppermute | solution.py:31
  8.0 2.6 %collective-permute-start.3 = (bf16[1,192,768]{2,1,0:T(8,128)(2,1)S(1)}, bf16[1,192,768]{2,1,0:T(8,128)(2,1)S(1)}, u32[]{:S(2)}, u32[]{:S(2)}) collective-permute-start(bf16[1,192,768]{2,1,0:T(8,128)(2,1)S(1)} %bitcast.49), channel_id=1, source_target_pairs={{0,2},{1,3},{2,0},{3,1},{4,6},{5,7},{6,4},{7,5},{8,10},{9,11},{10,... | collective-permute-start | bytes 884744 | tf_op jit(solution)/shard_map/ppermute | solution.py:31
  15.1 9.5 %collective-permute-done.3.refs_1_.rest_4_ = bf16[1,192,768]{2,1,0:T(8,128)(2,1)S(1)} collective-permute-done((bf16[1,192,768]{2,1,0:T(8,128)(2,1)S(1)}, bf16[1,192,768]{2,1,0:T(8,128)(2,1)S(1)}, u32[]{:S(2)}, u32[]{:S(2)}) %collective-permute-start.3) | collective-permute-done | bytes 294944 | tf_op jit(solution)/shard_map/ppermute | solution.py:31
  25.3 1.0 pad_maximum_fusion.2
  26.4 4.1 %collective-permute-start.9 = (bf16[2,192,768]{2,1,0:T(8,128)(2,1)S(1)}, bf16[2,192,768]{2,1,0:T(8,128)(2,1)S(1)}, u32[]{:S(2)}, u32[]{:S(2)}) collective-permute-start(bf16[2,192,768]{2,1,0:T(8,128)(2,1)S(1)} %pad_maximum_fusion.2), channel_id=1, source_target_pairs={{0,1},{1,0},{2,3},{3,2},{4,5},{5,4},{6,7},{7,6},{8,9},{9,8},{10,11... | collective-permute-start | bytes 1769480 | tf_op jit(solution)/shard_map/ppermute | solution.py:31
  33.6 7.9 %collective-permute-done.4.refs_1_ = bf16[1,192,768]{2,1,0:T(8,128)(2,1)S(1)} collective-permute-done((bf16[1,192,768]{2,1,0:T(8,128)(2,1)}, bf16[1,192,768]{2,1,0:T(8,128)(2,1)S(1)}, u32[]{:S(2)}, u32[]{:S(2)}) %collective-permute-start.4) | collective-permute-done | bytes 294944 | tf_op jit(solution)/shard_map/ppermute | solution.py:31
  41.7 0.9 copy-done.36
  44.3 5.3 %collective-permute-done.9.refs_0_ = bf16[2,192,768]{2,1,0:T(8,128)(2,1)S(1)} collective-permute-done((bf16[2,192,768]{2,1,0:T(8,128)(2,1)S(1)}, bf16[2,192,768]{2,1,0:T(8,128)(2,1)S(1)}, u32[]{:S(2)}, u32[]{:S(2)}) %collective-permute-start.9) | collective-permute-done | bytes 589856 | tf_op jit(solution)/shard_map/ppermute | solution.py:31
  49.7 0.8 copy-done.1
  52.5 1.0 copy.96
  53.5 7.1 %collective-permute-done.12.refs_2_ = bf16[1,2,48,768]{3,2,1,0:T(8,128)(2,1)S(1)} collective-permute-done((bf16[1,2,48,768]{3,2,1,0:T(8,128)(2,1)}, bf16[1,2,48,768]{3,2,1,0:T(8,128)(2,1)S(1)}, u32[]{:S(2)}, u32[]{:S(2)}) %collective-permute-start.12) | collective-permute-done | bytes 147488 | tf_op jit(solution)/shard_map/ppermute | solution.py:31
  61.4 3.2 %collective-permute-done.11.refs_1_.rest_9_.rest_13_ = bf16[2,192,768]{2,1,0:T(8,128)(2,1)S(1)} collective-permute-done((bf16[2,192,768]{2,1,0:T(8,128)(2,1)S(1)}, bf16[2,192,768]{2,1,0:T(8,128)(2,1)S(1)}, u32[]{:S(2)}, u32[]{:S(2)}) %collective-permute-start.11) | collective-permute-done | bytes 589856 | tf_op jit(solution)/shard_map/ppermute | solution.py:31
  64.6 1.5 collective-permute-start.15
  67.6 1.5 collective-permute-start.18
  69.1 5.0 %collective-permute-done.15 = bf16[2,2,48,768]{3,2,1,0:T(8,128)(2,1)} collective-permute-done((bf16[2,2,48,768]{3,2,1,0:T(8,128)(2,1)}, bf16[2,2,48,768]{3,2,1,0:T(8,128)(2,1)}, u32[]{:S(2)}, u32[]{:S(2)}) %collective-permute-start.15) | collective-permute-done | bytes 294944 | tf_op jit(solution)/shard_map/ppermute | solution.py:31
  74.1 1.5 fusion.9.place_ref
  75.6 1.1 pad_maximum_fusion.3
  76.7 1.5 gather_fusion.1
  78.2 1.2 select_bitcast_fusion
  80.3 5.0 %place_rows.2.refs_0_ = bf16[2,256,3072]{2,1,0:T(8,128)(2,1)} custom-call(s32[1]{0:T(128)} %bitcast.1.at_ref, bf16[4,128,192]{2,1,0:T(8,128)(2,1)} %fusion.9.place_ref, bf16[1,208,768]{2,1,0:T(8,128)(2,1)} %copy-done.22, bf16[1,208,768]{2,1,0:T(8,128)(2,1)} %copy-done.35, bf16[1,208,768]{2,1,0:T(8,128)(2,1)} %collective-permute-done.1.rest_2_, ...), custom_call_target="tpu_custom_call" | custom-call | flops 1 | bytes 1 | tf_op jit(solution)/shard_map/place_rows/pallas_call | solution.py:80
  85.3 26.3 %forward_units.1 = (bf16[2,256,2048]{2,1,0:T(8,128)(2,1)}, bf16[2,256,2048]{2,1,0:T(8,128)(2,1)}, bf16[2,256,2048]{2,1,0:T(8,128)(2,1)}, bf16[2,256,32]{2,1,0:T(8,128)(2,1)}) custom-call(bf16[2,256,3072]{2,1,0:T(8,128)(2,1)} %place_rows.2.refs_0_, bf16[2,3072,2048]{2,1,0:T(8,128)(2,1)} %refs_3_.3, bf16[2,3072,2048]{2,1,0:T(8,128)(2,1)} %refs_4_.5, ...), custom_call_target="tpu_custom_call" | custom-call | flops 1 | bytes 1 | tf_op jit(solution)/shard_map/forward_units/pallas_call | solution.py:128
  111.6 0.8 copy-done.6
  113.2 0.8 copy-done.7
  114.0 0.8 copy-done.5
  115.7 0.9 copy.98.rest_0_
  116.5 0.9 or_convert_fusion.refs_5_
  119.0 0.8 copy-done.20
  119.8 5.1 %place_rows.3.g_ref = bf16[2,256,3072]{2,1,0:T(8,128)(2,1)} custom-call(s32[1]{0:T(128)} %bitcast.1.at_ref, bf16[4,128,192]{2,1,0:T(8,128)(2,1)} %fusion.9.place_ref, f32[4,128,1]{2,1,0:T(8,128)} %copy.98.rest_0_, bf16[2,192,768]{2,1,0:T(8,128)(2,1)} %copy-done.3, bf16[2,192,768]{2,1,0:T(8,128)(2,1)} %tie.14.rest_2_.rest_6_, bf16[2,192,768]{2,1,0:T(8,128)(2,1)} %copy-done.4, ...), custom_call_target="tpu_custom_call" | custom-call | flops 1 | bytes 1 | tf_op jit(solution)/shard_map/place_rows/pallas_call | solution.py:80
  125.0 17.8 %hidden_back.1 = (bf16[2,256,2048]{2,1,0:T(8,128)(2,1)}, bf16[2,256,2048]{2,1,0:T(8,128)(2,1)}, bf16[2,256,48]{2,1,0:T(8,128)(2,1)}, bf16[2,256,16]{2,1,0:T(8,128)(2,1)}) custom-call(bf16[2,256,3072]{2,1,0:T(8,128)(2,1)} %place_rows.3.g_ref, bf16[2,2048,3072]{2,1,0:T(8,128)(2,1)} %wd_ref.1, bf16[2,16,3072]{2,1,0:T(8,128)(2,1)} %slice.247.out_ref, ...), custom_call_target="tpu_custom_call" | custom-call | flops 1 | bytes 1 | tf_op jit(solution)/shard_map/hidden_back/pallas_call | solution.py:175
  142.8 16.8 %row_back.2 = (bf16[384,768]{1,0:T(8,128)(2,1)}, bf16[384,768]{1,0:T(8,128)(2,1)}, bf16[384,768]{1,0:T(8,128)(2,1)}, bf16[384,768]{1,0:T(8,128)(2,1)}) custom-call(s32[2]{0:T(128)} %pad_add_fusion.1.refs_0_, bf16[2,256,2048]{2,1,0:T(8,128)(2,1)} %get-tuple-element.29.refs_1_, bf16[2,256,2048]{2,1,0:T(8,128)(2,1)} %get-tuple-element.30.refs_2_, ...), custom_call_target="tpu_custom_call" | custom-call | flops 1 | bytes 1 | tf_op jit(solution)/shard_map/row_back/pallas_call | solution.py:258
  160.1 1.8 collective-permute-done.21
  161.9 1.2 convert_add_fusion.3
  164.7 1.5 collective-permute-start.25
  166.8 1.0 copy.99
  167.9 1.0 copy.100
  168.9 16.7 %row_back.3 = (bf16[384,768]{1,0:T(8,128)(2,1)}, bf16[384,768]{1,0:T(8,128)(2,1)}, bf16[384,768]{1,0:T(8,128)(2,1)}, bf16[384,768]{1,0:T(8,128)(2,1)}) custom-call(s32[2]{0:T(128)} %pad_add_fusion.refs_0_, bf16[2,256,2048]{2,1,0:T(8,128)(2,1)} %get-tuple-element.29.refs_1_, bf16[2,256,2048]{2,1,0:T(8,128)(2,1)} %get-tuple-element.30.refs_2_, ...), custom_call_target="tpu_custom_call" | custom-call | flops 1 | bytes 1 | tf_op jit(solution)/shard_map/row_back/pallas_call | solution.py:258
  188.2 1.8 collective-permute-start.27
  191.7 1.2 convert_add_fusion.1
  192.9 1.0 copy-done.11
  194.6 4.0 %adapter_back.1 = (f32[2,16,2048]{2,1,0:T(8,128)}, f32[2,16,2048]{2,1,0:T(8,128)}, f32[2,16,2048]{2,1,0:T(8,128)}) custom-call(bf16[2,48,256]{2,1,0:T(8,128)(2,1)} %maximum_bitcast_fusion.1.refs_0_, bf16[2,256,2048]{2,1,0:T(8,128)(2,1)} %get-tuple-element.29.refs_1_, bf16[2,256,2048]{2,1,0:T(8,128)(2,1)} %get-tuple-element.30.refs_2_, ...), custom_call_target="tpu_custom_call" | custom-call | flops 1 | bytes 1 | tf_op jit(solution)/shard_map/adapter_back/pallas_call | solution.py:215
  198.7 6.4 %collective-permute-done.27.refs_1_ = bf16[416,768]{1,0:T(8,128)(2,1)S(1)} collective-permute-done((bf16[416,768]{1,0:T(8,128)(2,1)S(1)}, bf16[416,768]{1,0:T(8,128)(2,1)S(1)}, u32[]{:S(2)}, u32[]{:S(2)}) %collective-permute-start.27) | collective-permute-done | bytes 639008 | tf_op jit(solution)/shard_map/ppermute | solution.py:31
  205.9 1.1 fusion.4
  207.1 0.9 collective-permute-start.30
  208.5 16.6 %collective-permute-done.30 = bf16[224,768]{1,0:T(8,128)(2,1)S(1)} collective-permute-done((bf16[224,768]{1,0:T(8,128)(2,1)S(1)}, bf16[224,768]{1,0:T(8,128)(2,1)S(1)}, u32[]{:S(2)}, u32[]{:S(2)}) %collective-permute-start.30) | collective-permute-done | bytes 344096 | tf_op jit(solution)/shard_map/ppermute | solution.py:31
  225.3 1.5 convolution_multiply_fusion
  226.9 2.1 convolution_multiply_fusion.1
  229.7 0.8 fusion.3
  (225 shorter events, 31.5 us)
Async XLA Ops:
  0.6 7.3 %copy-start.27 = (bf16[192,768]{1,0:T(8,128)(2,1)S(1)}, bf16[192,768]{1,0:T(8,128)(2,1)}, u32[]{:S(2)}) copy-start(bf16[192,768]{1,0:T(8,128)(2,1)} %param.14) | copy-start | bytes 884740
  2.3 8.9 %copy-start.28 = (bf16[192,768]{1,0:T(8,128)(2,1)S(1)}, bf16[192,768]{1,0:T(8,128)(2,1)}, u32[]{:S(2)}) copy-start(bf16[192,768]{1,0:T(8,128)(2,1)} %param.15) | copy-start | bytes 884740
  3.9 8.0 %copy-start.37 = (bf16[2,16,768]{2,1,0:T(8,128)(2,1)S(1)}, bf16[2,16,768]{2,1,0:T(8,128)(2,1)}, u32[]{:S(2)}) copy-start(bf16[2,16,768]{2,1,0:T(8,128)(2,1)} %param.21) | copy-start | bytes 147460
  3.9 8.0 %copy-start.38 = (bf16[2,16,768]{2,1,0:T(8,128)(2,1)S(1)}, bf16[2,16,768]{2,1,0:T(8,128)(2,1)}, u32[]{:S(2)}) copy-start(bf16[2,16,768]{2,1,0:T(8,128)(2,1)} %param.23) | copy-start | bytes 147460
  3.9 8.0 %copy-start.39 = (bf16[2,16,768]{2,1,0:T(8,128)(2,1)S(1)}, bf16[2,16,768]{2,1,0:T(8,128)(2,1)}, u32[]{:S(2)}) copy-start(bf16[2,16,768]{2,1,0:T(8,128)(2,1)} %param.26) | copy-start | bytes 147460
  4.9 8.4 %copy-start.22 = (bf16[1,208,768]{2,1,0:T(8,128)(2,1)}, bf16[1,208,768]{2,1,0:T(8,128)(2,1)S(1)}, u32[]{:S(2)}) copy-start(bf16[1,208,768]{2,1,0:T(8,128)(2,1)S(1)} %maximum_bitcast_fusion.rest_0_) | copy-start | bytes 958468
  4.9 7.7 %copy-start = (s32[4]{0:T(128)S(1)}, s32[4]{0:T(128)}, u32[]{:S(2)}) copy-start(s32[4]{0:T(128)} %constant.50.clone) | copy-start | bytes 52
  4.9 27.3 %collective-permute-start = (bf16[1,208,768]{2,1,0:T(8,128)(2,1)S(1)}, bf16[1,208,768]{2,1,0:T(8,128)(2,1)S(1)}, u32[]{:S(2)}, u32[]{:S(2)}) collective-permute-start(bf16[1,208,768]{2,1,0:T(8,128)(2,1)S(1)} %maximum_bitcast_fusion.rest_0_), channel_id=1, source_target_pairs={{0,8},{4,12},{8,0},{12,4},{1,9},{5,13},{9,1},{13,5},{2,10},{6,14},... | collective-permute-start | bytes 958472 | tf_op jit(solution)/shard_map/ppermute | solution.py:31
  8.0 23.1 %collective-permute-start.1 = (bf16[1,208,768]{2,1,0:T(8,128)(2,1)S(1)}, bf16[1,208,768]{2,1,0:T(8,128)(2,1)}, u32[]{:S(2)}, u32[]{:S(2)}) collective-permute-start(bf16[1,208,768]{2,1,0:T(8,128)(2,1)S(1)} %maximum_bitcast_fusion.rest_0_), channel_id=1, source_target_pairs={{0,4},{4,0},{8,12},{12,8},{1,5},{5,1},{9,13},{13,9},{2,6},{6,2},{1... | collective-permute-start | bytes 958472 | tf_op jit(solution)/shard_map/ppermute | solution.py:31
  8.0 16.6 %collective-permute-start.3 = (bf16[1,192,768]{2,1,0:T(8,128)(2,1)S(1)}, bf16[1,192,768]{2,1,0:T(8,128)(2,1)S(1)}, u32[]{:S(2)}, u32[]{:S(2)}) collective-permute-start(bf16[1,192,768]{2,1,0:T(8,128)(2,1)S(1)} %bitcast.49), channel_id=1, source_target_pairs={{0,2},{1,3},{2,0},{3,1},{4,6},{5,7},{6,4},{7,5},{8,10},{9,11},{10,... | collective-permute-start | bytes 884744 | tf_op jit(solution)/shard_map/ppermute | solution.py:31
  11.9 48.6 %copy-start.21 = (bf16[2,48,768]{2,1,0:T(8,128)(2,1)}, bf16[2,48,768]{2,1,0:T(8,128)(2,1)S(1)}, u32[]{:S(2)}) copy-start(bf16[2,48,768]{2,1,0:T(8,128)(2,1)S(1)} %constant_dynamic-update-slice_fusion) | copy-start | bytes 442372
  25.3 16.2 %collective-permute-start.4 = (bf16[1,192,768]{2,1,0:T(8,128)(2,1)}, bf16[1,192,768]{2,1,0:T(8,128)(2,1)S(1)}, u32[]{:S(2)}, u32[]{:S(2)}) collective-permute-start(bf16[1,192,768]{2,1,0:T(8,128)(2,1)} %bitcast.48), channel_id=1, source_target_pairs={{0,2},{1,3},{2,0},{3,1},{4,6},{5,7},{6,4},{7,5},{8,10},{9,11},{10,... | collective-permute-start | bytes 884744 | tf_op jit(solution)/shard_map/ppermute | solution.py:31
  26.4 23.3 %collective-permute-start.9 = (bf16[2,192,768]{2,1,0:T(8,128)(2,1)S(1)}, bf16[2,192,768]{2,1,0:T(8,128)(2,1)S(1)}, u32[]{:S(2)}, u32[]{:S(2)}) collective-permute-start(bf16[2,192,768]{2,1,0:T(8,128)(2,1)S(1)} %pad_maximum_fusion.2), channel_id=1, source_target_pairs={{0,1},{1,0},{2,3},{3,2},{4,5},{5,4},{6,7},{7,6},{8,9},{9,8},{10,11... | collective-permute-start | bytes 1769480 | tf_op jit(solution)/shard_map/ppermute | solution.py:31
  30.5 13.8 %collective-permute-start.6 = (bf16[1,192,768]{2,1,0:T(8,128)(2,1)}, bf16[1,192,768]{2,1,0:T(8,128)(2,1)S(1)}, u32[]{:S(2)}, u32[]{:S(2)}) collective-permute-start(bf16[1,192,768]{2,1,0:T(8,128)(2,1)} %copy-done.17), channel_id=1, source_target_pairs={{0,8},{4,12},{8,0},{12,4},{1,9},{5,13},{9,1},{13,5},{2,10},{6,14},... | collective-permute-start | bytes 884744 | tf_op jit(solution)/shard_map/ppermute | solution.py:31
  31.0 36.6 %collective-permute-start.7 = (bf16[1,192,768]{2,1,0:T(8,128)(2,1)}, bf16[1,192,768]{2,1,0:T(8,128)(2,1)}, u32[]{:S(2)}, u32[]{:S(2)}) collective-permute-start(bf16[1,192,768]{2,1,0:T(8,128)(2,1)} %copy-done.17), channel_id=1, source_target_pairs={{0,4},{4,0},{8,12},{12,8},{1,5},{5,1},{9,13},{13,9},{2,6},{6,2},{1... | collective-permute-start | bytes 884744 | tf_op jit(solution)/shard_map/ppermute | solution.py:31
  32.3 9.3 %copy-start.35 = (bf16[1,208,768]{2,1,0:T(8,128)(2,1)}, bf16[1,208,768]{2,1,0:T(8,128)(2,1)S(1)}, u32[]{:S(2)}) copy-start(bf16[1,208,768]{2,1,0:T(8,128)(2,1)S(1)} %collective-permute-done.rest_1_) | copy-start | bytes 958468
  33.0 8.7 %collective-permute-start.2 = (bf16[1,208,768]{2,1,0:T(8,128)(2,1)S(1)}, bf16[1,208,768]{2,1,0:T(8,128)(2,1)S(1)}, u32[]{:S(2)}, u32[]{:S(2)}) collective-permute-start(bf16[1,208,768]{2,1,0:T(8,128)(2,1)S(1)} %collective-permute-done.rest_1_), channel_id=1, source_target_pairs={{0,4},{4,0},{8,12},{12,8},{1,5},{5,1},{9,13},{13,9},{2,6},{6,2},{1... | collective-permute-start | bytes 958472 | tf_op jit(solution)/shard_map/ppermute | solution.py:31
  41.5 8.1 %copy-start.25 = (bf16[1,192,768]{2,1,0:T(8,128)(2,1)}, bf16[1,192,768]{2,1,0:T(8,128)(2,1)S(1)}, u32[]{:S(2)}) copy-start(bf16[1,192,768]{2,1,0:T(8,128)(2,1)S(1)} %collective-permute-done.4.refs_1_) | copy-start | bytes 884740
  41.6 25.2 %copy-start.3 = (bf16[2,192,768]{2,1,0:T(8,128)(2,1)}, bf16[2,192,768]{2,1,0:T(8,128)(2,1)S(1)}, u32[]{:S(2)}) copy-start(bf16[2,192,768]{2,1,0:T(8,128)(2,1)S(1)} %pad_maximum_fusion.1.rest_1_.rest_5_) | copy-start | bytes 1769476
  41.6 23.0 %collective-permute-start.11 = (bf16[2,192,768]{2,1,0:T(8,128)(2,1)S(1)}, bf16[2,192,768]{2,1,0:T(8,128)(2,1)S(1)}, u32[]{:S(2)}, u32[]{:S(2)}) collective-permute-start(bf16[2,192,768]{2,1,0:T(8,128)(2,1)S(1)} %pad_maximum_fusion.1.rest_1_.rest_5_), channel_id=1, source_target_pairs={{0,1},{1,0},{2,3},{3,2},{4,5},{5,4},{6,7},{7,6},{8,9},{9,8},{10,11... | collective-permute-start | bytes 1769480 | tf_op jit(solution)/shard_map/ppermute | solution.py:31
  44.3 5.3 %copy-start.31 = (bf16[1,192,768]{2,1,0:T(8,128)(2,1)}, bf16[1,192,768]{2,1,0:T(8,128)(2,1)S(1)}, u32[]{:S(2)}) copy-start(bf16[1,192,768]{2,1,0:T(8,128)(2,1)S(1)} %collective-permute-done.6.refs_2_.rest_5_) | copy-start | bytes 884740
  50.5 15.7 %collective-permute-start.10 = (bf16[2,192,768]{2,1,0:T(8,128)(2,1)}, bf16[2,192,768]{2,1,0:T(8,128)(2,1)S(1)}, u32[]{:S(2)}, u32[]{:S(2)}) collective-permute-start(bf16[2,192,768]{2,1,0:T(8,128)(2,1)} %tie.11.refs_1_.rest_8_.rest_12_), channel_id=1, source_target_pairs={{0,8},{4,12},{8,0},{12,4},{1,9},{5,13},{9,1},{13,5},{2,10},{6,14},... | collective-permute-start | bytes 1769480 | tf_op jit(solution)/shard_map/ppermute | solution.py:31
  51.2 15.6 %collective-permute-start.13 = (bf16[2,192,768]{2,1,0:T(8,128)(2,1)}, bf16[2,192,768]{2,1,0:T(8,128)(2,1)S(1)}, u32[]{:S(2)}, u32[]{:S(2)}) collective-permute-start(bf16[2,192,768]{2,1,0:T(8,128)(2,1)} %tie.11.refs_1_.rest_8_.rest_12_), channel_id=1, source_target_pairs={{0,4},{4,0},{8,12},{12,8},{1,5},{5,1},{9,13},{13,9},{2,6},{6,2},{1... | collective-permute-start | bytes 1769480 | tf_op jit(solution)/shard_map/ppermute | solution.py:31
  51.2 9.4 %collective-permute-start.12 = (bf16[1,2,48,768]{3,2,1,0:T(8,128)(2,1)}, bf16[1,2,48,768]{3,2,1,0:T(8,128)(2,1)S(1)}, u32[]{:S(2)}, u32[]{:S(2)}) collective-permute-start(bf16[1,2,48,768]{3,2,1,0:T(8,128)(2,1)} %bitcast.52), channel_id=1, source_target_pairs={{0,2},{1,3},{2,0},{3,1},{4,6},{5,7},{6,4},{7,5},{8,10},{9,11},{10,... | collective-permute-start | bytes 442376 | tf_op jit(solution)/shard_map/ppermute | solution.py:31
  60.6 6.2 %copy-start.23 = (bf16[1,2,48,768]{3,2,1,0:T(8,128)(2,1)}, bf16[1,2,48,768]{3,2,1,0:T(8,128)(2,1)S(1)}, u32[]{:S(2)}) copy-start(bf16[1,2,48,768]{3,2,1,0:T(8,128)(2,1)S(1)} %collective-permute-done.12.refs_2_) | copy-start | bytes 442372
  60.6 8.5 %collective-permute-start.8 = (bf16[1,192,768]{2,1,0:T(8,128)(2,1)}, bf16[1,192,768]{2,1,0:T(8,128)(2,1)}, u32[]{:S(2)}, u32[]{:S(2)}) collective-permute-start(bf16[1,192,768]{2,1,0:T(8,128)(2,1)} %copy-done.31), channel_id=1, source_target_pairs={{0,4},{4,0},{8,12},{12,8},{1,5},{5,1},{9,13},{13,9},{2,6},{6,2},{1... | collective-permute-start | bytes 884744 | tf_op jit(solution)/shard_map/ppermute | solution.py:31
  64.6 9.5 %collective-permute-start.15 = (bf16[2,2,48,768]{3,2,1,0:T(8,128)(2,1)}, bf16[2,2,48,768]{3,2,1,0:T(8,128)(2,1)}, u32[]{:S(2)}, u32[]{:S(2)}) collective-permute-start(bf16[2,2,48,768]{3,2,1,0:T(8,128)(2,1)} %pad_maximum_fusion.5), channel_id=1, source_target_pairs={{0,1},{1,0},{2,3},{3,2},{4,5},{5,4},{6,7},{7,6},{8,9},{9,8},{10,11... | collective-permute-start | bytes 884744 | tf_op jit(solution)/shard_map/ppermute | solution.py:31
  66.2 45.4 %collective-permute-start.5 = (bf16[2,192,768]{2,1,0:T(8,128)(2,1)S(1)}, bf16[2,192,768]{2,1,0:T(8,128)(2,1)S(1)}, u32[]{:S(2)}, u32[]{:S(2)}) collective-permute-start(bf16[2,192,768]{2,1,0:T(8,128)(2,1)S(1)} %pad_maximum_fusion.1.rest_1_.rest_5_), channel_id=1, source_target_pairs={{0,8},{4,12},{8,0},{12,4},{1,9},{5,13},{9,1},{13,5},{2,10},{6,14},... | collective-permute-start | bytes 1769480 | tf_op jit(solution)/shard_map/ppermute | solution.py:31
  66.8 44.8 %collective-permute-start.16 = (bf16[2,192,768]{2,1,0:T(8,128)(2,1)S(1)}, bf16[2,192,768]{2,1,0:T(8,128)(2,1)S(1)}, u32[]{:S(2)}, u32[]{:S(2)}) collective-permute-start(bf16[2,192,768]{2,1,0:T(8,128)(2,1)S(1)} %pad_maximum_fusion.1.rest_1_.rest_5_), channel_id=1, source_target_pairs={{0,4},{4,0},{8,12},{12,8},{1,5},{5,1},{9,13},{13,9},{2,6},{6,2},{1... | collective-permute-start | bytes 1769480 | tf_op jit(solution)/shard_map/ppermute | solution.py:31
  67.6 45.5 %collective-permute-start.18 = (bf16[2,192,768]{2,1,0:T(8,128)(2,1)}, bf16[2,192,768]{2,1,0:T(8,128)(2,1)S(1)}, u32[]{:S(2)}, u32[]{:S(2)}) collective-permute-start(bf16[2,192,768]{2,1,0:T(8,128)(2,1)} %copy-done.2), channel_id=1, source_target_pairs={{0,8},{4,12},{8,0},{12,4},{1,9},{5,13},{9,1},{13,5},{2,10},{6,14},... | collective-permute-start | bytes 1769480 | tf_op jit(solution)/shard_map/ppermute | solution.py:31
  69.1 44.0 %collective-permute-start.19 = (bf16[2,192,768]{2,1,0:T(8,128)(2,1)}, bf16[2,192,768]{2,1,0:T(8,128)(2,1)S(1)}, u32[]{:S(2)}, u32[]{:S(2)}) collective-permute-start(bf16[2,192,768]{2,1,0:T(8,128)(2,1)} %copy-done.2), channel_id=1, source_target_pairs={{0,4},{4,0},{8,12},{12,8},{1,5},{5,1},{9,13},{13,9},{2,6},{6,2},{1... | collective-permute-start | bytes 1769480 | tf_op jit(solution)/shard_map/ppermute | solution.py:31
  74.1 6.2 %collective-permute-start.14 = (bf16[2,192,768]{2,1,0:T(8,128)(2,1)}, bf16[2,192,768]{2,1,0:T(8,128)(2,1)}, u32[]{:S(2)}, u32[]{:S(2)}) collective-permute-start(bf16[2,192,768]{2,1,0:T(8,128)(2,1)} %tie.13.rest_9_.rest_13_), channel_id=1, source_target_pairs={{0,4},{4,0},{8,12},{12,8},{1,5},{5,1},{9,13},{13,9},{2,6},{6,2},{1... | collective-permute-start | bytes 1769480 | tf_op jit(solution)/shard_map/ppermute | solution.py:31
  112.6 2.8 %copy-start.40 = (f32[128]{0:T(128)S(1)}, f32[128]{0:T(128)}, u32[]{:S(2)}) copy-start(f32[128]{0:T(128)} %add_convert_fusion) | copy-start | bytes 1540
  112.6 5.5 %collective-permute-start.17 = (bf16[2,192,768]{2,1,0:T(8,128)(2,1)}, bf16[2,192,768]{2,1,0:T(8,128)(2,1)S(1)}, u32[]{:S(2)}, u32[]{:S(2)}) collective-permute-start(bf16[2,192,768]{2,1,0:T(8,128)(2,1)} %tie.14.rest_2_.rest_6_), channel_id=1, source_target_pairs={{0,4},{4,0},{8,12},{12,8},{1,5},{5,1},{9,13},{13,9},{2,6},{6,2},{1... | collective-permute-start | bytes 1769480 | tf_op jit(solution)/shard_map/ppermute | solution.py:31
  114.8 3.4 %collective-permute-start.20 = (bf16[2,192,768]{2,1,0:T(8,128)(2,1)}, bf16[2,192,768]{2,1,0:T(8,128)(2,1)S(1)}, u32[]{:S(2)}, u32[]{:S(2)}) collective-permute-start(bf16[2,192,768]{2,1,0:T(8,128)(2,1)} %tie.15.rest_10_.rest_14_), channel_id=1, source_target_pairs={{0,4},{4,0},{8,12},{12,8},{1,5},{5,1},{9,13},{13,9},{2,6},{6,2},{1... | collective-permute-start | bytes 1769480 | tf_op jit(solution)/shard_map/ppermute | solution.py:31
  159.6 2.3 %collective-permute-start.21 = (bf16[384,768]{1,0:T(8,128)(2,1)}, bf16[384,768]{1,0:T(8,128)(2,1)S(1)}, u32[]{:S(2)}, u32[]{:S(2)}) collective-permute-start(bf16[384,768]{1,0:T(8,128)(2,1)} %get-tuple-element.33), channel_id=1, source_target_pairs={{0,4},{4,0},{8,12},{12,8},{1,5},{5,1},{9,13},{13,9},{2,6},{6,2},{1... | collective-permute-start | bytes 1769480 | tf_op jit(solution)/shard_map/ppermute | solution.py:31
  160.1 3.8 %collective-permute-start.22 = (bf16[384,768]{1,0:T(8,128)(2,1)}, bf16[384,768]{1,0:T(8,128)(2,1)S(1)}, u32[]{:S(2)}, u32[]{:S(2)}) collective-permute-start(bf16[384,768]{1,0:T(8,128)(2,1)} %get-tuple-element.35), channel_id=1, source_target_pairs={{0,4},{4,0},{8,12},{12,8},{1,5},{5,1},{9,13},{13,9},{2,6},{6,2},{1... | collective-permute-start | bytes 1769480 | tf_op jit(solution)/shard_map/ppermute | solution.py:31
  163.2 22.4 %collective-permute-start.26 = (bf16[192,768]{1,0:T(8,128)(2,1)S(1)}, bf16[192,768]{1,0:T(8,128)(2,1)S(1)}, u32[]{:S(2)}, u32[]{:S(2)}) collective-permute-start(bf16[192,768]{1,0:T(8,128)(2,1)S(1)} %slice.329.refs_8_), channel_id=1, source_target_pairs={{0,8},{4,12},{8,0},{12,4},{1,9},{5,13},{9,1},{13,5},{2,10},{6,14},... | collective-permute-start | bytes 884744 | tf_op jit(solution)/shard_map/ppermute | solution.py:31
  163.8 3.9 %copy-start.24 = (bf16[2,256,48]{2,1,0:T(8,128)(2,1)S(1)}, bf16[2,256,48]{2,1,0:T(8,128)(2,1)}, u32[]{:S(2)}) copy-start(bf16[2,256,48]{2,1,0:T(8,128)(2,1)} %get-tuple-element.31.refs_6_) | copy-start | bytes 147460
  164.7 21.7 %collective-permute-start.25 = (bf16[192,768]{1,0:T(8,128)(2,1)}, bf16[192,768]{1,0:T(8,128)(2,1)S(1)}, u32[]{:S(2)}, u32[]{:S(2)}) collective-permute-start(bf16[192,768]{1,0:T(8,128)(2,1)} %slice.328.refs_9_), channel_id=1, source_target_pairs={{0,8},{4,12},{8,0},{12,4},{1,9},{5,13},{9,1},{13,5},{2,10},{6,14},... | collective-permute-start | bytes 884744 | tf_op jit(solution)/shard_map/ppermute | solution.py:31
  185.6 5.8 %collective-permute-start.23 = (bf16[384,768]{1,0:T(8,128)(2,1)}, bf16[384,768]{1,0:T(8,128)(2,1)}, u32[]{:S(2)}, u32[]{:S(2)}) collective-permute-start(bf16[384,768]{1,0:T(8,128)(2,1)} %get-tuple-element.37), channel_id=1, source_target_pairs={{0,4},{4,0},{8,12},{12,8},{1,5},{5,1},{9,13},{13,9},{2,6},{6,2},{1... | collective-permute-start | bytes 1769480 | tf_op jit(solution)/shard_map/ppermute | solution.py:31
  187.1 3.5 %collective-permute-start.28 = (bf16[384,768]{1,0:T(8,128)(2,1)}, bf16[384,768]{1,0:T(8,128)(2,1)S(1)}, u32[]{:S(2)}, u32[]{:S(2)}) collective-permute-start(bf16[384,768]{1,0:T(8,128)(2,1)} %tie.18), channel_id=1, source_target_pairs={{0,4},{4,0},{8,12},{12,8},{1,5},{5,1},{9,13},{13,9},{2,6},{6,2},{1... | collective-permute-start | bytes 1769480 | tf_op jit(solution)/shard_map/ppermute | solution.py:31
  188.2 16.8 %collective-permute-start.27 = (bf16[416,768]{1,0:T(8,128)(2,1)S(1)}, bf16[416,768]{1,0:T(8,128)(2,1)S(1)}, u32[]{:S(2)}, u32[]{:S(2)}) collective-permute-start(bf16[416,768]{1,0:T(8,128)(2,1)S(1)} %pad_maximum_fusion), channel_id=1, source_target_pairs={{0,1},{1,0},{2,3},{3,2},{4,5},{5,4},{6,7},{7,6},{8,9},{9,8},{10,11... | collective-permute-start | bytes 1916936 | tf_op jit(solution)/shard_map/ppermute | solution.py:31
  190.8 3.8 %copy-start.30 = (bf16[192,768]{1,0:T(8,128)(2,1)}, bf16[192,768]{1,0:T(8,128)(2,1)S(1)}, u32[]{:S(2)}) copy-start(bf16[192,768]{1,0:T(8,128)(2,1)S(1)} %slice.326.refs_4_) | copy-start | bytes 884740
  190.8 14.4 %collective-permute-start.29 = (bf16[192,768]{1,0:T(8,128)(2,1)S(1)}, bf16[192,768]{1,0:T(8,128)(2,1)S(1)}, u32[]{:S(2)}, u32[]{:S(2)}) collective-permute-start(bf16[192,768]{1,0:T(8,128)(2,1)S(1)} %slice.326.refs_4_), channel_id=1, source_target_pairs={{0,8},{4,12},{8,0},{12,4},{1,9},{5,13},{9,1},{13,5},{2,10},{6,14},... | collective-permute-start | bytes 884744 | tf_op jit(solution)/shard_map/ppermute | solution.py:31
  207.1 18.0 %collective-permute-start.30 = (bf16[224,768]{1,0:T(8,128)(2,1)S(1)}, bf16[224,768]{1,0:T(8,128)(2,1)S(1)}, u32[]{:S(2)}, u32[]{:S(2)}) collective-permute-start(bf16[224,768]{1,0:T(8,128)(2,1)S(1)} %pad_maximum_fusion.4), channel_id=1, source_target_pairs={{0,2},{1,3},{2,0},{3,1},{4,6},{5,7},{6,4},{7,5},{8,10},{9,11},{10,... | collective-permute-start | bytes 1032200 | tf_op jit(solution)/shard_map/ppermute | solution.py:31
  207.9 21.7 %collective-permute-start.24 = (bf16[192,768]{1,0:T(8,128)(2,1)S(1)}, bf16[192,768]{1,0:T(8,128)(2,1)S(1)}, u32[]{:S(2)}, u32[]{:S(2)}) collective-permute-start(bf16[192,768]{1,0:T(8,128)(2,1)S(1)} %copy-done.29), channel_id=1, source_target_pairs={{0,8},{4,12},{8,0},{12,4},{1,9},{5,13},{9,1},{13,5},{2,10},{6,14},... | collective-permute-start | bytes 884744 | tf_op jit(solution)/shard_map/ppermute | solution.py:31
  225.3 4.3 %copy-start.12 = (f32[384,768]{1,0:T(8,128)S(1)}, f32[384,768]{1,0:T(8,128)}, u32[]{:S(2)}) copy-start(f32[384,768]{1,0:T(8,128)} %copy-done.11) | copy-start | bytes 3538948
  (24 other events, 26.9 us)

commit v3 on v2

--- a/solution.py
+++ b/solution.py
@@ -16,14 +16,15 @@
 BF16 = jnp.bfloat16
 NN = (((1,), (0,)), ((), ()))
 NT = (((1,), (1,)), ((), ()))
+TN = (((0,), (0,)), ((), ()))
 
 
 def mm(a, b, dims=NN):
     return lax.dot_general(a, b, dims, preferred_element_type=F32)
 
 
-def params(semantics):
-    return pltpu.CompilerParams(dimension_semantics=semantics, vmem_limit_bytes=56 * 1024 * 1024)
+def params(semantics, mib=56):
+    return pltpu.CompilerParams(dimension_semantics=semantics, vmem_limit_bytes=mib * 1024 * 1024)
 
 
 def swap(x, k, axis):
@@ -91,66 +92,88 @@
             out_specs=whole(count, n, len(far) * col),
         ),
         out_shape=jax.ShapeDtypeStruct((count, n, len(far) * col), BF16),
-        compiler_params=params(("arbitrary",)),
+        compiler_params=params(("arbitrary",), 61),
         cost_estimate=COST,
         name="place_rows",
     )(at, place, *gates, *[array for array, _ in pieces])
 
 
-def forward_kernel(x_ref, wg_ref, wu_ref, in_ref, go_ref, uo_ref, a_ref, b_ref, h_ref, low_ref):
+def low_rank(rows_ref, at_ref, far, factor_refs, ranks):
+    total = 0.0
+    for k, ref in zip(far, factor_refs):
+        col = ref.shape[3]
+        columns = pl.ds(pl.multiple_of((at_ref[0] ^ k) * col, col), col) if len(far) > 1 else slice(None)
+        total = total + mm(rows_ref[0, :, columns], ref[0, 0, ranks], NT)
+    return total.astype(BF16)
+
+
+def factor_specs(factors):
+    return [
+        pl.BlockSpec((1, 1) + array.shape[2:], lambda l, f, p, index=index: (index, l, 0, 0))
+        for array, index in factors
+    ]
+
+
+def forward_kernel(far, at_ref, x_ref, wg_ref, wu_ref, go_ref, uo_ref, *rest):
+    *factor_refs, a_ref, b_ref, h_ref, low_ref = rest
     x = x_ref[0]
     rank = go_ref.shape[1]
 
     @pl.when(pl.program_id(1) == 0)
     def _():
-        low_ref[0] = mm(x, in_ref[0], NT).astype(BF16)
+        low_ref[0] = low_rank(x_ref, at_ref, far, factor_refs, slice(0, 2 * rank))
 
     low = low_ref[0]
-    gate = mm(x, wg_ref[0]) + adapter_scale * mm(low[:, :rank], go_ref[0])
-    up = mm(x, wu_ref[0]) + adapter_scale * mm(low[:, rank:], uo_ref[0])
-    q = jax.nn.sigmoid(gate)
-    silu = gate * q
-    a_ref[0] = (up * (q + silu * (1.0 - q))).astype(BF16)
-    b_ref[0] = silu.astype(BF16)
-    h_ref[0] = (silu * up).astype(BF16)
-
-
-def forward(first, number, rows, wg, wu, factor_in, go, uo, held=()):
+    units = go_ref.shape[2]
+    step = min(512, units)
+    for start in range(0, units, step):
+        f = slice(start, start + step)
+        gate = mm(x, wg_ref[0, :, f]) + adapter_scale * mm(low[:, :rank], go_ref[0, :, f])
+        up = mm(x, wu_ref[0, :, f]) + adapter_scale * mm(low[:, rank:], uo_ref[0, :, f])
+        q = 0.5 * jnp.tanh(0.5 * gate) + 0.5
+        silu = gate * q
+        a_ref[0, :, f] = (up * (q + silu * (1.0 - q))).astype(BF16)
+        b_ref[0, :, f] = silu.astype(BF16)
+        h_ref[0, :, f] = (silu * up).astype(BF16)
+
+
+def forward(at, rows, wg, wu, go, uo, factors, far):
     count, n, width = rows.shape
     units = wg.shape[2]
     rank = go.shape[1]
-    ft = min(512, units)
+    ft = min(1024, units)
     out = jax.ShapeDtypeStruct((count, n, units), BF16)
-    wide = pl.BlockSpec((1, n, ft), lambda l, f: (l + first, 0, f))
-    weight = pl.BlockSpec((1, width, ft), lambda l, f: (l + first, 0, f))
-    factor = pl.BlockSpec((1, rank, ft), lambda l, f: (l + first, 0, f))
-    one = lambda *shape: pl.BlockSpec((1,) + shape, lambda l, f: (l + first, 0, 0))
+    wide = pl.BlockSpec((1, n, ft), lambda l, f, p: (l, 0, f))
+    weight = pl.BlockSpec((1, width, ft), lambda l, f, p: (l, 0, f))
+    factor = pl.BlockSpec((1, rank, ft), lambda l, f, p: (l, 0, f))
+    one = lambda *shape: pl.BlockSpec((1,) + shape, lambda l, f, p: (l, 0, 0))
     return pl.pallas_call(
-        without(forward_kernel, 6, len(held)),
-        grid=(number, units // ft),
-        in_specs=[one(n, width), weight, weight, one(2 * rank, width), factor, factor]
-        + [ANY for _ in held],
-        out_specs=[wide, wide, wide, one(n, 2 * rank)],
+        functools.partial(forward_kernel, far),
+        grid_spec=pltpu.PrefetchScalarGridSpec(
+            num_scalar_prefetch=1,
+            grid=(count, units // ft),
+            in_specs=[one(n, width), weight, weight, factor, factor] + factor_specs(factors),
+            out_specs=[wide, wide, wide, one(n, 2 * rank)],
+        ),
         out_shape=[out, out, out, jax.ShapeDtypeStruct((count, n, 2 * rank), BF16)],
-        input_output_aliases={6 + i: i for i in range(len(held))},
         compiler_params=params(("arbitrary", "arbitrary")),
         cost_estimate=COST,
         name="forward_units",
-    )(rows, wg, wu, factor_in, go, uo, *held)
+    )(at, rows, wg, wu, go, uo, *[array for array, _ in factors])
 
 
 def hidden_kernel(
-    g_ref, wd_ref, out_ref, di_ref, go_ref, uo_ref, a_ref, b_ref, h_ref,
-    gg_ref, ug_ref, proj_ref, low_ref, sum_ref,
+    far, at_ref, g_ref, wd_ref, di_ref, go_ref, uo_ref, a_ref, b_ref, h_ref, *rest
 ):
-    g = g_ref[0]
+    *factor_refs, gg_ref, ug_ref, proj_ref, low_ref, sum_ref = rest
+    rank = di_ref.shape[1]
     first = pl.program_id(1) == 0
 
     @pl.when(first)
     def _():
-        low_ref[0] = mm(g, out_ref[0], NT).astype(BF16)
-
-    hg = mm(g, wd_ref[0], NT) + adapter_scale * mm(low_ref[0], di_ref[0])
+        low_ref[0] = low_rank(g_ref, at_ref, far, factor_refs, slice(2 * rank, 3 * rank))
+
+    hg = mm(g_ref[0], wd_ref[0], NT) + adapter_scale * mm(low_ref[0], di_ref[0])
     gg = (hg * a_ref[0].astype(F32)).astype(BF16)
     ug = (hg * b_ref[0].astype(F32)).astype(BF16)
     gg_ref[0] = gg
@@ -163,65 +186,68 @@
     proj_ref[0] = total.astype(BF16)
 
 
-def hidden_back(rows, wd, factor_out, di, go, uo, a, b, h):
+def hidden_back(at, rows, wd, di, go, uo, a, b, h, factors, far):
     count, n, width = rows.shape
     units = wd.shape[1]
     rank = di.shape[1]
     ft = min(1024, units)
-    wide = pl.BlockSpec((1, n, ft), lambda l, f: (l, 0, f))
-    factor = pl.BlockSpec((1, rank, ft), lambda l, f: (l, 0, f))
-    one = lambda *shape: pl.BlockSpec((1,) + shape, lambda l, f: (l, 0, 0))
+    wide = pl.BlockSpec((1, n, ft), lambda l, f, p: (l, 0, f))
+    factor = pl.BlockSpec((1, rank, ft), lambda l, f, p: (l, 0, f))
+    one = lambda *shape: pl.BlockSpec((1,) + shape, lambda l, f, p: (l, 0, 0))
     out = jax.ShapeDtypeStruct((count, n, units), BF16)
     return pl.pallas_call(
-        hidden_kernel,
-        grid=(count, units // ft),
-        in_specs=[
-            one(n, width),
-            pl.BlockSpec((1, ft, width), lambda l, f: (l, f, 0)),
-            one(rank, width),
-            factor,
-            factor,
-            factor,
-            wide,
-            wide,
-            wide,
-        ],
-        out_specs=[wide, wide, one(n, 3 * rank), one(n, rank)],
+        functools.partial(hidden_kernel, far),
+        grid_spec=pltpu.PrefetchScalarGridSpec(
+            num_scalar_prefetch=1,
+            grid=(count, units // ft),
+            in_specs=[
+                one(n, width),
+                pl.BlockSpec((1, ft, width), lambda l, f, p: (l, f, 0)),
+                factor,
+                factor,
+                factor,
+                wide,
+                wide,
+                wide,
+            ]
+            + factor_specs(factors),
+            out_specs=[wide, wide, one(n, 3 * rank), one(n, rank)],
+            scratch_shapes=[pltpu.VMEM((n, 3 * rank), F32)],
+        ),
         out_shape=[
             out,
             out,
             jax.ShapeDtypeStruct((count, n, 3 * rank), BF16),
             jax.ShapeDtypeStruct((count, n, rank), BF16),
         ],
-        scratch_shapes=[pltpu.VMEM((n, 3 * rank), F32)],
         compiler_params=params(("arbitrary", "arbitrary")),
         cost_estimate=COST,
         name="hidden_back",
-    )(rows, wd, factor_out, di, go, uo, a, b, h)
-
-
-def adapter_kernel(lowt_ref, gg_ref, ug_ref, h_ref, ggo_ref, guo_ref, gdi_ref):
+    )(at, rows, wd, di, go, uo, a, b, h, *[array for array, _ in factors])
+
+
+def adapter_kernel(low_x_ref, low_g_ref, gg_ref, ug_ref, h_ref, ggo_ref, guo_ref, gdi_ref):
     rank = ggo_ref.shape[1]
-    lowt = lowt_ref[0]
-    ggo_ref[0] = adapter_scale * mm(lowt[:rank], gg_ref[0])
-    guo_ref[0] = adapter_scale * mm(lowt[rank : 2 * rank], ug_ref[0])
-    gdi_ref[0] = adapter_scale * mm(lowt[2 * rank :], h_ref[0])
-
-
-def adapter_back(lowt, gg, ug, h, wait=()):
+    low = low_x_ref[0]
+    ggo_ref[0] = adapter_scale * mm(low[:, :rank], gg_ref[0], TN)
+    guo_ref[0] = adapter_scale * mm(low[:, rank:], ug_ref[0], TN)
+    gdi_ref[0] = adapter_scale * mm(low_g_ref[0], h_ref[0], TN)
+
+
+def adapter_back(low_x, low_g, gg, ug, h, wait=()):
     count, n, units = gg.shape
-    rank = lowt.shape[1] // 3
+    rank = low_g.shape[2]
     one = lambda *shape: pl.BlockSpec((1,) + shape, lambda l: (l, 0, 0))
     return pl.pallas_call(
-        without(adapter_kernel, 4, len(wait)),
+        without(adapter_kernel, 5, len(wait)),
         grid=(count,),
-        in_specs=[one(3 * rank, n)] + [one(n, units)] * 3 + [ANY for _ in wait],
+        in_specs=[one(n, 2 * rank), one(n, rank)] + [one(n, units)] * 3 + [ANY for _ in wait],
         out_specs=[one(rank, units)] * 3,
         out_shape=[jax.ShapeDtypeStruct((count, rank, units), F32)] * 3,
         compiler_params=params(("arbitrary",)),
         cost_estimate=COST,
         name="adapter_back",
-    )(lowt, gg, ug, h, *wait)
+    )(low_x, low_g, gg, ug, h, *wait)
 
 
 def rows_kernel(at_ref, gg_ref, ug_ref, wg_ref, wu_ref, back_ref, proj_ref, in_ref, *rest):
@@ -230,9 +256,9 @@
     l = pl.program_id(1)
     tiles = len(out_refs) // 2
     count = pl.num_programs(1)
-    rank2 = in_ref.shape[1]
+    rank2 = in_ref.shape[2] // 3 * 2
     y = mm(gg_ref[l], wg_ref[0], NT) + mm(ug_ref[l], wu_ref[0], NT)
-    y = y + adapter_scale * mm(proj_ref[l][:, :rank2], in_ref[0])
+    y = y + adapter_scale * mm(proj_ref[l][:, :rank2], in_ref[0, 0, :rank2])
     groups, tokens, _ = back_ref.shape
     y_ref[l] = y.astype(BF16).reshape(groups, SLOT, -1)
 
@@ -248,7 +274,7 @@
         )
 
 
-def row_back(at, gg, ug, wg, wu, back, proj, factor_in, dt, wait=()):
+def row_back(at, gg, ug, wg, wu, back, proj, factors, order, dt, wait=()):
     count, n, units = gg.shape
     groups, tokens, _ = back.shape
     tiles = at.shape[0]
@@ -267,7 +293,9 @@
                 weight,
                 whole(*back.shape),
                 whole(*proj.shape),
-                pl.BlockSpec((1, factor_in.shape[1], dt), lambda d, l, p: (l, 0, p[d])),
+                pl.BlockSpec(
+                    (1, 1, factors.shape[2], dt), lambda d, l, p: (order(d)[0], l, 0, order(d)[1])
+                ),
             ]
             + [ANY for _ in wait],
             out_specs=[whole(half, dt)] * (2 * tiles),
@@ -277,7 +305,7 @@
         compiler_params=params(("arbitrary", "arbitrary")),
         cost_estimate=COST,
         name="row_back",
-    )(at, gg, ug, wg, wu, back, proj, factor_in, *wait)
+    )(at, gg, ug, wg, wu, back, proj, factors, *wait)
 
 
 def slots_of(experts):
@@ -364,39 +392,41 @@
         def over_cuts(x, k):
             return swap(x, k, "cuts")
 
+        x2 = over_cuts(inputs[None], 2)
         own = jnp.concatenate([inputs, written(experts, routes, route_gates, col)])[None]
-        x2 = over_cuts(inputs[None], 2)
         own_over = other_chip(own)
+        x2 = tie(x2, own_over)
         own_cross, own_both = other_core(own), other_core(own_over)
-        first = [own, own_over, own_cross, own_both]
-        routes = jnp.concatenate([read(x[0, tokens:], tokens) for x in first])
-        place, back, gate = routing(routes, me, count)
         x13 = over_cuts(jnp.concatenate([inputs[None], x2]), 1)
         g2 = over_cuts(tie(out_grad, x2)[None], 2)
-        x2_over = other_chip(x2)
-        x2_cross = other_core(x2)
+        x2_over, x2_cross = other_chip(x2), other_core(x2)
+        routes = jnp.concatenate(
+            [read(x[0, tokens:], tokens) for x in (own, own_over, own_cross, own_both)]
+        )
+        place, back, gate = routing(routes, me, count)
         x13 = tie(x13, g2, x2_over)
+        x2_both = other_core(x2_over)
         g02 = jnp.concatenate([out_grad[None], g2])
         g13 = over_cuts(g02, 1)
         far_factors = over_cuts(tie(factors, x13)[None], 2)
         x13_over, x13_cross = other_chip(x13), other_core(x13)
-        x13_over = tie(x13_over, g13, far_factors, x13_cross)
-        x2_both, x13_both = other_core(x2_over), other_core(x13_over)
+        x13_over = tie(x13_over, g13, far_factors, x13_cross, place, back, gate)
+        x13_both = other_core(x13_over)
         f02 = jnp.concatenate([factors[None], far_factors])
         f13 = over_cuts(f02, 1)
-        all_factors = jnp.concatenate([f02, f13])
-        near = jnp.array([0, 2, 1, 3], jnp.int32)
-        all_factors = jnp.take(all_factors, near[cut ^ jnp.arange(cuts)], axis=0)
-        all_factors = jnp.moveaxis(all_factors, 0, 2).reshape(count, 3 * rank, width)
+        far = (0, 2, 1, 3)
+        all_factors = [(f02, 0), (f02, 1), (f13, 0), (f13, 1)]
         at = jnp.reshape(cut, (1,)).astype(jnp.int32)
-        pieces = [(x, 0) for x in first]
+        pieces = [(x, 0) for x in (own, own_over, own_cross, own_both)]
         pieces += [(x, 0) for x in (x2, x2_over, x2_cross, x2_both)]
         pieces += [(x, 0) for x in (x13, x13_over, x13_cross, x13_both)]
         pieces += [(x, 1) for x in (x13, x13_over, x13_cross, x13_both)]
-        rows_x = place_rows(at, place, pieces, (0, 2, 1, 3), count)
+        rows_x = place_rows(at, place, pieces, far, count)
     else:
         place, back, gate = routing(lax.all_gather(routes, "expert"), me, count)
-        all_factors = lax.all_gather(factors, "cuts", axis=2, tiled=True)
+        every_factor = lax.all_gather(factors, "cuts", axis=2, tiled=True)[None]
+        far, all_factors = (0,), [(every_factor, 0)]
+        at = jnp.zeros((1,), jnp.int32)
 
         def collect(x, gate=None):
             x = lax.all_gather(x, "expert")
@@ -409,9 +439,8 @@
 
         rows_x = collect(inputs)
 
-    factors_in = all_factors[:, : 2 * rank]
     a, b, h, low_x = forward(
-        0, count, rows_x, gate_proj, up_proj, factors_in, gate_out, up_out
+        at, rows_x, gate_proj, up_proj, gate_out, up_out, all_factors, far
     )
     if paired:
         pieces = []
@@ -420,70 +449,75 @@
             over = tie(over, h, cross)
             both = other_core(over)
             pieces += [(y, i) for i in range(2) for y in (x, over, cross, both)]
-        rows_g = place_rows(at, place, pieces, (0, 2, 1, 3), count, gate)
+        rows_g = place_rows(at, place, pieces, far, count, gate)
     else:
         rows_g = collect(out_grad, gate)
     gg, ug, proj, low_g = hidden_back(
-        rows_g, down_proj, all_factors[:, 2 * rank :], down_in, gate_out, up_out, a, b, h
+        at, rows_g, down_proj, down_in, gate_out, up_out, a, b, h, all_factors, far
     )
-    lowt = jnp.swapaxes(jnp.concatenate([low_x, low_g], axis=2), 1, 2)
+    own_x = lax.dynamic_slice(rows_x, (0, 0, cut * col), (count, n, col))
+    own_g = lax.dynamic_slice(rows_g, (0, 0, cut * col), (count, n, col))
+
+    def factor_grads(proj):
+        grad_x = adapter_scale * jnp.einsum(
+            "lnr,lnd->lrd", proj[:, :, : 2 * rank], own_x, preferred_element_type=F32
+        )
+        grad_g = adapter_scale * jnp.einsum(
+            "lnr,lnd->lrd", proj[:, :, 2 * rank :], own_g, preferred_element_type=F32
+        )
+        return grad_x, grad_g
 
     if paired:
-        def chunks(first, second, wait=()):
+        def chunks(far, held, pieces, wait=()):
             return row_back(
-                jnp.stack([cut ^ first, cut ^ second]).astype(jnp.int32),
-                gg, ug, gate_proj, up_proj, back, proj, factors_in, col, wait,
+                jnp.stack([cut ^ k for k in far]).astype(jnp.int32),
+                gg, ug, gate_proj, up_proj, back, proj, held, pieces, col, wait,
             )
 
         def to_chip(keep, send):
             total = keep.astype(F32) + other_core(send).astype(F32)
             return total[:tokens], total[tokens:].astype(BF16)
 
-        keep3, send3, keep1, send1 = chunks(3, 1)
-        half3, send3 = to_chip(keep3, send3)
-        half1, send1 = to_chip(keep1, send1)
-        keep2, send2, keep0, send0 = chunks(2, 0, [send3, send1])
+        near_rows = swap(proj, 1, "cuts")
+        keep3, send3, keep1, send1 = chunks((3, 1), f13, lambda d: (1 - d, 0))
+        half3, send3 = to_chip(keep3, tie(send3, near_rows))
+        half1, send1 = to_chip(keep1, tie(send1, near_rows))
+        rows = proj.astype(F32) + near_rows.astype(F32)
+        sent = rows.astype(BF16)
+        keep2, send2 = chunks((2,), f02, lambda d: (1, 0), [send3, send1, sent])
         over3 = tie(other_chip(send3), keep2)
         over1 = tie(other_chip(send1), keep2)
-        half2, send2 = to_chip(keep2, tie(send2, over3, over1))
-        half0, send0 = to_chip(keep0, send0)
-        rows = proj.reshape(-1, col)
-        near = swap(
-            jnp.concatenate(
-                [(half1 + over1.astype(F32)).astype(BF16), (half3 + over3.astype(F32)).astype(BF16), rows]
-            ),
-            1,
-            "cuts",
-        )
-        grads = adapter_back(lowt, gg, ug, h, [send2, send0])
-        over2 = tie(other_chip(send2), near, grads[0])
-        over0 = other_chip(send0)
+        far_rows = swap(sent, 2, "cuts")
+        half2, send2 = to_chip(keep2, tie(send2, over3, over1, far_rows))
+        proj_all = (rows + far_rows.astype(F32)).astype(BF16)
+        near = jnp.concatenate(
+            [(half1 + over1.astype(F32)).astype(BF16), (half3 + over3.astype(F32)).astype(BF16)]
+        )
+        keep0, send0 = chunks((0,), f02, lambda d: (0, 0), [send2, near])
+        near = tie(swap(near, 1, "cuts"), keep0)
+        over2 = tie(other_chip(send2), keep0)
+        half0, send0 = to_chip(keep0, tie(send0, near, over2))
         near = near.astype(F32)
-        rows = rows.astype(F32) + near[2 * tokens :]
-        sum2 = half2 + over2.astype(F32) + near[tokens : 2 * tokens]
-        far = swap(jnp.concatenate([sum2.astype(BF16), rows.astype(BF16)]), 2, "cuts").astype(F32)
-        input_grad = (half0 + over0.astype(F32) + near[:tokens] + far[:tokens]).astype(BF16)
-        proj = (rows + far[tokens:]).astype(BF16).reshape(proj.shape)
+        sum2 = (half2 + over2.astype(F32) + near[tokens:]).astype(BF16)
+        grads = adapter_back(low_x, low_g, gg, ug, h, [send0, sum2])
+        grad_x, grad_down_out = factor_grads(tie(proj_all, sum2))
+        far = tie(swap(sum2, 2, "cuts"), grads[0], grad_x, grad_down_out).astype(F32)
+        over0 = other_chip(send0).astype(F32)
+        input_grad = (half0 + over0 + near[:tokens] + far).astype(BF16)
     else:
-        grads = adapter_back(lowt, gg, ug, h)
+        grads = adapter_back(low_x, low_g, gg, ug, h)
         dt = 768 if width % 768 == 0 else width
         at = jnp.arange(width // dt, dtype=jnp.int32)
-        chunks = row_back(at, gg, ug, gate_proj, up_proj, back, proj, factors_in, dt)
+        chunks = row_back(
+            at, gg, ug, gate_proj, up_proj, back, proj, every_factor, lambda d: (0, d), dt
+        )
         partial = jnp.concatenate(
             [jnp.concatenate(chunks[i : i + 2]) for i in range(0, len(chunks), 2)], axis=1
         )
         partial = lax.psum_scatter(partial, "expert", scatter_dimension=0, tiled=True)
         input_grad = lax.psum_scatter(partial, "cuts", scatter_dimension=1, tiled=True)
-        proj = lax.psum(proj.astype(F32), "cuts").astype(BF16)
-
-    own_x = lax.dynamic_slice(rows_x, (0, 0, cut * col), (count, n, col))
-    own_g = lax.dynamic_slice(rows_g, (0, 0, cut * col), (count, n, col))
-    grad_x = adapter_scale * jnp.einsum(
-        "lnr,lnd->lrd", proj[:, :, : 2 * rank], own_x, preferred_element_type=F32
-    )
-    grad_down_out = adapter_scale * jnp.einsum(
-        "lnr,lnd->lrd", proj[:, :, 2 * rank :], own_g, preferred_element_type=F32
-    )
+        grad_x, grad_down_out = factor_grads(lax.psum(proj.astype(F32), "cuts").astype(BF16))
+
     return (
         input_grad,
         grad_x[:, :rank],

time: 231 us -> 215 us (0.931)
  waiting for transfers between devices: 62.9 us -> 50.7 us
  other arithmetic: 19.8 us -> 13.2 us
  local copies, waits for them, and re-layouts: 27.5 us -> 21.7 us
  starting transfers between devices: 23.3 us -> 28.6 us
  Pallas kernels: 91.8 us -> 94.8 us
    ppermute x31 -> x33, waiting for transfers between devices: 62.9 us -> 50.7 us  [swap(): return lax.ppermute(x, axis, [(i, i ^ k) for i in range(n)])]
    ppermute x31 -> x33, starting transfers between devices: 23.3 us -> 28.6 us  [swap(): return lax.ppermute(x, axis, [(i, i ^ k) for i in range(n)])]
    pallas_call x2 -> x3, Pallas kernels: 33.5 us -> 37.5 us  [row_back(): pl.pallas_call(without(rows_kernel, 8, len(wait)), grid_spec=pltpu.Prefet...]
    unnamed x99 -> x125, local copies, waits for them, and re-layouts: 15 us -> 17.5 us
  transfers between devices with their start and end apart: 31 -> 33, of which waited for: 9 -> 14; matrix products, arithmetic and copies ran while one was open for 15% -> 8% of each run, Pallas kernels for 23% -> 34%
where the time goes in v3:
time: 215 us; the launch traced here: 214 us
  Pallas kernels  94.8 us (44%)
  waiting for transfers between devices  50.7 us (24%)
  starting transfers between devices  28.6 us (13%)
  local copies, waits for them, and re-layouts  21.7 us (10%)
  other arithmetic  13.2 us (6%)
  matrix products  3.79 us (2%)
    ppermute x33, waiting for transfers between devices, swap(): return lax.ppermute(x, axis, [(i, i ^ k) for i in range(n)])  50.7 us
    pallas_call x3, Pallas kernels, row_back(): pl.pallas_call(without(rows_kernel, 8, len(wait)), grid_spec=pltpu.Prefet...  37.5 us
    ppermute x33, starting transfers between devices, swap(): return lax.ppermute(x, axis, [(i, i ^ k) for i in range(n)])  28.6 us
    pallas_call x1, Pallas kernels, forward(): pl.pallas_call(functools.partial(forward_kernel, far), grid_spec=pltpu.Pr...  25.6 us
    unnamed x125, local copies, waits for them, and re-layouts  17.5 us
    pallas_call x1, Pallas kernels, hidden_back(): pl.pallas_call(functools.partial(hidden_kernel, far), grid_spec=pltpu.Pre...  17.4 us
    pallas_call x2, Pallas kernels, place_rows(): pl.pallas_call(functools.partial(place_kernel, gate is not None, far), gr...  10.1 us
  transfers between devices with their start and end apart: 33, of which 14 were waited for; matrix products, arithmetic and copies ran while one was open for 8% of the time, Pallas kernels for 34%

profile of v3, /device:TPU:0, one launch (start us, length us, event | category | flops | bytes accessed | tf_op | source)
XLA Modules:
  0.0 214.2 jit_solution(5166406131789909625)
XLA Ops:
  3.9 1.0 maximum_bitcast_fusion.rest_0_
  4.9 3.0 %collective-permute-start = (bf16[1,208,768]{2,1,0:T(8,128)(2,1)S(1)}, bf16[1,208,768]{2,1,0:T(8,128)(2,1)S(1)}, u32[]{:S(2)}, u32[]{:S(2)}) collective-permute-start(bf16[1,208,768]{2,1,0:T(8,128)(2,1)S(1)} %maximum_bitcast_fusion.rest_0_), channel_id=1, source_target_pairs={{0,8},{4,12},{8,0},{12,4},{1,9},{5,13},{9,1},{13,5},{2,10},{6,14},... | collective-permute-start | bytes 958472 | tf_op jit(solution)/shard_map/ppermute | solution.py:32
  7.9 2.6 %collective-permute-start.3 = (bf16[1,192,768]{2,1,0:T(8,128)(2,1)S(1)}, bf16[1,192,768]{2,1,0:T(8,128)(2,1)S(1)}, u32[]{:S(2)}, u32[]{:S(2)}) collective-permute-start(bf16[1,192,768]{2,1,0:T(8,128)(2,1)S(1)} %bitcast.33), channel_id=1, source_target_pairs={{0,2},{1,3},{2,0},{3,1},{4,6},{5,7},{6,4},{7,5},{8,10},{9,11},{10,... | collective-permute-start | bytes 884744 | tf_op jit(solution)/shard_map/ppermute | solution.py:32
  12.7 11.9 %collective-permute-done.3.refs_0_ = bf16[1,192,768]{2,1,0:T(8,128)(2,1)S(1)} collective-permute-done((bf16[1,192,768]{2,1,0:T(8,128)(2,1)S(1)}, bf16[1,192,768]{2,1,0:T(8,128)(2,1)S(1)}, u32[]{:S(2)}, u32[]{:S(2)}) %collective-permute-start.3) | collective-permute-done | bytes 294944 | tf_op jit(solution)/shard_map/ppermute | solution.py:32
  26.5 1.1 pad_maximum_fusion.1
  29.4 4.1 %collective-permute-start.9 = (bf16[2,192,768]{2,1,0:T(8,128)(2,1)S(1)}, bf16[2,192,768]{2,1,0:T(8,128)(2,1)S(1)}, u32[]{:S(2)}, u32[]{:S(2)}) collective-permute-start(bf16[2,192,768]{2,1,0:T(8,128)(2,1)S(1)} %pad_maximum_fusion.1), channel_id=1, source_target_pairs={{0,1},{1,0},{2,3},{3,2},{4,5},{5,4},{6,7},{7,6},{8,9},{9,8},{10,11... | collective-permute-start | bytes 1769480 | tf_op jit(solution)/shard_map/ppermute | solution.py:32
  33.7 11.7 %collective-permute-done.4.refs_1_ = bf16[1,192,768]{2,1,0:T(8,128)(2,1)S(1)} collective-permute-done((bf16[1,192,768]{2,1,0:T(8,128)(2,1)}, bf16[1,192,768]{2,1,0:T(8,128)(2,1)S(1)}, u32[]{:S(2)}, u32[]{:S(2)}) %collective-permute-start.4) | collective-permute-done | bytes 294944 | tf_op jit(solution)/shard_map/ppermute | solution.py:32
  45.6 0.9 copy-done.49
  47.3 5.6 %collective-permute-done.9.refs_0_ = bf16[2,192,768]{2,1,0:T(8,128)(2,1)S(1)} collective-permute-done((bf16[2,192,768]{2,1,0:T(8,128)(2,1)S(1)}, bf16[2,192,768]{2,1,0:T(8,128)(2,1)S(1)}, u32[]{:S(2)}, u32[]{:S(2)}) %collective-permute-start.9) | collective-permute-done | bytes 589856 | tf_op jit(solution)/shard_map/ppermute | solution.py:32
  53.7 1.3 collective-permute-start.10
  55.3 0.8 fusion.10.refs_4_.place_ref
  56.1 0.9 copy.95.refs_6_.rest_0_
  57.0 1.5 collective-permute-start.12
  58.5 0.9 or_convert_fusion.refs_5_
  59.4 5.1 %collective-permute-done.12.refs_2_ = bf16[1,2,48,768]{3,2,1,0:T(8,128)(2,1)S(1)} collective-permute-done((bf16[1,2,48,768]{3,2,1,0:T(8,128)(2,1)}, bf16[1,2,48,768]{3,2,1,0:T(8,128)(2,1)S(1)}, u32[]{:S(2)}, u32[]{:S(2)}) %collective-permute-start.12) | collective-permute-done | bytes 147488 | tf_op jit(solution)/shard_map/ppermute | solution.py:32
  64.6 2.9 %collective-permute-done.11.refs_1_.rest_9_.rest_13_ = bf16[2,192,768]{2,1,0:T(8,128)(2,1)S(1)} collective-permute-done((bf16[2,192,768]{2,1,0:T(8,128)(2,1)S(1)}, bf16[2,192,768]{2,1,0:T(8,128)(2,1)S(1)}, u32[]{:S(2)}, u32[]{:S(2)}) %collective-permute-start.11) | collective-permute-done | bytes 589856 | tf_op jit(solution)/shard_map/ppermute | solution.py:32
  68.6 0.8 copy-done.11
  70.0 1.3 collective-permute-start.5
  71.9 1.4 collective-permute-start.18
  73.3 0.9 pad_maximum_fusion.3.rest_0_.rest_1_.refs_7_
  74.3 1.9 collective-permute-start.15
  76.2 5.0 %place_rows.2.x_ref = bf16[2,256,3072]{2,1,0:T(8,128)(2,1)} custom-call(s32[1]{0:T(128)} %bitcast.at_ref.refs_0_, bf16[4,128,192]{2,1,0:T(8,128)(2,1)} %fusion.10.refs_4_.place_ref, bf16[1,208,768]{2,1,0:T(8,128)(2,1)} %copy-done.31, bf16[1,208,768]{2,1,0:T(8,128)(2,1)} %copy-done.32, bf16[1,208,768]{2,1,0:T(8,128)(2,1)} %copy-done.48, ...), custom_call_target="tpu_custom_call" | custom-call | flops 1 | bytes 1 | tf_op jit(solution)/shard_map/place_rows/pallas_call | solution.py:81
  81.2 2.6 %collective-permute-done.15.rest_2_.rest_3_.refs_7_ = bf16[2,2,48,768]{3,2,1,0:T(8,128)(2,1)S(1)} collective-permute-done((bf16[2,2,48,768]{3,2,1,0:T(8,128)(2,1)S(1)}, bf16[2,2,48,768]{3,2,1,0:T(8,128)(2,1)S(1)}, u32[]{:S(2)}, u32[]{:S(2)}) %collective-permute-start.15) | collective-permute-done | bytes 294944 | tf_op jit(solution)/shard_map/ppermute | solution.py:32
  84.5 25.6 %forward_units.1 = (bf16[2,256,2048]{2,1,0:T(8,128)(2,1)}, bf16[2,256,2048]{2,1,0:T(8,128)(2,1)}, bf16[2,256,2048]{2,1,0:T(8,128)(2,1)}, bf16[2,256,32]{2,1,0:T(8,128)(2,1)}) custom-call(s32[1]{0:T(128)} %bitcast.at_ref.refs_0_, bf16[2,256,3072]{2,1,0:T(8,128)(2,1)} %place_rows.2.x_ref, bf16[2,3072,2048]{2,1,0:T(8,128)(2,1)} %refs_3_.5, ...), custom_call_target="tpu_custom_call" | custom-call | flops 1 | bytes 1 | tf_op jit(solution)/shard_map/forward_units/pallas_call | solution.py:150
  111.0 0.9 copy-done.6
  113.2 1.0 collective-permute-done.20.rest_12_.rest_16_
  115.1 5.1 %place_rows.3.g_ref = bf16[2,256,3072]{2,1,0:T(8,128)(2,1)} custom-call(s32[1]{0:T(128)} %bitcast.at_ref.refs_0_, bf16[4,128,192]{2,1,0:T(8,128)(2,1)} %fusion.10.refs_4_.place_ref, f32[4,128,1]{2,1,0:T(8,128)} %copy.95.refs_6_.rest_0_, bf16[2,192,768]{2,1,0:T(8,128)(2,1)} %copy-done.3, bf16[2,192,768]{2,1,0:T(8,128)(2,1)} %tie.22.rest_2_.rest_6_, ...), custom_call_target="tpu_custom_call" | custom-call | flops 1 | bytes 1 | tf_op jit(solution)/shard_map/place_rows/pallas_call | solution.py:81
  120.2 17.4 %hidden_back.1 = (bf16[2,256,2048]{2,1,0:T(8,128)(2,1)}, bf16[2,256,2048]{2,1,0:T(8,128)(2,1)}, bf16[2,256,48]{2,1,0:T(8,128)(2,1)}, bf16[2,256,16]{2,1,0:T(8,128)(2,1)}) custom-call(s32[1]{0:T(128)} %bitcast.at_ref.refs_0_, bf16[2,256,3072]{2,1,0:T(8,128)(2,1)} %place_rows.3.g_ref, bf16[2,2048,3072]{2,1,0:T(8,128)(2,1)} %wd_ref.1, ...), custom_call_target="tpu_custom_call" | custom-call | flops 1 | bytes 1 | tf_op jit(solution)/shard_map/hidden_back/pallas_call | solution.py:198
  137.6 1.8 collective-permute-start.21
  140.0 16.7 %row_back.3 = (bf16[384,768]{1,0:T(8,128)(2,1)}, bf16[384,768]{1,0:T(8,128)(2,1)}, bf16[384,768]{1,0:T(8,128)(2,1)}, bf16[384,768]{1,0:T(8,128)(2,1)}) custom-call(s32[2]{0:T(128)} %pad_add_fusion.refs_0_, bf16[2,256,2048]{2,1,0:T(8,128)(2,1)} %get-tuple-element.29.refs_1_.refs_2_, bf16[2,256,2048]{2,1,0:T(8,128)(2,1)} %get-tuple-element.30.refs_2_.refs_3_, ...), custom_call_target="tpu_custom_call" | custom-call | flops 1 | bytes 1 | tf_op jit(solution)/shard_map/row_back/pallas_call | solution.py:284
  157.9 1.7 collective-permute-done.22
  161.6 1.2 collective-permute-start.25
  162.8 1.6 collective-permute-start.26
  164.4 10.4 %row_back.4 = (bf16[384,768]{1,0:T(8,128)(2,1)}, bf16[384,768]{1,0:T(8,128)(2,1)}) custom-call(s32[1]{0:T(128)} %bitcast.12.refs_0_, bf16[2,256,2048]{2,1,0:T(8,128)(2,1)} %get-tuple-element.29.refs_1_.refs_2_, bf16[2,256,2048]{2,1,0:T(8,128)(2,1)} %get-tuple-element.30.refs_2_.refs_3_, bf16[2,3072,2048]{2,1,0:T(8,128)(2,1)} %refs_3_.5, ...), custom_call_target="tpu_custom_call" | custom-call | flops 1 | bytes 1 | tf_op jit(solution)/shard_map/row_back/pallas_call | solution.py:284
  176.4 0.9 copy-done.21
  178.8 0.9 collective-permute-start.29
  179.7 10.4 %row_back.5 = (bf16[384,768]{1,0:T(8,128)(2,1)}, bf16[384,768]{1,0:T(8,128)(2,1)}) custom-call(s32[1]{0:T(128)} %bitcast.at_ref.refs_0_, bf16[2,256,2048]{2,1,0:T(8,128)(2,1)} %get-tuple-element.29.refs_1_.refs_2_, bf16[2,256,2048]{2,1,0:T(8,128)(2,1)} %get-tuple-element.30.refs_2_.refs_3_, bf16[2,3072,2048]{2,1,0:T(8,128)(2,1)} %refs_3_.5, ...), custom_call_target="tpu_custom_call" | custom-call | flops 1 | bytes 1 | tf_op jit(solution)/shard_map/row_back/pallas_call | solution.py:284
  190.0 2.3 %collective-permute-done.28.refs_0_ = bf16[384,768]{1,0:T(8,128)(2,1)S(1)} collective-permute-done((bf16[384,768]{1,0:T(8,128)(2,1)S(1)}, bf16[384,768]{1,0:T(8,128)(2,1)S(1)}, u32[]{:S(2)}, u32[]{:S(2)}) %collective-permute-start.28) | collective-permute-done | bytes 589856 | tf_op jit(solution)/shard_map/ppermute | solution.py:32
  192.4 0.8 copy-done.7
  194.9 1.6 add_convert_fusion.refs_0_
  196.7 1.5 collective-permute-start.32
  198.1 1.5 convolution_multiply_fusion.refs_2_
  199.7 1.3 convert_add_fusion
  201.0 0.9 collective-permute-start.31
  201.9 2.1 convolution_multiply_fusion.1.refs_3_
  204.7 4.1 %adapter_back.1 = (f32[2,16,2048]{2,1,0:T(8,128)}, f32[2,16,2048]{2,1,0:T(8,128)}, f32[2,16,2048]{2,1,0:T(8,128)}) custom-call(bf16[2,256,32]{2,1,0:T(8,128)(2,1)} %get-tuple-element.40.refs_0_, bf16[2,256,16]{2,1,0:T(8,128)(2,1)} %get-tuple-element.41.refs_1_, bf16[2,256,2048]{2,1,0:T(8,128)(2,1)} %get-tuple-element.29.refs_1_.refs_2_, ...), custom_call_target="tpu_custom_call" | custom-call | flops 1 | bytes 1 | tf_op jit(solution)/shard_map/adapter_back/pallas_call | solution.py:241
  208.8 3.6 %collective-permute-done.32.refs_0_ = bf16[192,768]{1,0:T(8,128)(2,1)} collective-permute-done((bf16[192,768]{1,0:T(8,128)(2,1)S(1)}, bf16[192,768]{1,0:T(8,128)(2,1)}, u32[]{:S(2)}, u32[]{:S(2)}) %collective-permute-start.32) | collective-permute-done | bytes 294944 | tf_op jit(solution)/shard_map/ppermute | solution.py:32
  212.4 1.8 fusion.5
  (244 shorter events, 26.3 us)
Async XLA Ops:
  0.6 7.3 %copy-start.37 = (bf16[192,768]{1,0:T(8,128)(2,1)S(1)}, bf16[192,768]{1,0:T(8,128)(2,1)}, u32[]{:S(2)}) copy-start(bf16[192,768]{1,0:T(8,128)(2,1)} %param.13) | copy-start | bytes 884740
  2.5 8.6 %copy-start.38 = (bf16[192,768]{1,0:T(8,128)(2,1)S(1)}, bf16[192,768]{1,0:T(8,128)(2,1)}, u32[]{:S(2)}) copy-start(bf16[192,768]{1,0:T(8,128)(2,1)} %param.14) | copy-start | bytes 884740
  3.9 8.0 %copy-start.51 = (bf16[2,16,768]{2,1,0:T(8,128)(2,1)S(1)}, bf16[2,16,768]{2,1,0:T(8,128)(2,1)}, u32[]{:S(2)}) copy-start(bf16[2,16,768]{2,1,0:T(8,128)(2,1)} %param.20) | copy-start | bytes 147460
  3.9 8.0 %copy-start.52 = (bf16[2,16,768]{2,1,0:T(8,128)(2,1)S(1)}, bf16[2,16,768]{2,1,0:T(8,128)(2,1)}, u32[]{:S(2)}) copy-start(bf16[2,16,768]{2,1,0:T(8,128)(2,1)} %param.22) | copy-start | bytes 147460
  4.9 7.8 %copy-start.31 = (bf16[1,208,768]{2,1,0:T(8,128)(2,1)}, bf16[1,208,768]{2,1,0:T(8,128)(2,1)S(1)}, u32[]{:S(2)}) copy-start(bf16[1,208,768]{2,1,0:T(8,128)(2,1)S(1)} %maximum_bitcast_fusion.rest_0_) | copy-start | bytes 958468
  4.9 7.0 %copy-start.53 = (bf16[2,16,768]{2,1,0:T(8,128)(2,1)S(1)}, bf16[2,16,768]{2,1,0:T(8,128)(2,1)}, u32[]{:S(2)}) copy-start(bf16[2,16,768]{2,1,0:T(8,128)(2,1)} %param.25) | copy-start | bytes 147460
  4.9 19.7 %collective-permute-start = (bf16[1,208,768]{2,1,0:T(8,128)(2,1)S(1)}, bf16[1,208,768]{2,1,0:T(8,128)(2,1)S(1)}, u32[]{:S(2)}, u32[]{:S(2)}) collective-permute-start(bf16[1,208,768]{2,1,0:T(8,128)(2,1)S(1)} %maximum_bitcast_fusion.rest_0_), channel_id=1, source_target_pairs={{0,8},{4,12},{8,0},{12,4},{1,9},{5,13},{9,1},{13,5},{2,10},{6,14},... | collective-permute-start | bytes 958472 | tf_op jit(solution)/shard_map/ppermute | solution.py:32
  7.9 19.7 %collective-permute-start.1 = (bf16[1,208,768]{2,1,0:T(8,128)(2,1)S(1)}, bf16[1,208,768]{2,1,0:T(8,128)(2,1)S(1)}, u32[]{:S(2)}, u32[]{:S(2)}) collective-permute-start(bf16[1,208,768]{2,1,0:T(8,128)(2,1)S(1)} %maximum_bitcast_fusion.rest_0_), channel_id=1, source_target_pairs={{0,4},{4,0},{8,12},{12,8},{1,5},{5,1},{9,13},{13,9},{2,6},{6,2},{1... | collective-permute-start | bytes 958472 | tf_op jit(solution)/shard_map/ppermute | solution.py:32
  7.9 16.6 %collective-permute-start.3 = (bf16[1,192,768]{2,1,0:T(8,128)(2,1)S(1)}, bf16[1,192,768]{2,1,0:T(8,128)(2,1)S(1)}, u32[]{:S(2)}, u32[]{:S(2)}) collective-permute-start(bf16[1,192,768]{2,1,0:T(8,128)(2,1)S(1)} %bitcast.33), channel_id=1, source_target_pairs={{0,2},{1,3},{2,0},{3,1},{4,6},{5,7},{6,4},{7,5},{8,10},{9,11},{10,... | collective-permute-start | bytes 884744 | tf_op jit(solution)/shard_map/ppermute | solution.py:32
  11.9 15.6 %copy-start.42 = (bf16[2,48,768]{2,1,0:T(8,128)(2,1)}, bf16[2,48,768]{2,1,0:T(8,128)(2,1)S(1)}, u32[]{:S(2)}) copy-start(bf16[2,48,768]{2,1,0:T(8,128)(2,1)S(1)} %constant_dynamic-update-slice_fusion) | copy-start | bytes 442372
  26.0 21.2 %collective-permute-start.6 = (bf16[1,192,768]{2,1,0:T(8,128)(2,1)}, bf16[1,192,768]{2,1,0:T(8,128)(2,1)S(1)}, u32[]{:S(2)}, u32[]{:S(2)}) collective-permute-start(bf16[1,192,768]{2,1,0:T(8,128)(2,1)} %tie.17.refs_1_.rest_4_), channel_id=1, source_target_pairs={{0,8},{4,12},{8,0},{12,4},{1,9},{5,13},{9,1},{13,5},{2,10},{6,14},... | collective-permute-start | bytes 884744 | tf_op jit(solution)/shard_map/ppermute | solution.py:32
  28.8 4.9 %copy-start.33 = (bf16[1,208,768]{2,1,0:T(8,128)(2,1)S(1)}, bf16[1,208,768]{2,1,0:T(8,128)(2,1)}, u32[]{:S(2)}) copy-start(bf16[1,208,768]{2,1,0:T(8,128)(2,1)} %copy-done.32) | copy-start | bytes 958468
  29.3 16.1 %collective-permute-start.4 = (bf16[1,192,768]{2,1,0:T(8,128)(2,1)}, bf16[1,192,768]{2,1,0:T(8,128)(2,1)S(1)}, u32[]{:S(2)}, u32[]{:S(2)}) collective-permute-start(bf16[1,192,768]{2,1,0:T(8,128)(2,1)} %bitcast.32), channel_id=1, source_target_pairs={{0,2},{1,3},{2,0},{3,1},{4,6},{5,7},{6,4},{7,5},{8,10},{9,11},{10,... | collective-permute-start | bytes 884744 | tf_op jit(solution)/shard_map/ppermute | solution.py:32
  29.4 23.5 %collective-permute-start.9 = (bf16[2,192,768]{2,1,0:T(8,128)(2,1)S(1)}, bf16[2,192,768]{2,1,0:T(8,128)(2,1)S(1)}, u32[]{:S(2)}, u32[]{:S(2)}) collective-permute-start(bf16[2,192,768]{2,1,0:T(8,128)(2,1)S(1)} %pad_maximum_fusion.1), channel_id=1, source_target_pairs={{0,1},{1,0},{2,3},{3,2},{4,5},{5,4},{6,7},{7,6},{8,9},{9,8},{10,11... | collective-permute-start | bytes 1769480 | tf_op jit(solution)/shard_map/ppermute | solution.py:32
  33.7 12.0 %collective-permute-start.2 = (bf16[1,208,768]{2,1,0:T(8,128)(2,1)S(1)}, bf16[1,208,768]{2,1,0:T(8,128)(2,1)S(1)}, u32[]{:S(2)}, u32[]{:S(2)}) collective-permute-start(bf16[1,208,768]{2,1,0:T(8,128)(2,1)S(1)} %copy-done.33), channel_id=1, source_target_pairs={{0,4},{4,0},{8,12},{12,8},{1,5},{5,1},{9,13},{13,9},{2,6},{6,2},{1... | collective-permute-start | bytes 958472 | tf_op jit(solution)/shard_map/ppermute | solution.py:32
  45.5 25.8 %copy-start.3 = (bf16[2,192,768]{2,1,0:T(8,128)(2,1)}, bf16[2,192,768]{2,1,0:T(8,128)(2,1)S(1)}, u32[]{:S(2)}) copy-start(bf16[2,192,768]{2,1,0:T(8,128)(2,1)S(1)} %pad_maximum_fusion.rest_1_.rest_5_) | copy-start | bytes 1769476
  45.5 22.0 %collective-permute-start.11 = (bf16[2,192,768]{2,1,0:T(8,128)(2,1)S(1)}, bf16[2,192,768]{2,1,0:T(8,128)(2,1)S(1)}, u32[]{:S(2)}, u32[]{:S(2)}) collective-permute-start(bf16[2,192,768]{2,1,0:T(8,128)(2,1)S(1)} %pad_maximum_fusion.rest_1_.rest_5_), channel_id=1, source_target_pairs={{0,1},{1,0},{2,3},{3,2},{4,5},{5,4},{6,7},{7,6},{8,9},{9,8},{10,11... | collective-permute-start | bytes 1769480 | tf_op jit(solution)/shard_map/ppermute | solution.py:32
  47.3 5.6 %copy-start.39 = (bf16[1,192,768]{2,1,0:T(8,128)(2,1)}, bf16[1,192,768]{2,1,0:T(8,128)(2,1)S(1)}, u32[]{:S(2)}) copy-start(bf16[1,192,768]{2,1,0:T(8,128)(2,1)S(1)} %collective-permute-done.6.refs_2_.rest_5_) | copy-start | bytes 884740
  53.7 13.8 %collective-permute-start.10 = (bf16[2,192,768]{2,1,0:T(8,128)(2,1)}, bf16[2,192,768]{2,1,0:T(8,128)(2,1)S(1)}, u32[]{:S(2)}, u32[]{:S(2)}) collective-permute-start(bf16[2,192,768]{2,1,0:T(8,128)(2,1)} %tie.19.refs_1_.rest_8_.rest_12_), channel_id=1, source_target_pairs={{0,8},{4,12},{8,0},{12,4},{1,9},{5,13},{9,1},{13,5},{2,10},{6,14},... | collective-permute-start | bytes 1769480 | tf_op jit(solution)/shard_map/ppermute | solution.py:32
  55.0 12.5 %collective-permute-start.13 = (bf16[2,192,768]{2,1,0:T(8,128)(2,1)}, bf16[2,192,768]{2,1,0:T(8,128)(2,1)S(1)}, u32[]{:S(2)}, u32[]{:S(2)}) collective-permute-start(bf16[2,192,768]{2,1,0:T(8,128)(2,1)} %tie.19.refs_1_.rest_8_.rest_12_), channel_id=1, source_target_pairs={{0,4},{4,0},{8,12},{12,8},{1,5},{5,1},{9,13},{13,9},{2,6},{6,2},{1... | collective-permute-start | bytes 1769480 | tf_op jit(solution)/shard_map/ppermute | solution.py:32
  57.0 7.6 %collective-permute-start.12 = (bf16[1,2,48,768]{3,2,1,0:T(8,128)(2,1)}, bf16[1,2,48,768]{3,2,1,0:T(8,128)(2,1)S(1)}, u32[]{:S(2)}, u32[]{:S(2)}) collective-permute-start(bf16[1,2,48,768]{3,2,1,0:T(8,128)(2,1)} %bitcast.37), channel_id=1, source_target_pairs={{0,2},{1,3},{2,0},{3,1},{4,6},{5,7},{6,4},{7,5},{8,10},{9,11},{10,... | collective-permute-start | bytes 442376 | tf_op jit(solution)/shard_map/ppermute | solution.py:32
  59.4 10.0 %copy-start.14 = (bf16[1,192,768]{2,1,0:T(8,128)(2,1)S(1)}, bf16[1,192,768]{2,1,0:T(8,128)(2,1)}, u32[]{:S(2)}) copy-start(bf16[1,192,768]{2,1,0:T(8,128)(2,1)} %tie.17.refs_1_.rest_4_) | copy-start | bytes 884740
  59.4 10.5 %copy-start.40 = (bf16[1,192,768]{2,1,0:T(8,128)(2,1)S(1)}, bf16[1,192,768]{2,1,0:T(8,128)(2,1)}, u32[]{:S(2)}) copy-start(bf16[1,192,768]{2,1,0:T(8,128)(2,1)} %copy-done.39) | copy-start | bytes 884740
  59.4 13.9 %copy-start.43 = (bf16[2,48,768]{2,1,0:T(8,128)(2,1)S(1)}, bf16[2,48,768]{2,1,0:T(8,128)(2,1)}, u32[]{:S(2)}) copy-start(bf16[2,48,768]{2,1,0:T(8,128)(2,1)} %copy-done.42) | copy-start | bytes 442372
  69.4 4.9 %collective-permute-start.14 = (bf16[2,192,768]{2,1,0:T(8,128)(2,1)}, bf16[2,192,768]{2,1,0:T(8,128)(2,1)}, u32[]{:S(2)}, u32[]{:S(2)}) collective-permute-start(bf16[2,192,768]{2,1,0:T(8,128)(2,1)} %tie.21.rest_9_.rest_13_), channel_id=1, source_target_pairs={{0,4},{4,0},{8,12},{12,8},{1,5},{5,1},{9,13},{13,9},{2,6},{6,2},{1... | collective-permute-start | bytes 1769480 | tf_op jit(solution)/shard_map/ppermute | solution.py:32
  69.4 2.5 %collective-permute-start.7 = (bf16[1,192,768]{2,1,0:T(8,128)(2,1)S(1)}, bf16[1,192,768]{2,1,0:T(8,128)(2,1)S(1)}, u32[]{:S(2)}, u32[]{:S(2)}) collective-permute-start(bf16[1,192,768]{2,1,0:T(8,128)(2,1)S(1)} %copy-done.14), channel_id=1, source_target_pairs={{0,4},{4,0},{8,12},{12,8},{1,5},{5,1},{9,13},{13,9},{2,6},{6,2},{1... | collective-permute-start | bytes 884744 | tf_op jit(solution)/shard_map/ppermute | solution.py:32
  69.9 3.3 %collective-permute-start.8 = (bf16[1,192,768]{2,1,0:T(8,128)(2,1)S(1)}, bf16[1,192,768]{2,1,0:T(8,128)(2,1)}, u32[]{:S(2)}, u32[]{:S(2)}) collective-permute-start(bf16[1,192,768]{2,1,0:T(8,128)(2,1)S(1)} %copy-done.40), channel_id=1, source_target_pairs={{0,4},{4,0},{8,12},{12,8},{1,5},{5,1},{9,13},{13,9},{2,6},{6,2},{1... | collective-permute-start | bytes 884744 | tf_op jit(solution)/shard_map/ppermute | solution.py:32
  70.0 40.2 %collective-permute-start.5 = (bf16[2,192,768]{2,1,0:T(8,128)(2,1)S(1)}, bf16[2,192,768]{2,1,0:T(8,128)(2,1)}, u32[]{:S(2)}, u32[]{:S(2)}) collective-permute-start(bf16[2,192,768]{2,1,0:T(8,128)(2,1)S(1)} %pad_maximum_fusion.rest_1_.rest_5_), channel_id=1, source_target_pairs={{0,8},{4,12},{8,0},{12,4},{1,9},{5,13},{9,1},{13,5},{2,10},{6,14},... | collective-permute-start | bytes 1769480 | tf_op jit(solution)/shard_map/ppermute | solution.py:32
  71.3 38.8 %collective-permute-start.16 = (bf16[2,192,768]{2,1,0:T(8,128)(2,1)S(1)}, bf16[2,192,768]{2,1,0:T(8,128)(2,1)S(1)}, u32[]{:S(2)}, u32[]{:S(2)}) collective-permute-start(bf16[2,192,768]{2,1,0:T(8,128)(2,1)S(1)} %pad_maximum_fusion.rest_1_.rest_5_), channel_id=1, source_target_pairs={{0,4},{4,0},{8,12},{12,8},{1,5},{5,1},{9,13},{13,9},{2,6},{6,2},{1... | collective-permute-start | bytes 1769480 | tf_op jit(solution)/shard_map/ppermute | solution.py:32
  71.9 39.1 %collective-permute-start.18 = (bf16[2,192,768]{2,1,0:T(8,128)(2,1)}, bf16[2,192,768]{2,1,0:T(8,128)(2,1)}, u32[]{:S(2)}, u32[]{:S(2)}) collective-permute-start(bf16[2,192,768]{2,1,0:T(8,128)(2,1)} %copy-done.4), channel_id=1, source_target_pairs={{0,8},{4,12},{8,0},{12,4},{1,9},{5,13},{9,1},{13,5},{2,10},{6,14},... | collective-permute-start | bytes 1769480 | tf_op jit(solution)/shard_map/ppermute | solution.py:32
  73.2 37.8 %collective-permute-start.19 = (bf16[2,192,768]{2,1,0:T(8,128)(2,1)}, bf16[2,192,768]{2,1,0:T(8,128)(2,1)S(1)}, u32[]{:S(2)}, u32[]{:S(2)}) collective-permute-start(bf16[2,192,768]{2,1,0:T(8,128)(2,1)} %copy-done.4), channel_id=1, source_target_pairs={{0,4},{4,0},{8,12},{12,8},{1,5},{5,1},{9,13},{13,9},{2,6},{6,2},{1... | collective-permute-start | bytes 1769480 | tf_op jit(solution)/shard_map/ppermute | solution.py:32
  74.3 6.9 %copy-start = (bf16[2,2,48,768]{3,2,1,0:T(8,128)(2,1)}, bf16[2,2,48,768]{3,2,1,0:T(8,128)(2,1)S(1)}, u32[]{:S(2)}) copy-start(bf16[2,2,48,768]{3,2,1,0:T(8,128)(2,1)S(1)} %pad_maximum_fusion.3.rest_0_.rest_1_.refs_7_) | copy-start | bytes 884740
  74.3 9.5 %collective-permute-start.15 = (bf16[2,2,48,768]{3,2,1,0:T(8,128)(2,1)S(1)}, bf16[2,2,48,768]{3,2,1,0:T(8,128)(2,1)S(1)}, u32[]{:S(2)}, u32[]{:S(2)}) collective-permute-start(bf16[2,2,48,768]{3,2,1,0:T(8,128)(2,1)S(1)} %pad_maximum_fusion.3.rest_0_.rest_1_.refs_7_), channel_id=1, source_target_pairs={{0,1},{1,0},{2,3},{3,2},{4,5},{5,4},{6,7},{7,6},{8,9},{9,8},{10,11... | collective-permute-start | bytes 884744 | tf_op jit(solution)/shard_map/ppermute | solution.py:32
  111.0 2.2 %collective-permute-start.17 = (bf16[2,192,768]{2,1,0:T(8,128)(2,1)}, bf16[2,192,768]{2,1,0:T(8,128)(2,1)S(1)}, u32[]{:S(2)}, u32[]{:S(2)}) collective-permute-start(bf16[2,192,768]{2,1,0:T(8,128)(2,1)} %tie.22.rest_2_.rest_6_), channel_id=1, source_target_pairs={{0,4},{4,0},{8,12},{12,8},{1,5},{5,1},{9,13},{13,9},{2,6},{6,2},{1... | collective-permute-start | bytes 1769480 | tf_op jit(solution)/shard_map/ppermute | solution.py:32
  111.9 2.3 %collective-permute-start.20 = (bf16[2,192,768]{2,1,0:T(8,128)(2,1)}, bf16[2,192,768]{2,1,0:T(8,128)(2,1)S(1)}, u32[]{:S(2)}, u32[]{:S(2)}) collective-permute-start(bf16[2,192,768]{2,1,0:T(8,128)(2,1)} %tie.23.rest_10_.rest_14_), channel_id=1, source_target_pairs={{0,4},{4,0},{8,12},{12,8},{1,5},{5,1},{9,13},{13,9},{2,6},{6,2},{1... | collective-permute-start | bytes 1769480 | tf_op jit(solution)/shard_map/ppermute | solution.py:32
  137.6 19.1 %collective-permute-start.21 = (bf16[2,256,48]{2,1,0:T(8,128)(2,1)}, bf16[2,256,48]{2,1,0:T(8,128)(2,1)S(1)}, u32[]{:S(2)}, u32[]{:S(2)}) collective-permute-start(bf16[2,256,48]{2,1,0:T(8,128)(2,1)} %get-tuple-element.31.refs_6_), channel_id=1, source_target_pairs={{0,1},{1,0},{2,3},{3,2},{4,5},{5,4},{6,7},{7,6},{8,9},{9,8},{10,11... | collective-permute-start | bytes 147464 | tf_op jit(solution)/shard_map/ppermute | solution.py:32
  157.4 2.2 %collective-permute-start.22 = (bf16[384,768]{1,0:T(8,128)(2,1)}, bf16[384,768]{1,0:T(8,128)(2,1)S(1)}, u32[]{:S(2)}, u32[]{:S(2)}) collective-permute-start(bf16[384,768]{1,0:T(8,128)(2,1)} %tie.24), channel_id=1, source_target_pairs={{0,4},{4,0},{8,12},{12,8},{1,5},{5,1},{9,13},{13,9},{2,6},{6,2},{1... | collective-permute-start | bytes 1769480 | tf_op jit(solution)/shard_map/ppermute | solution.py:32
  157.4 3.0 %collective-permute-start.23 = (bf16[384,768]{1,0:T(8,128)(2,1)}, bf16[384,768]{1,0:T(8,128)(2,1)S(1)}, u32[]{:S(2)}, u32[]{:S(2)}) collective-permute-start(bf16[384,768]{1,0:T(8,128)(2,1)} %tie.25), channel_id=1, source_target_pairs={{0,4},{4,0},{8,12},{12,8},{1,5},{5,1},{9,13},{13,9},{2,6},{6,2},{1... | collective-permute-start | bytes 1769480 | tf_op jit(solution)/shard_map/ppermute | solution.py:32
  159.8 15.1 %collective-permute-start.24 = (bf16[192,768]{1,0:T(8,128)(2,1)S(1)}, bf16[192,768]{1,0:T(8,128)(2,1)S(1)}, u32[]{:S(2)}, u32[]{:S(2)}) collective-permute-start(bf16[192,768]{1,0:T(8,128)(2,1)S(1)} %slice.291.refs_8_), channel_id=1, source_target_pairs={{0,8},{4,12},{8,0},{12,4},{1,9},{5,13},{9,1},{13,5},{2,10},{6,14},... | collective-permute-start | bytes 884744 | tf_op jit(solution)/shard_map/ppermute | solution.py:32
  161.6 14.0 %collective-permute-start.25 = (bf16[192,768]{1,0:T(8,128)(2,1)}, bf16[192,768]{1,0:T(8,128)(2,1)S(1)}, u32[]{:S(2)}, u32[]{:S(2)}) collective-permute-start(bf16[192,768]{1,0:T(8,128)(2,1)} %slice.290.refs_9_), channel_id=1, source_target_pairs={{0,8},{4,12},{8,0},{12,4},{1,9},{5,13},{9,1},{13,5},{2,10},{6,14},... | collective-permute-start | bytes 884744 | tf_op jit(solution)/shard_map/ppermute | solution.py:32
  162.8 13.5 %collective-permute-start.26 = (bf16[2,256,48]{2,1,0:T(8,128)(2,1)S(1)}, bf16[2,256,48]{2,1,0:T(8,128)(2,1)}, u32[]{:S(2)}, u32[]{:S(2)}) collective-permute-start(bf16[2,256,48]{2,1,0:T(8,128)(2,1)S(1)} %fusion.11.refs_10_), channel_id=1, source_target_pairs={{0,2},{1,3},{2,0},{3,1},{4,6},{5,7},{6,4},{7,5},{8,10},{9,11},{10,... | collective-permute-start | bytes 147464 | tf_op jit(solution)/shard_map/ppermute | solution.py:32
  176.3 2.3 %collective-permute-start.27 = (bf16[384,768]{1,0:T(8,128)(2,1)}, bf16[384,768]{1,0:T(8,128)(2,1)S(1)}, u32[]{:S(2)}, u32[]{:S(2)}) collective-permute-start(bf16[384,768]{1,0:T(8,128)(2,1)} %tie.28), channel_id=1, source_target_pairs={{0,4},{4,0},{8,12},{12,8},{1,5},{5,1},{9,13},{13,9},{2,6},{6,2},{1... | collective-permute-start | bytes 1769480 | tf_op jit(solution)/shard_map/ppermute | solution.py:32
  177.5 14.9 %collective-permute-start.28 = (bf16[384,768]{1,0:T(8,128)(2,1)S(1)}, bf16[384,768]{1,0:T(8,128)(2,1)S(1)}, u32[]{:S(2)}, u32[]{:S(2)}) collective-permute-start(bf16[384,768]{1,0:T(8,128)(2,1)S(1)} %pad_maximum_fusion.2.refs_9_), channel_id=1, source_target_pairs={{0,1},{1,0},{2,3},{3,2},{4,5},{5,4},{6,7},{7,6},{8,9},{9,8},{10,11... | collective-permute-start | bytes 1769480 | tf_op jit(solution)/shard_map/ppermute | solution.py:32
  178.8 14.4 %collective-permute-start.29 = (bf16[192,768]{1,0:T(8,128)(2,1)S(1)}, bf16[192,768]{1,0:T(8,128)(2,1)S(1)}, u32[]{:S(2)}, u32[]{:S(2)}) collective-permute-start(bf16[192,768]{1,0:T(8,128)(2,1)S(1)} %slice.289.refs_8_), channel_id=1, source_target_pairs={{0,8},{4,12},{8,0},{12,4},{1,9},{5,13},{9,1},{13,5},{2,10},{6,14},... | collective-permute-start | bytes 884744 | tf_op jit(solution)/shard_map/ppermute | solution.py:32
  194.0 5.7 %collective-permute-start.30 = (bf16[384,768]{1,0:T(8,128)(2,1)}, bf16[384,768]{1,0:T(8,128)(2,1)}, u32[]{:S(2)}, u32[]{:S(2)}) collective-permute-start(bf16[384,768]{1,0:T(8,128)(2,1)} %tie.31), channel_id=1, source_target_pairs={{0,4},{4,0},{8,12},{12,8},{1,5},{5,1},{9,13},{13,9},{2,6},{6,2},{1... | collective-permute-start | bytes 1769480 | tf_op jit(solution)/shard_map/ppermute | solution.py:32
  196.7 15.7 %collective-permute-start.32 = (bf16[192,768]{1,0:T(8,128)(2,1)S(1)}, bf16[192,768]{1,0:T(8,128)(2,1)}, u32[]{:S(2)}, u32[]{:S(2)}) collective-permute-start(bf16[192,768]{1,0:T(8,128)(2,1)S(1)} %fusion.3.refs_6_.refs_1_), channel_id=1, source_target_pairs={{0,2},{1,3},{2,0},{3,1},{4,6},{5,7},{6,4},{7,5},{8,10},{9,11},{10,... | collective-permute-start | bytes 884744 | tf_op jit(solution)/shard_map/ppermute | solution.py:32
  199.6 4.4 %copy-start.30 = (f32[2,32,768]{2,1,0:T(8,128)}, f32[2,32,768]{2,1,0:T(8,128)S(1)}, u32[]{:S(2)}) copy-start(f32[2,32,768]{2,1,0:T(8,128)S(1)} %convolution_multiply_fusion.refs_2_) | copy-start | bytes 589828
  201.0 11.4 %collective-permute-start.31 = (bf16[192,768]{1,0:T(8,128)(2,1)S(1)}, bf16[192,768]{1,0:T(8,128)(2,1)S(1)}, u32[]{:S(2)}, u32[]{:S(2)}) collective-permute-start(bf16[192,768]{1,0:T(8,128)(2,1)S(1)} %slice.288.refs_5_), channel_id=1, source_target_pairs={{0,8},{4,12},{8,0},{12,4},{1,9},{5,13},{9,1},{13,5},{2,10},{6,14},... | collective-permute-start | bytes 884744 | tf_op jit(solution)/shard_map/ppermute | solution.py:32
  (40 other events, 58.1 us)

commit v4 on v3

--- a/solution.py
+++ b/solution.py
@@ -393,15 +393,17 @@
             return swap(x, k, "cuts")
 
         x2 = over_cuts(inputs[None], 2)
-        own = jnp.concatenate([inputs, written(experts, routes, route_gates, col)])[None]
+        own = inputs[None]
         own_over = other_chip(own)
         x2 = tie(x2, own_over)
         own_cross, own_both = other_core(own), other_core(own_over)
         x13 = over_cuts(jnp.concatenate([inputs[None], x2]), 1)
         g2 = over_cuts(tie(out_grad, x2)[None], 2)
         x2_over, x2_cross = other_chip(x2), other_core(x2)
+        routes = tie(written(experts, routes, route_gates, col), x2)
+        over = other_chip(routes)
         routes = jnp.concatenate(
-            [read(x[0, tokens:], tokens) for x in (own, own_over, own_cross, own_both)]
+            [read(x, tokens) for x in (routes, over, other_core(routes), other_core(over))]
         )
         place, back, gate = routing(routes, me, count)
         x13 = tie(x13, g2, x2_over)

time: 215 us -> 212 us (0.986)
  waiting for transfers between devices: 50.7 us -> 45.2 us
  starting transfers between devices: 28.6 us -> 31.4 us
    ppermute x33 -> x36, waiting for transfers between devices: 50.7 us -> 45.2 us  [swap(): return lax.ppermute(x, axis, [(i, i ^ k) for i in range(n)])]
    ppermute x33 -> x36, starting transfers between devices: 28.6 us -> 31.4 us  [swap(): return lax.ppermute(x, axis, [(i, i ^ k) for i in range(n)])]
    unnamed x125 -> x123, local copies, waits for them, and re-layouts: 17.5 us -> 17.4 us
  transfers between devices with their start and end apart: 33 -> 36, of which waited for: 14 -> 14; matrix products, arithmetic and copies ran while one was open for 8% -> 11% of each run, Pallas kernels for 34% -> 34%
where the time goes in v4:
time: 212 us
  Pallas kernels  94.8 us (45%)
  waiting for transfers between devices  45.2 us (21%)
  starting transfers between devices  31.4 us (15%)
  local copies, waits for them, and re-layouts  23 us (11%)
  other arithmetic  12.3 us (6%)
  matrix products  3.79 us (2%)
    ppermute x36, waiting for transfers between devices, swap(): return lax.ppermute(x, axis, [(i, i ^ k) for i in range(n)])  45.2 us
    pallas_call x3, Pallas kernels, row_back(): pl.pallas_call(without(rows_kernel, 8, len(wait)), grid_spec=pltpu.Prefet...  37.5 us
    ppermute x36, starting transfers between devices, swap(): return lax.ppermute(x, axis, [(i, i ^ k) for i in range(n)])  31.4 us
    pallas_call x1, Pallas kernels, forward(): pl.pallas_call(functools.partial(forward_kernel, far), grid_spec=pltpu.Pr...  25.6 us
    unnamed x123, local copies, waits for them, and re-layouts  17.4 us
    pallas_call x1, Pallas kernels, hidden_back(): pl.pallas_call(functools.partial(hidden_kernel, far), grid_spec=pltpu.Pre...  17.4 us
    pallas_call x2, Pallas kernels, place_rows(): pl.pallas_call(functools.partial(place_kernel, gate is not None, far), gr...  10.1 us
  transfers between devices with their start and end apart: 36, of which 14 were waited for; matrix products, arithmetic and copies ran while one was open for 11% of the time, Pallas kernels for 34%

profile of v4, /device:TPU:0, one launch (start us, length us, event | category | flops | bytes accessed | tf_op | source)
XLA Modules:
  0.0 211.8 jit_solution(16214022845809722583)
XLA Ops:
  0.7 4.1 %collective-permute-start = (bf16[1,192,768]{2,1,0:T(8,128)(2,1)}, bf16[1,192,768]{2,1,0:T(8,128)(2,1)S(1)}, u32[]{:S(2)}, u32[]{:S(2)}) collective-permute-start(bf16[1,192,768]{2,1,0:T(8,128)(2,1)} %bitcast.32), channel_id=1, source_target_pairs={{0,2},{1,3},{2,0},{3,1},{4,6},{5,7},{6,4},{7,5},{8,10},{9,11},{10,... | collective-permute-start | bytes 884744 | tf_op jit(solution)/shard_map/ppermute | solution.py:32
  4.8 1.5 collective-permute-start.1
  10.0 1.7 copy.123.refs_0_
  11.8 6.5 %collective-permute-done.refs_0_ = bf16[1,192,768]{2,1,0:T(8,128)(2,1)S(1)} collective-permute-done((bf16[1,192,768]{2,1,0:T(8,128)(2,1)}, bf16[1,192,768]{2,1,0:T(8,128)(2,1)S(1)}, u32[]{:S(2)}, u32[]{:S(2)}) %collective-permute-start) | collective-permute-done | bytes 294944 | tf_op jit(solution)/shard_map/ppermute | solution.py:32
  20.4 1.5 collective-permute-start.2
  23.3 1.0 pad_maximum_fusion.1
  25.0 4.1 %collective-permute-start.12 = (bf16[2,192,768]{2,1,0:T(8,128)(2,1)S(1)}, bf16[2,192,768]{2,1,0:T(8,128)(2,1)S(1)}, u32[]{:S(2)}, u32[]{:S(2)}) collective-permute-start(bf16[2,192,768]{2,1,0:T(8,128)(2,1)S(1)} %pad_maximum_fusion.1), channel_id=1, source_target_pairs={{0,1},{1,0},{2,3},{3,2},{4,5},{5,4},{6,7},{7,6},{8,9},{9,8},{10,11... | collective-permute-start | bytes 1769480 | tf_op jit(solution)/shard_map/ppermute | solution.py:32
  30.5 1.2 collective-permute-done.4
  32.4 9.2 %collective-permute-done.5.refs_1_ = bf16[1,192,768]{2,1,0:T(8,128)(2,1)S(1)} collective-permute-done((bf16[1,192,768]{2,1,0:T(8,128)(2,1)}, bf16[1,192,768]{2,1,0:T(8,128)(2,1)S(1)}, u32[]{:S(2)}, u32[]{:S(2)}) %collective-permute-start.5) | collective-permute-done | bytes 294944 | tf_op jit(solution)/shard_map/ppermute | solution.py:32
  41.8 6.7 %collective-permute-done.12.refs_0_ = bf16[2,192,768]{2,1,0:T(8,128)(2,1)S(1)} collective-permute-done((bf16[2,192,768]{2,1,0:T(8,128)(2,1)S(1)}, bf16[2,192,768]{2,1,0:T(8,128)(2,1)S(1)}, u32[]{:S(2)}, u32[]{:S(2)}) %collective-permute-start.12) | collective-permute-done | bytes 589856 | tf_op jit(solution)/shard_map/ppermute | solution.py:32
  49.4 1.5 collective-permute-start.13
  52.0 0.9 copy.96.refs_6_.rest_0_
  52.9 1.2 collective-permute-start.15
  54.0 0.9 or_convert_fusion.refs_5_
  55.0 5.8 %collective-permute-done.15.refs_2_ = bf16[1,2,48,768]{3,2,1,0:T(8,128)(2,1)S(1)} collective-permute-done((bf16[1,2,48,768]{3,2,1,0:T(8,128)(2,1)}, bf16[1,2,48,768]{3,2,1,0:T(8,128)(2,1)S(1)}, u32[]{:S(2)}, u32[]{:S(2)}) %collective-permute-start.15) | collective-permute-done | bytes 147488 | tf_op jit(solution)/shard_map/ppermute | solution.py:32
  60.8 2.9 %collective-permute-done.14.refs_1_.rest_9_.rest_13_ = bf16[2,192,768]{2,1,0:T(8,128)(2,1)S(1)} collective-permute-done((bf16[2,192,768]{2,1,0:T(8,128)(2,1)S(1)}, bf16[2,192,768]{2,1,0:T(8,128)(2,1)S(1)}, u32[]{:S(2)}, u32[]{:S(2)}) %collective-permute-start.14) | collective-permute-done | bytes 589856 | tf_op jit(solution)/shard_map/ppermute | solution.py:32
  66.7 1.4 collective-permute-done.7.rest_2_
  68.0 1.6 collective-permute-start.6
  69.7 1.0 collective-permute-start.21
  71.4 1.0 pad_maximum_fusion.3.rest_0_.rest_1_.refs_7_
  72.5 1.9 collective-permute-start.18
  74.4 5.0 %place_rows.2.x_ref = bf16[2,256,3072]{2,1,0:T(8,128)(2,1)} custom-call(s32[1]{0:T(128)} %bitcast.at_ref.refs_0_, bf16[4,128,192]{2,1,0:T(8,128)(2,1)} %fusion.10.refs_4_.place_ref, bf16[1,192,768]{2,1,0:T(8,128)(2,1)} %bitcast.34, bf16[1,192,768]{2,1,0:T(8,128)(2,1)} %copy-done.36, bf16[1,192,768]{2,1,0:T(8,128)(2,1)} %copy-done.47, ...), custom_call_target="tpu_custom_call" | custom-call | flops 1 | bytes 1 | tf_op jit(solution)/shard_map/place_rows/pallas_call | solution.py:81
  79.4 2.3 %collective-permute-done.18.rest_2_.rest_3_.refs_7_ = bf16[2,2,48,768]{3,2,1,0:T(8,128)(2,1)S(1)} collective-permute-done((bf16[2,2,48,768]{3,2,1,0:T(8,128)(2,1)S(1)}, bf16[2,2,48,768]{3,2,1,0:T(8,128)(2,1)S(1)}, u32[]{:S(2)}, u32[]{:S(2)}) %collective-permute-start.18) | collective-permute-done | bytes 294944 | tf_op jit(solution)/shard_map/ppermute | solution.py:32
  82.4 25.6 %forward_units.1 = (bf16[2,256,2048]{2,1,0:T(8,128)(2,1)}, bf16[2,256,2048]{2,1,0:T(8,128)(2,1)}, bf16[2,256,2048]{2,1,0:T(8,128)(2,1)}, bf16[2,256,32]{2,1,0:T(8,128)(2,1)}) custom-call(s32[1]{0:T(128)} %bitcast.at_ref.refs_0_, bf16[2,256,3072]{2,1,0:T(8,128)(2,1)} %place_rows.2.x_ref, bf16[2,3072,2048]{2,1,0:T(8,128)(2,1)} %refs_3_.5, ...), custom_call_target="tpu_custom_call" | custom-call | flops 1 | bytes 1 | tf_op jit(solution)/shard_map/forward_units/pallas_call | solution.py:150
  108.9 0.9 copy-done.8
  111.1 1.0 collective-permute-done.23.rest_12_.rest_16_
  113.0 5.1 %place_rows.3.g_ref = bf16[2,256,3072]{2,1,0:T(8,128)(2,1)} custom-call(s32[1]{0:T(128)} %bitcast.at_ref.refs_0_, bf16[4,128,192]{2,1,0:T(8,128)(2,1)} %fusion.10.refs_4_.place_ref, f32[4,128,1]{2,1,0:T(8,128)} %copy.96.refs_6_.rest_0_, bf16[2,192,768]{2,1,0:T(8,128)(2,1)} %copy-done.5, bf16[2,192,768]{2,1,0:T(8,128)(2,1)} %tie.24.rest_2_.rest_6_, ...), custom_call_target="tpu_custom_call" | custom-call | flops 1 | bytes 1 | tf_op jit(solution)/shard_map/place_rows/pallas_call | solution.py:81
  118.1 17.4 %hidden_back.1 = (bf16[2,256,2048]{2,1,0:T(8,128)(2,1)}, bf16[2,256,2048]{2,1,0:T(8,128)(2,1)}, bf16[2,256,48]{2,1,0:T(8,128)(2,1)}, bf16[2,256,16]{2,1,0:T(8,128)(2,1)}) custom-call(s32[1]{0:T(128)} %bitcast.at_ref.refs_0_, bf16[2,256,3072]{2,1,0:T(8,128)(2,1)} %place_rows.3.g_ref, bf16[2,2048,3072]{2,1,0:T(8,128)(2,1)} %wd_ref.1, ...), custom_call_target="tpu_custom_call" | custom-call | flops 1 | bytes 1 | tf_op jit(solution)/shard_map/hidden_back/pallas_call | solution.py:198
  135.5 1.8 collective-permute-start.24
  137.9 16.7 %row_back.3 = (bf16[384,768]{1,0:T(8,128)(2,1)}, bf16[384,768]{1,0:T(8,128)(2,1)}, bf16[384,768]{1,0:T(8,128)(2,1)}, bf16[384,768]{1,0:T(8,128)(2,1)}) custom-call(s32[2]{0:T(128)} %pad_add_fusion.refs_0_, bf16[2,256,2048]{2,1,0:T(8,128)(2,1)} %get-tuple-element.29.refs_1_.refs_2_, bf16[2,256,2048]{2,1,0:T(8,128)(2,1)} %get-tuple-element.30.refs_2_.refs_3_, ...), custom_call_target="tpu_custom_call" | custom-call | flops 1 | bytes 1 | tf_op jit(solution)/shard_map/row_back/pallas_call | solution.py:284
  155.8 1.7 collective-permute-done.25
  157.6 1.2 collective-permute-start.27
  159.8 0.9 collective-permute-start.28
  160.7 1.2 collective-permute-start.29
  161.9 10.4 %row_back.4 = (bf16[384,768]{1,0:T(8,128)(2,1)}, bf16[384,768]{1,0:T(8,128)(2,1)}) custom-call(s32[1]{0:T(128)} %bitcast.11.refs_0_, bf16[2,256,2048]{2,1,0:T(8,128)(2,1)} %get-tuple-element.29.refs_1_.refs_2_, bf16[2,256,2048]{2,1,0:T(8,128)(2,1)} %get-tuple-element.30.refs_2_.refs_3_, bf16[2,3072,2048]{2,1,0:T(8,128)(2,1)} %refs_3_.5, ...), custom_call_target="tpu_custom_call" | custom-call | flops 1 | bytes 1 | tf_op jit(solution)/shard_map/row_back/pallas_call | solution.py:284
  173.9 0.9 copy-done.21
  176.3 1.2 collective-permute-start.32
  177.5 10.4 %row_back.5 = (bf16[384,768]{1,0:T(8,128)(2,1)}, bf16[384,768]{1,0:T(8,128)(2,1)}) custom-call(s32[1]{0:T(128)} %bitcast.at_ref.refs_0_, bf16[2,256,2048]{2,1,0:T(8,128)(2,1)} %get-tuple-element.29.refs_1_.refs_2_, bf16[2,256,2048]{2,1,0:T(8,128)(2,1)} %get-tuple-element.30.refs_2_.refs_3_, bf16[2,3072,2048]{2,1,0:T(8,128)(2,1)} %refs_3_.5, ...), custom_call_target="tpu_custom_call" | custom-call | flops 1 | bytes 1 | tf_op jit(solution)/shard_map/row_back/pallas_call | solution.py:284
  187.9 2.0 collective-permute-done.31.refs_0_
  192.4 1.6 add_convert_fusion.refs_0_
  194.2 1.8 collective-permute-start.35
  196.0 1.5 convolution_multiply_fusion.refs_2_
  197.5 1.3 convert_add_fusion
  198.9 1.2 collective-permute-start.34
  200.1 2.1 convolution_multiply_fusion.1.refs_3_
  202.9 4.1 %adapter_back.1 = (f32[2,16,2048]{2,1,0:T(8,128)}, f32[2,16,2048]{2,1,0:T(8,128)}, f32[2,16,2048]{2,1,0:T(8,128)}) custom-call(bf16[2,256,32]{2,1,0:T(8,128)(2,1)} %get-tuple-element.40.refs_0_, bf16[2,256,16]{2,1,0:T(8,128)(2,1)} %get-tuple-element.41.refs_1_, bf16[2,256,2048]{2,1,0:T(8,128)(2,1)} %get-tuple-element.29.refs_1_.refs_2_, ...), custom_call_target="tpu_custom_call" | custom-call | flops 1 | bytes 1 | tf_op jit(solution)/shard_map/adapter_back/pallas_call | solution.py:241
  207.0 3.0 %collective-permute-done.35.refs_0_ = bf16[192,768]{1,0:T(8,128)(2,1)} collective-permute-done((bf16[192,768]{1,0:T(8,128)(2,1)S(1)}, bf16[192,768]{1,0:T(8,128)(2,1)}, u32[]{:S(2)}, u32[]{:S(2)}) %collective-permute-start.35) | collective-permute-done | bytes 294944 | tf_op jit(solution)/shard_map/ppermute | solution.py:32
  210.0 1.8 fusion.5
  (243 shorter events, 28.7 us)
Async XLA Ops:
  0.6 11.1 %copy-start.50 = (bf16[2,16,768]{2,1,0:T(8,128)(2,1)S(1)}, bf16[2,16,768]{2,1,0:T(8,128)(2,1)}, u32[]{:S(2)}) copy-start(bf16[2,16,768]{2,1,0:T(8,128)(2,1)} %param.20) | copy-start | bytes 147460
  0.6 11.1 %copy-start.51 = (bf16[2,16,768]{2,1,0:T(8,128)(2,1)S(1)}, bf16[2,16,768]{2,1,0:T(8,128)(2,1)}, u32[]{:S(2)}) copy-start(bf16[2,16,768]{2,1,0:T(8,128)(2,1)} %param.22) | copy-start | bytes 147460
  0.7 11.2 %copy-start.52 = (bf16[2,16,768]{2,1,0:T(8,128)(2,1)S(1)}, bf16[2,16,768]{2,1,0:T(8,128)(2,1)}, u32[]{:S(2)}) copy-start(bf16[2,16,768]{2,1,0:T(8,128)(2,1)} %param.25) | copy-start | bytes 147460
  0.7 17.6 %collective-permute-start = (bf16[1,192,768]{2,1,0:T(8,128)(2,1)}, bf16[1,192,768]{2,1,0:T(8,128)(2,1)S(1)}, u32[]{:S(2)}, u32[]{:S(2)}) collective-permute-start(bf16[1,192,768]{2,1,0:T(8,128)(2,1)} %bitcast.32), channel_id=1, source_target_pairs={{0,2},{1,3},{2,0},{3,1},{4,6},{5,7},{6,4},{7,5},{8,10},{9,11},{10,... | collective-permute-start | bytes 884744 | tf_op jit(solution)/shard_map/ppermute | solution.py:32
  4.8 13.5 %collective-permute-start.1 = (bf16[1,192,768]{2,1,0:T(8,128)(2,1)}, bf16[1,192,768]{2,1,0:T(8,128)(2,1)S(1)}, u32[]{:S(2)}, u32[]{:S(2)}) collective-permute-start(bf16[1,192,768]{2,1,0:T(8,128)(2,1)} %bitcast.33), channel_id=1, source_target_pairs={{0,8},{4,12},{8,0},{12,4},{1,9},{5,13},{9,1},{13,5},{2,10},{6,14},... | collective-permute-start | bytes 884744 | tf_op jit(solution)/shard_map/ppermute | solution.py:32
  10.0 13.3 %copy-start.40 = (bf16[192,768]{1,0:T(8,128)(2,1)S(1)}, bf16[192,768]{1,0:T(8,128)(2,1)}, u32[]{:S(2)}) copy-start(bf16[192,768]{1,0:T(8,128)(2,1)} %param.13) | copy-start | bytes 884740
  11.8 13.1 %copy-start.42 = (bf16[2,48,768]{2,1,0:T(8,128)(2,1)}, bf16[2,48,768]{2,1,0:T(8,128)(2,1)S(1)}, u32[]{:S(2)}) copy-start(bf16[2,48,768]{2,1,0:T(8,128)(2,1)S(1)} %constant_dynamic-update-slice_fusion) | copy-start | bytes 442372
  20.4 9.3 %collective-permute-start.2 = (bf16[16,768]{1,0:T(8,128)(2,1)}, bf16[16,768]{1,0:T(8,128)(2,1)S(1)}, u32[]{:S(2)}, u32[]{:S(2)}) collective-permute-start(bf16[16,768]{1,0:T(8,128)(2,1)} %tie.19), channel_id=1, source_target_pairs={{0,8},{4,12},{8,0},{12,4},{1,9},{5,13},{9,1},{13,5},{2,10},{6,14},... | collective-permute-start | bytes 73736 | tf_op jit(solution)/shard_map/ppermute | solution.py:32
  22.0 7.2 %collective-permute-start.3 = (bf16[16,768]{1,0:T(8,128)(2,1)}, bf16[16,768]{1,0:T(8,128)(2,1)S(1)}, u32[]{:S(2)}, u32[]{:S(2)}) collective-permute-start(bf16[16,768]{1,0:T(8,128)(2,1)} %tie.19), channel_id=1, source_target_pairs={{0,4},{4,0},{8,12},{12,8},{1,5},{5,1},{9,13},{13,9},{2,6},{6,2},{1... | collective-permute-start | bytes 73736 | tf_op jit(solution)/shard_map/ppermute | solution.py:32
  22.8 19.0 %collective-permute-start.9 = (bf16[1,192,768]{2,1,0:T(8,128)(2,1)}, bf16[1,192,768]{2,1,0:T(8,128)(2,1)S(1)}, u32[]{:S(2)}, u32[]{:S(2)}) collective-permute-start(bf16[1,192,768]{2,1,0:T(8,128)(2,1)} %tie.18.refs_1_.rest_4_), channel_id=1, source_target_pairs={{0,8},{4,12},{8,0},{12,4},{1,9},{5,13},{9,1},{13,5},{2,10},{6,14},... | collective-permute-start | bytes 884744 | tf_op jit(solution)/shard_map/ppermute | solution.py:32
  24.9 16.7 %collective-permute-start.5 = (bf16[1,192,768]{2,1,0:T(8,128)(2,1)}, bf16[1,192,768]{2,1,0:T(8,128)(2,1)S(1)}, u32[]{:S(2)}, u32[]{:S(2)}) collective-permute-start(bf16[1,192,768]{2,1,0:T(8,128)(2,1)} %bitcast.30), channel_id=1, source_target_pairs={{0,2},{1,3},{2,0},{3,1},{4,6},{5,7},{6,4},{7,5},{8,10},{9,11},{10,... | collective-permute-start | bytes 884744 | tf_op jit(solution)/shard_map/ppermute | solution.py:32
  25.0 23.6 %collective-permute-start.12 = (bf16[2,192,768]{2,1,0:T(8,128)(2,1)S(1)}, bf16[2,192,768]{2,1,0:T(8,128)(2,1)S(1)}, u32[]{:S(2)}, u32[]{:S(2)}) collective-permute-start(bf16[2,192,768]{2,1,0:T(8,128)(2,1)S(1)} %pad_maximum_fusion.1), channel_id=1, source_target_pairs={{0,1},{1,0},{2,3},{3,2},{4,5},{5,4},{6,7},{7,6},{8,9},{9,8},{10,11... | collective-permute-start | bytes 1769480 | tf_op jit(solution)/shard_map/ppermute | solution.py:32
  30.0 11.7 %copy-start.35 = (bf16[192,768]{1,0:T(8,128)(2,1)S(1)}, bf16[192,768]{1,0:T(8,128)(2,1)}, u32[]{:S(2)}) copy-start(bf16[192,768]{1,0:T(8,128)(2,1)} %param.14) | copy-start | bytes 884740
  30.4 1.3 collective-permute-start.4
  41.6 6.9 %copy-start.34 = (bf16[1,192,768]{2,1,0:T(8,128)(2,1)}, bf16[1,192,768]{2,1,0:T(8,128)(2,1)S(1)}, u32[]{:S(2)}) copy-start(bf16[1,192,768]{2,1,0:T(8,128)(2,1)S(1)} %collective-permute-done.5.refs_1_) | copy-start | bytes 884740
  41.7 30.7 %copy-start.5 = (bf16[2,192,768]{2,1,0:T(8,128)(2,1)}, bf16[2,192,768]{2,1,0:T(8,128)(2,1)S(1)}, u32[]{:S(2)}) copy-start(bf16[2,192,768]{2,1,0:T(8,128)(2,1)S(1)} %pad_maximum_fusion.rest_1_.rest_5_) | copy-start | bytes 1769476
  41.7 22.0 %collective-permute-start.14 = (bf16[2,192,768]{2,1,0:T(8,128)(2,1)S(1)}, bf16[2,192,768]{2,1,0:T(8,128)(2,1)S(1)}, u32[]{:S(2)}, u32[]{:S(2)}) collective-permute-start(bf16[2,192,768]{2,1,0:T(8,128)(2,1)S(1)} %pad_maximum_fusion.rest_1_.rest_5_), channel_id=1, source_target_pairs={{0,1},{1,0},{2,3},{3,2},{4,5},{5,4},{6,7},{7,6},{8,9},{9,8},{10,11... | collective-permute-start | bytes 1769480 | tf_op jit(solution)/shard_map/ppermute | solution.py:32
  49.4 14.3 %collective-permute-start.13 = (bf16[2,192,768]{2,1,0:T(8,128)(2,1)}, bf16[2,192,768]{2,1,0:T(8,128)(2,1)S(1)}, u32[]{:S(2)}, u32[]{:S(2)}) collective-permute-start(bf16[2,192,768]{2,1,0:T(8,128)(2,1)} %tie.21.refs_1_.rest_8_.rest_12_), channel_id=1, source_target_pairs={{0,8},{4,12},{8,0},{12,4},{1,9},{5,13},{9,1},{13,5},{2,10},{6,14},... | collective-permute-start | bytes 1769480 | tf_op jit(solution)/shard_map/ppermute | solution.py:32
  50.9 12.8 %collective-permute-start.16 = (bf16[2,192,768]{2,1,0:T(8,128)(2,1)}, bf16[2,192,768]{2,1,0:T(8,128)(2,1)S(1)}, u32[]{:S(2)}, u32[]{:S(2)}) collective-permute-start(bf16[2,192,768]{2,1,0:T(8,128)(2,1)} %tie.21.refs_1_.rest_8_.rest_12_), channel_id=1, source_target_pairs={{0,4},{4,0},{8,12},{12,8},{1,5},{5,1},{9,13},{13,9},{2,6},{6,2},{1... | collective-permute-start | bytes 1769480 | tf_op jit(solution)/shard_map/ppermute | solution.py:32
  52.9 7.9 %collective-permute-start.15 = (bf16[1,2,48,768]{3,2,1,0:T(8,128)(2,1)}, bf16[1,2,48,768]{3,2,1,0:T(8,128)(2,1)S(1)}, u32[]{:S(2)}, u32[]{:S(2)}) collective-permute-start(bf16[1,2,48,768]{3,2,1,0:T(8,128)(2,1)} %bitcast.38), channel_id=1, source_target_pairs={{0,2},{1,3},{2,0},{3,1},{4,6},{5,7},{6,4},{7,5},{8,10},{9,11},{10,... | collective-permute-start | bytes 442376 | tf_op jit(solution)/shard_map/ppermute | solution.py:32
  55.0 11.1 %copy-start.37 = (bf16[1,192,768]{2,1,0:T(8,128)(2,1)S(1)}, bf16[1,192,768]{2,1,0:T(8,128)(2,1)}, u32[]{:S(2)}) copy-start(bf16[1,192,768]{2,1,0:T(8,128)(2,1)} %copy-done.36) | copy-start | bytes 884740
  55.0 11.1 %copy-start.3 = (bf16[1,192,768]{2,1,0:T(8,128)(2,1)S(1)}, bf16[1,192,768]{2,1,0:T(8,128)(2,1)}, u32[]{:S(2)}) copy-start(bf16[1,192,768]{2,1,0:T(8,128)(2,1)} %tie.18.refs_1_.rest_4_) | copy-start | bytes 884740
  55.0 11.6 %copy-start.39 = (bf16[1,192,768]{2,1,0:T(8,128)(2,1)S(1)}, bf16[1,192,768]{2,1,0:T(8,128)(2,1)}, u32[]{:S(2)}) copy-start(bf16[1,192,768]{2,1,0:T(8,128)(2,1)} %copy-done.38) | copy-start | bytes 884740
  65.6 6.9 %collective-permute-start.17 = (bf16[2,192,768]{2,1,0:T(8,128)(2,1)}, bf16[2,192,768]{2,1,0:T(8,128)(2,1)S(1)}, u32[]{:S(2)}, u32[]{:S(2)}) collective-permute-start(bf16[2,192,768]{2,1,0:T(8,128)(2,1)} %tie.23.rest_9_.rest_13_), channel_id=1, source_target_pairs={{0,4},{4,0},{8,12},{12,8},{1,5},{5,1},{9,13},{13,9},{2,6},{6,2},{1... | collective-permute-start | bytes 1769480 | tf_op jit(solution)/shard_map/ppermute | solution.py:32
  65.6 2.5 %collective-permute-start.7 = (bf16[1,192,768]{2,1,0:T(8,128)(2,1)S(1)}, bf16[1,192,768]{2,1,0:T(8,128)(2,1)S(1)}, u32[]{:S(2)}, u32[]{:S(2)}) collective-permute-start(bf16[1,192,768]{2,1,0:T(8,128)(2,1)S(1)} %bitcast.36), channel_id=1, source_target_pairs={{0,4},{4,0},{8,12},{12,8},{1,5},{5,1},{9,13},{13,9},{2,6},{6,2},{1... | collective-permute-start | bytes 884744 | tf_op jit(solution)/shard_map/ppermute | solution.py:32
  66.1 3.5 %collective-permute-start.8 = (bf16[1,192,768]{2,1,0:T(8,128)(2,1)S(1)}, bf16[1,192,768]{2,1,0:T(8,128)(2,1)}, u32[]{:S(2)}, u32[]{:S(2)}) collective-permute-start(bf16[1,192,768]{2,1,0:T(8,128)(2,1)S(1)} %copy-done.37), channel_id=1, source_target_pairs={{0,4},{4,0},{8,12},{12,8},{1,5},{5,1},{9,13},{13,9},{2,6},{6,2},{1... | collective-permute-start | bytes 884744 | tf_op jit(solution)/shard_map/ppermute | solution.py:32
  66.1 3.6 %collective-permute-start.10 = (bf16[1,192,768]{2,1,0:T(8,128)(2,1)S(1)}, bf16[1,192,768]{2,1,0:T(8,128)(2,1)S(1)}, u32[]{:S(2)}, u32[]{:S(2)}) collective-permute-start(bf16[1,192,768]{2,1,0:T(8,128)(2,1)S(1)} %copy-done.3), channel_id=1, source_target_pairs={{0,4},{4,0},{8,12},{12,8},{1,5},{5,1},{9,13},{13,9},{2,6},{6,2},{1... | collective-permute-start | bytes 884744 | tf_op jit(solution)/shard_map/ppermute | solution.py:32
  66.6 4.1 %collective-permute-start.11 = (bf16[1,192,768]{2,1,0:T(8,128)(2,1)S(1)}, bf16[1,192,768]{2,1,0:T(8,128)(2,1)S(1)}, u32[]{:S(2)}, u32[]{:S(2)}) collective-permute-start(bf16[1,192,768]{2,1,0:T(8,128)(2,1)S(1)} %copy-done.39), channel_id=1, source_target_pairs={{0,4},{4,0},{8,12},{12,8},{1,5},{5,1},{9,13},{13,9},{2,6},{6,2},{1... | collective-permute-start | bytes 884744 | tf_op jit(solution)/shard_map/ppermute | solution.py:32
  68.0 40.0 %collective-permute-start.6 = (bf16[2,192,768]{2,1,0:T(8,128)(2,1)S(1)}, bf16[2,192,768]{2,1,0:T(8,128)(2,1)}, u32[]{:S(2)}, u32[]{:S(2)}) collective-permute-start(bf16[2,192,768]{2,1,0:T(8,128)(2,1)S(1)} %pad_maximum_fusion.rest_1_.rest_5_), channel_id=1, source_target_pairs={{0,8},{4,12},{8,0},{12,4},{1,9},{5,13},{9,1},{13,5},{2,10},{6,14},... | collective-permute-start | bytes 1769480 | tf_op jit(solution)/shard_map/ppermute | solution.py:32
  69.6 38.5 %collective-permute-start.19 = (bf16[2,192,768]{2,1,0:T(8,128)(2,1)S(1)}, bf16[2,192,768]{2,1,0:T(8,128)(2,1)S(1)}, u32[]{:S(2)}, u32[]{:S(2)}) collective-permute-start(bf16[2,192,768]{2,1,0:T(8,128)(2,1)S(1)} %pad_maximum_fusion.rest_1_.rest_5_), channel_id=1, source_target_pairs={{0,4},{4,0},{8,12},{12,8},{1,5},{5,1},{9,13},{13,9},{2,6},{6,2},{1... | collective-permute-start | bytes 1769480 | tf_op jit(solution)/shard_map/ppermute | solution.py:32
  69.7 39.2 %collective-permute-start.21 = (bf16[2,192,768]{2,1,0:T(8,128)(2,1)}, bf16[2,192,768]{2,1,0:T(8,128)(2,1)}, u32[]{:S(2)}, u32[]{:S(2)}) collective-permute-start(bf16[2,192,768]{2,1,0:T(8,128)(2,1)} %copy-done.6), channel_id=1, source_target_pairs={{0,8},{4,12},{8,0},{12,4},{1,9},{5,13},{9,1},{13,5},{2,10},{6,14},... | collective-permute-start | bytes 1769480 | tf_op jit(solution)/shard_map/ppermute | solution.py:32
  70.7 38.2 %collective-permute-start.22 = (bf16[2,192,768]{2,1,0:T(8,128)(2,1)}, bf16[2,192,768]{2,1,0:T(8,128)(2,1)S(1)}, u32[]{:S(2)}, u32[]{:S(2)}) collective-permute-start(bf16[2,192,768]{2,1,0:T(8,128)(2,1)} %copy-done.6), channel_id=1, source_target_pairs={{0,4},{4,0},{8,12},{12,8},{1,5},{5,1},{9,13},{13,9},{2,6},{6,2},{1... | collective-permute-start | bytes 1769480 | tf_op jit(solution)/shard_map/ppermute | solution.py:32
  72.5 7.0 %copy-start = (bf16[2,2,48,768]{3,2,1,0:T(8,128)(2,1)}, bf16[2,2,48,768]{3,2,1,0:T(8,128)(2,1)S(1)}, u32[]{:S(2)}) copy-start(bf16[2,2,48,768]{3,2,1,0:T(8,128)(2,1)S(1)} %pad_maximum_fusion.3.rest_0_.rest_1_.refs_7_) | copy-start | bytes 884740
  72.5 9.2 %collective-permute-start.18 = (bf16[2,2,48,768]{3,2,1,0:T(8,128)(2,1)S(1)}, bf16[2,2,48,768]{3,2,1,0:T(8,128)(2,1)S(1)}, u32[]{:S(2)}, u32[]{:S(2)}) collective-permute-start(bf16[2,2,48,768]{3,2,1,0:T(8,128)(2,1)S(1)} %pad_maximum_fusion.3.rest_0_.rest_1_.refs_7_), channel_id=1, source_target_pairs={{0,1},{1,0},{2,3},{3,2},{4,5},{5,4},{6,7},{7,6},{8,9},{9,8},{10,11... | collective-permute-start | bytes 884744 | tf_op jit(solution)/shard_map/ppermute | solution.py:32
  108.9 2.2 %collective-permute-start.20 = (bf16[2,192,768]{2,1,0:T(8,128)(2,1)}, bf16[2,192,768]{2,1,0:T(8,128)(2,1)S(1)}, u32[]{:S(2)}, u32[]{:S(2)}) collective-permute-start(bf16[2,192,768]{2,1,0:T(8,128)(2,1)} %tie.24.rest_2_.rest_6_), channel_id=1, source_target_pairs={{0,4},{4,0},{8,12},{12,8},{1,5},{5,1},{9,13},{13,9},{2,6},{6,2},{1... | collective-permute-start | bytes 1769480 | tf_op jit(solution)/shard_map/ppermute | solution.py:32
  109.8 2.3 %collective-permute-start.23 = (bf16[2,192,768]{2,1,0:T(8,128)(2,1)}, bf16[2,192,768]{2,1,0:T(8,128)(2,1)S(1)}, u32[]{:S(2)}, u32[]{:S(2)}) collective-permute-start(bf16[2,192,768]{2,1,0:T(8,128)(2,1)} %tie.25.rest_10_.rest_14_), channel_id=1, source_target_pairs={{0,4},{4,0},{8,12},{12,8},{1,5},{5,1},{9,13},{13,9},{2,6},{6,2},{1... | collective-permute-start | bytes 1769480 | tf_op jit(solution)/shard_map/ppermute | solution.py:32
  135.5 19.1 %collective-permute-start.24 = (bf16[2,256,48]{2,1,0:T(8,128)(2,1)}, bf16[2,256,48]{2,1,0:T(8,128)(2,1)S(1)}, u32[]{:S(2)}, u32[]{:S(2)}) collective-permute-start(bf16[2,256,48]{2,1,0:T(8,128)(2,1)} %get-tuple-element.31.refs_6_), channel_id=1, source_target_pairs={{0,1},{1,0},{2,3},{3,2},{4,5},{5,4},{6,7},{7,6},{8,9},{9,8},{10,11... | collective-permute-start | bytes 147464 | tf_op jit(solution)/shard_map/ppermute | solution.py:32
  155.2 2.2 %collective-permute-start.25 = (bf16[384,768]{1,0:T(8,128)(2,1)}, bf16[384,768]{1,0:T(8,128)(2,1)S(1)}, u32[]{:S(2)}, u32[]{:S(2)}) collective-permute-start(bf16[384,768]{1,0:T(8,128)(2,1)} %tie.26), channel_id=1, source_target_pairs={{0,4},{4,0},{8,12},{12,8},{1,5},{5,1},{9,13},{13,9},{2,6},{6,2},{1... | collective-permute-start | bytes 1769480 | tf_op jit(solution)/shard_map/ppermute | solution.py:32
  155.3 3.5 %collective-permute-start.26 = (bf16[384,768]{1,0:T(8,128)(2,1)}, bf16[384,768]{1,0:T(8,128)(2,1)S(1)}, u32[]{:S(2)}, u32[]{:S(2)}) collective-permute-start(bf16[384,768]{1,0:T(8,128)(2,1)} %tie.27), channel_id=1, source_target_pairs={{0,4},{4,0},{8,12},{12,8},{1,5},{5,1},{9,13},{13,9},{2,6},{6,2},{1... | collective-permute-start | bytes 1769480 | tf_op jit(solution)/shard_map/ppermute | solution.py:32
  157.6 14.7 %collective-permute-start.27 = (bf16[192,768]{1,0:T(8,128)(2,1)S(1)}, bf16[192,768]{1,0:T(8,128)(2,1)S(1)}, u32[]{:S(2)}, u32[]{:S(2)}) collective-permute-start(bf16[192,768]{1,0:T(8,128)(2,1)S(1)} %slice.271.refs_8_), channel_id=1, source_target_pairs={{0,8},{4,12},{8,0},{12,4},{1,9},{5,13},{9,1},{13,5},{2,10},{6,14},... | collective-permute-start | bytes 884744 | tf_op jit(solution)/shard_map/ppermute | solution.py:32
  159.8 13.3 %collective-permute-start.28 = (bf16[192,768]{1,0:T(8,128)(2,1)}, bf16[192,768]{1,0:T(8,128)(2,1)S(1)}, u32[]{:S(2)}, u32[]{:S(2)}) collective-permute-start(bf16[192,768]{1,0:T(8,128)(2,1)} %slice.270.refs_9_), channel_id=1, source_target_pairs={{0,8},{4,12},{8,0},{12,4},{1,9},{5,13},{9,1},{13,5},{2,10},{6,14},... | collective-permute-start | bytes 884744 | tf_op jit(solution)/shard_map/ppermute | solution.py:32
  160.7 13.1 %collective-permute-start.29 = (bf16[2,256,48]{2,1,0:T(8,128)(2,1)S(1)}, bf16[2,256,48]{2,1,0:T(8,128)(2,1)}, u32[]{:S(2)}, u32[]{:S(2)}) collective-permute-start(bf16[2,256,48]{2,1,0:T(8,128)(2,1)S(1)} %fusion.11.refs_10_), channel_id=1, source_target_pairs={{0,2},{1,3},{2,0},{3,1},{4,6},{5,7},{6,4},{7,5},{8,10},{9,11},{10,... | collective-permute-start | bytes 147464 | tf_op jit(solution)/shard_map/ppermute | solution.py:32
  173.8 2.3 %collective-permute-start.30 = (bf16[384,768]{1,0:T(8,128)(2,1)}, bf16[384,768]{1,0:T(8,128)(2,1)S(1)}, u32[]{:S(2)}, u32[]{:S(2)}) collective-permute-start(bf16[384,768]{1,0:T(8,128)(2,1)} %tie.30), channel_id=1, source_target_pairs={{0,4},{4,0},{8,12},{12,8},{1,5},{5,1},{9,13},{13,9},{2,6},{6,2},{1... | collective-permute-start | bytes 1769480 | tf_op jit(solution)/shard_map/ppermute | solution.py:32
  175.0 14.9 %collective-permute-start.31 = (bf16[384,768]{1,0:T(8,128)(2,1)S(1)}, bf16[384,768]{1,0:T(8,128)(2,1)S(1)}, u32[]{:S(2)}, u32[]{:S(2)}) collective-permute-start(bf16[384,768]{1,0:T(8,128)(2,1)S(1)} %pad_maximum_fusion.2.refs_9_), channel_id=1, source_target_pairs={{0,1},{1,0},{2,3},{3,2},{4,5},{5,4},{6,7},{7,6},{8,9},{9,8},{10,11... | collective-permute-start | bytes 1769480 | tf_op jit(solution)/shard_map/ppermute | solution.py:32
  176.3 14.4 %collective-permute-start.32 = (bf16[192,768]{1,0:T(8,128)(2,1)S(1)}, bf16[192,768]{1,0:T(8,128)(2,1)S(1)}, u32[]{:S(2)}, u32[]{:S(2)}) collective-permute-start(bf16[192,768]{1,0:T(8,128)(2,1)S(1)} %slice.269.refs_8_), channel_id=1, source_target_pairs={{0,8},{4,12},{8,0},{12,4},{1,9},{5,13},{9,1},{13,5},{2,10},{6,14},... | collective-permute-start | bytes 884744 | tf_op jit(solution)/shard_map/ppermute | solution.py:32
  191.5 6.1 %collective-permute-start.33 = (bf16[384,768]{1,0:T(8,128)(2,1)}, bf16[384,768]{1,0:T(8,128)(2,1)}, u32[]{:S(2)}, u32[]{:S(2)}) collective-permute-start(bf16[384,768]{1,0:T(8,128)(2,1)} %tie.33), channel_id=1, source_target_pairs={{0,4},{4,0},{8,12},{12,8},{1,5},{5,1},{9,13},{13,9},{2,6},{6,2},{1... | collective-permute-start | bytes 1769480 | tf_op jit(solution)/shard_map/ppermute | solution.py:32
  194.2 15.8 %collective-permute-start.35 = (bf16[192,768]{1,0:T(8,128)(2,1)S(1)}, bf16[192,768]{1,0:T(8,128)(2,1)}, u32[]{:S(2)}, u32[]{:S(2)}) collective-permute-start(bf16[192,768]{1,0:T(8,128)(2,1)S(1)} %fusion.3.refs_6_.refs_1_), channel_id=1, source_target_pairs={{0,2},{1,3},{2,0},{3,1},{4,6},{5,7},{6,4},{7,5},{8,10},{9,11},{10,... | collective-permute-start | bytes 884744 | tf_op jit(solution)/shard_map/ppermute | solution.py:32
  198.9 11.1 %collective-permute-start.34 = (bf16[192,768]{1,0:T(8,128)(2,1)S(1)}, bf16[192,768]{1,0:T(8,128)(2,1)S(1)}, u32[]{:S(2)}, u32[]{:S(2)}) collective-permute-start(bf16[192,768]{1,0:T(8,128)(2,1)S(1)} %slice.268.refs_5_), channel_id=1, source_target_pairs={{0,8},{4,12},{8,0},{12,4},{1,9},{5,13},{9,1},{13,5},{2,10},{6,14},... | collective-permute-start | bytes 884744 | tf_op jit(solution)/shard_map/ppermute | solution.py:32
  (41 other events, 67.2 us)
